TPU v7x, 32 devices: a whole 2x2x4 slice. The times are simulated.
32 devices in a mesh: runs: 2 (over y), blk: 4 (over z), term: 4 (over x, core).
Axes of the slice: x: 2, y: 2, z: 4, core: 2. Of those that a mesh axis runs over, the one named last changes fastest.
Arguments:
- two_site: bfloat16 [8, 4, 256, 256], P(('runs', 'blk')), parts along dimension 0, may hold values from -6 to 6
- left_env: bfloat16 [8, 4, 256, 256], P(('runs', 'term'), 'blk'), parts along dimension 0, may hold values from -0.375 to 0.375
- right_env: bfloat16 [8, 4, 256, 256], P(('runs', 'term'), 'blk'), parts along dimension 0, may hold values from -0.375 to 0.375
- row_size: int32 [8], P(('runs', 'blk')), parts along dimension 0, may hold values from 64 to 256
- col_size: int32 [8], P('runs'), parts along dimension 0, may hold values from 64 to 256
- block_live: int32 [8, 4], P(('runs', 'blk')), parts along dimension 0, may hold values 0 or 1
Outputs:
- first_image: bfloat16 [8, 4, 256, 256], P(('runs', 'blk'), 'term'), parts along dimension 0
- second_image: bfloat16 [8, 4, 256, 256], P(('runs', 'blk'), 'term'), parts along dimension 0
There are 2 independent parts, one for each index of `runs`. A program takes and returns all parts, laid end to end along the dimension named above; each array names one. Nothing has to cross between parts.
All inputs are finite; a program needn't handle non-finite values. No bound on the sum of `block_live` on one device may be relied on, other than what follows from the above.
Results may differ from a plain program's by a relative error of at most 0.029.
Values may be sent and summed in bfloat16 or wider, within the bound.
No kernel may reach another device: no remote copies, remote signals or barrier semaphores. Data moves between devices by JAX's collectives and lax.ppermute only.
A program may use at most 64 MiB of HBM per device.

v0:
```python
import jax
import jax.numpy as jnp
from jax import lax
from jax.sharding import PartitionSpec as P


def build_mask(row_size, col_size, block_live, width):
    index = jnp.arange(width, dtype=jnp.int32)
    rows_ok = index[None, :] < row_size[:, None]
    cols_ok = index[None, :] < col_size[:, None]
    return (
        (block_live[:, :, None, None] == 1) & rows_ok[:, None, :, None] & cols_ok[None, :, None, :]
    )


def left_apply(left_block, tiles):
    return jnp.einsum(
        "aij,acjk->acik", left_block, tiles, preferred_element_type=jnp.float32
    ).astype(jnp.bfloat16)


def right_apply(tiles, right_block):
    return jnp.einsum(
        "acij,cjk->acik", tiles, right_block, preferred_element_type=jnp.float32
    ).astype(jnp.bfloat16)


def finish(left_part, right_block, own_mask):
    partial_cols = right_apply(
        lax.all_to_all(left_part, "blk", split_axis=1, concat_axis=0, tiled=True), right_block
    )
    partial_rows = lax.all_to_all(partial_cols, "blk", split_axis=0, concat_axis=1, tiled=True)
    summed = lax.psum_scatter(
        partial_rows.astype(jnp.float32).astype(jnp.bfloat16),
        "term",
        scatter_dimension=1,
        tiled=True,
    ).astype(jnp.float32)
    return jnp.where(own_mask, summed, jnp.zeros_like(summed)).astype(jnp.bfloat16)


def local(two_site, left_env, right_env, row_size, col_size, block_live):
    width = two_site.shape[2]
    live_mask = build_mask(row_size, col_size, block_live, width)
    start = jnp.where(live_mask, two_site, jnp.zeros_like(two_site))
    own_cols = two_site.shape[1] // lax.axis_size("term")
    first_col = lax.axis_index("term") * own_cols
    own_mask = lax.dynamic_slice_in_dim(live_mask, first_col, own_cols, 1)
    left_block = left_env[0]
    right_block = right_env[0]
    first_left = left_apply(left_block, start)
    first_image = finish(first_left, right_block, own_mask)
    wide = first_image.astype(jnp.float32)
    local_sum = jnp.sum(wide * wide)
    norm_sum = lax.psum(local_sum, ("blk", "term"))
    total_count = two_site.shape[0] * lax.axis_size("blk") * two_site.shape[1] * width * width
    unit = (wide * lax.rsqrt(norm_sum / total_count + 1e-06)).astype(jnp.bfloat16)
    second_left = left_apply(left_block, lax.all_gather(unit, "term", axis=1, tiled=True))
    second_image = finish(second_left, right_block, own_mask)
    return (first_image, second_image)


def solution(mesh):
    return jax.shard_map(
        local,
        mesh=mesh,
        in_specs=(
            P(("runs", "blk"), None, None, None),
            P(("runs", "term"), "blk", None, None),
            P(("runs", "term"), "blk", None, None),
            P(("runs", "blk")),
            P("runs"),
            P(("runs", "blk"), None),
        ),
        out_specs=(P(("runs", "blk"), "term", None, None), P(("runs", "blk"), "term", None, None)),
        check_vma=False,
    )
```

profile of v0, /device:TPU:0, one launch (start us, length us, event | category | flops | bytes accessed | tf_op | source)
XLA Modules:
  0.0 176.0 jit_solution(12713348126124191536)
XLA Ops:
  7.2 0.0 copy-start
  7.2 0.0 reduce-scatter.3.cloned.1.call-start
  7.9 0.0 copy-start.4
  7.9 0.6 copy-done.4
  8.6 0.0 copy-start.3
  8.6 0.6 copy-done.3
  9.2 0.1 iota_compare_fusion
  9.3 0.0 copy-done
  9.3 1.6 fusion
  10.9 0.0 copy-start.1
  10.9 20.7 %all_to_all.42 = bf16[1,4,256,256]{2,3,0,1:T(8,128)(2,1)S(1)} all-to-all(bf16[1,4,256,256]{2,3,0,1:T(8,128)(2,1)S(1)} %fusion), channel_id=1, replica_groups=mesh['runs'=2,'blk'=4,'term'=4] {'blk'}, dimensions={1} | all-to-all | bytes 1048576 | tf_op jit(solution)/shard_map/all_to_all | solution.py:30
  31.6 0.0 copy-done.1
  31.6 0.4 fusion.1
  32.0 16.7 %all_to_all.43 = bf16[4,1,256,256]{3,2,1,0:T(8,128)(2,1)} all-to-all(bf16[4,1,256,256]{3,2,1,0:T(8,128)(2,1)S(1)} %fusion.1), channel_id=1, replica_groups=mesh['runs'=2,'blk'=4,'term'=4] {'blk'}, dimensions={0} | all-to-all | bytes 1048576 | tf_op jit(solution)/shard_map/all_to_all | solution.py:32
  48.7 0.0 reduce-scatter.3.cloned.1.call-update
  48.7 0.0 reduce-scatter.5.cloned.1.call-start
  48.8 0.2 broadcast_and_fusion
  49.0 20.6 %reduce-scatter.3.cloned.1.call-done = bf16[1,1,256,256]{3,2,1,0:T(8,128)(2,1)} async-done(((bf16[1,4,256,256]{3,2,1,0:T(8,128)(2,1)}), bf16[1,1,256,256]{3,2,1,0:T(8,128)(2,1)}) %reduce-scatter.3.cloned.1.call-update) | async-done | bytes 131088 | tf_op jit(solution)/shard_map/reduce_scatter | solution.py:33
  69.6 1.6 fusion.9
  71.2 0.0 copy-start.2
  71.2 32.9 %psum.7 = f32[]{:T(128)} all-reduce(f32[]{:T(128)} %get-tuple-element.2), channel_id=1, replica_groups=mesh['runs'=2,'blk'=4,'term'=4] {'blk','term'}, use_global_device_ids=true, to_apply=%region_2.3 | all-reduce | flops 1 | bytes 8 | tf_op jit(solution)/shard_map/psum | solution.py:55
  104.8 0.0 copy-done.2
  104.8 6.5 %all_gather.3 = bf16[1,4,256,256]{3,2,0,1:T(8,128)(2,1)S(1)} all-gather(bf16[1,1,256,256]{3,2,0,1:T(8,128)(2,1)S(1)} %fusion.12), channel_id=1, replica_groups=mesh['runs'=2,'blk'=4,'term'=4] {'term'}, dimensions={1}, use_global_device_ids=true | all-gather | bytes 655360 | tf_op jit(solution)/shard_map/all_gather | solution.py:58
  111.3 0.3 fusion.2
  111.7 17.7 %all_to_all.44 = bf16[1,4,256,256]{2,3,0,1:T(8,128)(2,1)S(1)} all-to-all(bf16[1,4,256,256]{2,3,0,1:T(8,128)(2,1)S(1)} %fusion.2), channel_id=1, replica_groups=mesh['runs'=2,'blk'=4,'term'=4] {'blk'}, dimensions={1} | all-to-all | bytes 1048576 | tf_op jit(solution)/shard_map/all_to_all | solution.py:30
  129.4 0.4 fusion.3
  129.7 17.3 %all_to_all.45 = bf16[4,1,256,256]{3,2,1,0:T(8,128)(2,1)} all-to-all(bf16[4,1,256,256]{3,2,1,0:T(8,128)(2,1)S(1)} %fusion.3), channel_id=1, replica_groups=mesh['runs'=2,'blk'=4,'term'=4] {'blk'}, dimensions={0} | all-to-all | bytes 1048576 | tf_op jit(solution)/shard_map/all_to_all | solution.py:32
  147.0 0.0 reduce-scatter.5.cloned.1.call-update
  147.0 20.6 %reduce-scatter.5.cloned.1.call-done = bf16[1,1,256,256]{3,2,1,0:T(8,128)(2,1)} async-done(((bf16[1,4,256,256]{3,2,1,0:T(8,128)(2,1)}), bf16[1,1,256,256]{3,2,1,0:T(8,128)(2,1)}) %reduce-scatter.5.cloned.1.call-update) | async-done | bytes 131088 | tf_op jit(solution)/shard_map/reduce_scatter | solution.py:33
  167.6 1.6 select_convert_fusion
  (3 shorter events, 0.0 us)
Async XLA Ops:
  7.2 2.1 %copy-start = (bf16[1,1,256,256]{3,2,1,0:T(8,128)(2,1)S(1)}, bf16[1,1,256,256]{3,2,1,0:T(8,128)(2,1)}, u32[]{:S(2)}) copy-start(bf16[1,1,256,256]{3,2,1,0:T(8,128)(2,1)} %param.7) | copy-start | bytes 393220
  7.2 62.5 %reduce-scatter.3.cloned.1.call-start = ((), (), s32[]{:S(2)}) async-start(), calls=%async_computation.6 | async-start | bytes 655360 | tf_op jit(solution)/shard_map/reduce_scatter | solution.py:33
  7.9 0.7 copy-start.4
  8.6 0.7 copy-start.3
  10.9 20.8 %copy-start.1 = (bf16[1,1,256,256]{3,2,1,0:T(8,128)(2,1)S(1)}, bf16[1,1,256,256]{3,2,1,0:T(8,128)(2,1)}, u32[]{:S(2)}) copy-start(bf16[1,1,256,256]{3,2,1,0:T(8,128)(2,1)} %param.8) | copy-start | bytes 393220
  48.7 118.9 %reduce-scatter.5.cloned.1.call-start = ((), (), s32[]{:S(2)}) async-start(), calls=%async_computation.7 | async-start | bytes 655360 | tf_op jit(solution)/shard_map/reduce_scatter | solution.py:33
  71.2 33.6 %copy-start.2 = (bf16[1,1,256,256]{3,2,1,0:T(8,128)(2,1)}, bf16[1,1,256,256]{3,2,1,0:T(8,128)(2,1)S(1)}, u32[]{:S(2)}) copy-start(bf16[1,1,256,256]{3,2,1,0:T(8,128)(2,1)S(1)} %get-tuple-element.3) | copy-start | bytes 393220
Sparse Core Ops, SparseCore 0:
  48.9 20.7 reduce-scatter.2
  147.2 20.4 reduce-scatter.4
where the time goes:
time: 176 us
  blocking collectives  112 us (64%)
  waiting for transfers between devices  41.2 us (23%)
  between operations  15.5 us (9%)
  other arithmetic  3.49 us (2%)
  matrix products  2.65 us (2%)
    reduce_scatter x2, waiting for transfers between devices, finish(): lax.psum_scatter(partial_rows.astype(jnp.float32).astype(jnp.bfloat16), '...  41.2 us
    all_to_all x2, blocking collectives, finish(): lax.all_to_all(left_part, 'blk', split_axis=1, concat_axis=0, tiled=True)  38.4 us
    all_to_all x2, blocking collectives, finish(): lax.all_to_all(partial_cols, 'blk', split_axis=0, concat_axis=1, tiled=True)  34 us
    psum x1, blocking collectives, local(): norm_sum = lax.psum(local_sum, ('blk', 'term'))  32.9 us
    all_gather x1, blocking collectives, local(): lax.all_gather(unit, 'term', axis=1, tiled=True)  6.51 us
  transfers between devices with their start and end apart: 2, of which 2 were waited for; matrix products, arithmetic and copies ran while one was open for 0% of the time, Pallas kernels for 0%

commit v1 on v0

v1 whole, which is shorter than its diff:
```python
import functools

import jax
import jax.numpy as jnp
from jax import lax
from jax.experimental import pallas as pl
from jax.experimental.pallas import tpu as pltpu
from jax.sharding import PartitionSpec as P

AXES = ("blk", "term")


def move(value, pairs, terms):
    return lax.ppermute(
        value, AXES, [(a * terms + b, c * terms + d) for (a, b), (c, d) in pairs]
    )


def apply_tile(left, right, tile, keep):
    terms, width = left.shape[0], tile.shape[0]
    wide = jnp.dot(
        left[...].reshape(terms * width, width), tile, preferred_element_type=jnp.float32
    ).astype(jnp.bfloat16)
    total = jnp.zeros((width, width), jnp.float32)
    for t in range(terms):
        total += jnp.dot(
            wide[t * width : (t + 1) * width], right[t], preferred_element_type=jnp.float32
        )
    return jnp.where(keep, total, 0.0)


def keep_mask(width, rows, cols, live):
    at_row = lax.broadcasted_iota(jnp.int32, (width, width), 0)
    at_col = lax.broadcasted_iota(jnp.int32, (width, width), 1)
    return (at_row < rows) & (at_col < cols) & (live == 1)


def first_kernel(terms, own, place, rows, cols, live, tiles, *refs):
    lefts, rights = refs[:terms], refs[terms : terms + own * terms]
    image, left, right, partial = refs[terms + own * terms :]
    width = tiles.shape[-1]
    blk, term = place[0], place[1]
    for m in range(terms):
        left[term ^ m] = lefts[m][0, 0]
    for k in range(own * terms):
        right[blk ^ k] = rights[k][0, 0]
    partial[...] = jnp.zeros_like(partial)
    for o in range(own):
        col = term * own + o
        keep = keep_mask(width, rows[0], cols[col], live[0, col])
        start = jnp.where(keep, tiles[0, col], jnp.zeros((), tiles.dtype))
        out = apply_tile(left, right.at[pl.ds(o * terms, terms)], start, keep).astype(jnp.bfloat16)
        image[0, o] = out
        out = out.astype(jnp.float32)
        partial[...] += jnp.sum((out * out).reshape(-1, 8, width), axis=0)


def second_kernel(terms, own, place, rows, cols, live, image, left, right, raw):
    width = image.shape[-1]
    for o in range(own):
        col = place[1] * own + o
        keep = keep_mask(width, rows[0], cols[col], live[0, col])
        raw[0, o] = apply_tile(left, right.at[pl.ds(o * terms, terms)], image[0, o], keep)


def scale_kernel(count, raw, norm, image):
    total = jnp.sum(norm[...])
    image[...] = (raw[...] * lax.rsqrt(total / count + 1e-06)).astype(jnp.bfloat16)


def total_over(value, axis, size, other):
    step = 1
    while step < size:
        if axis == "blk":
            pairs = [((a, b), (a ^ step, b)) for a in range(size) for b in range(other)]
            value = value + move(value, pairs, other)
        else:
            pairs = [((a, b), (a, b ^ step)) for a in range(other) for b in range(size)]
            value = value + move(value, pairs, size)
        step *= 2
    return value


def local(blocks, terms, two_site, left_env, right_env, row_size, col_size, block_live):
    width = two_site.shape[2]
    n_cols = two_site.shape[1]
    own = n_cols // terms
    vmem, smem = pl.BlockSpec(memory_space=pltpu.VMEM), pl.BlockSpec(memory_space=pltpu.SMEM)
    params = pltpu.CompilerParams(vmem_limit_bytes=32 * 1024 * 1024)
    place = jnp.stack([lax.axis_index("blk"), lax.axis_index("term")]).astype(jnp.int32)

    rights = []
    for k in range(blocks):
        pairs = [
            ((c, t), (((c % own) * terms + t) ^ k, c // own))
            for c in range(blocks)
            for t in range(terms)
        ]
        rights.append(move(right_env, pairs, terms))
    lefts = [left_env] + [
        move(left_env, [((a, t), (a, t ^ m)) for a in range(blocks) for t in range(terms)], terms)
        for m in range(1, terms)
    ]

    first_image, left, right, partial = pl.pallas_call(
        functools.partial(first_kernel, terms, own),
        out_shape=(
            jax.ShapeDtypeStruct((1, own, width, width), jnp.bfloat16),
            jax.ShapeDtypeStruct((terms, width, width), jnp.bfloat16),
            jax.ShapeDtypeStruct((own * terms, width, width), jnp.bfloat16),
            jax.ShapeDtypeStruct((8, width), jnp.float32),
        ),
        in_specs=[smem] * 4 + [vmem] * (1 + terms + blocks),
        out_specs=(vmem,) * 4,
        compiler_params=params,
    )(place, row_size, col_size, block_live, two_site, *lefts, *rights)

    raw = pl.pallas_call(
        functools.partial(second_kernel, terms, own),
        out_shape=jax.ShapeDtypeStruct((1, own, width, width), jnp.float32),
        in_specs=[smem] * 4 + [vmem] * 3,
        out_specs=vmem,
        compiler_params=params,
    )(place, row_size, col_size, block_live, first_image, left, right)

    norm = total_over(total_over(partial, "term", terms, blocks), "blk", blocks, terms)
    second_image = pl.pallas_call(
        functools.partial(scale_kernel, float(blocks * n_cols * width * width)),
        out_shape=jax.ShapeDtypeStruct((1, own, width, width), jnp.bfloat16),
        in_specs=[vmem] * 2,
        out_specs=vmem,
        compiler_params=params,
    )(raw, norm)
    return first_image, second_image


def solution(mesh):
    return jax.shard_map(
        functools.partial(local, mesh.shape["blk"], mesh.shape["term"]),
        mesh=mesh,
        in_specs=(
            P(("runs", "blk"), None, None, None),
            P(("runs", "term"), "blk", None, None),
            P(("runs", "term"), "blk", None, None),
            P(("runs", "blk")),
            P("runs"),
            P(("runs", "blk"), None),
        ),
        out_specs=(P(("runs", "blk"), "term", None, None), P(("runs", "blk"), "term", None, None)),
        check_vma=False,
    )
```

time: 176 us -> 41.6 us (0.24)
  blocking collectives: 112 us -> 0 us
  waiting for transfers between devices: 41.2 us -> 11 us
  starting transfers between devices: 0.08 us -> 22.2 us
  between operations: 15.5 us -> 1.33 us
  Pallas kernels: 0 us -> 3.89 us
  other arithmetic: 3.49 us -> 0.09 us
  matrix products: 2.65 us -> 0 us
    all_to_all x4 -> x0, blocking collectives: 72.4 us -> none  [the longest x2 38.4 us: finish(): lax.all_to_all(left_part, 'blk', split_axis=1, concat_axis=0, tiled=True)]
    reduce_scatter x2 -> x0, waiting for transfers between devices: 41.2 us -> none  [finish(): lax.psum_scatter(partial_rows.astype(jnp.float32).astype(jnp.bfloat16), '...]
    psum x1 -> x0, blocking collectives: 32.9 us -> none  [local(): norm_sum = lax.psum(local_sum, ('blk', 'term'))]
    ppermute x0 -> x11, starting transfers between devices: none -> 22.2 us  [move(): lax.ppermute(value, AXES, [(a * terms + b, c * terms + d) for (a, b), (c,...]
    ppermute x0 -> x11, waiting for transfers between devices: none -> 11 us  [move(): lax.ppermute(value, AXES, [(a * terms + b, c * terms + d) for (a, b), (c,...]
    all_gather x1 -> x0, blocking collectives: 6.51 us -> none  [local(): lax.all_gather(unit, 'term', axis=1, tiled=True)]
    pallas_call x0 -> x3, Pallas kernels: none -> 3.89 us  [the longest x1 1.9 us: local(): pl.pallas_call(functools.partial(first_kernel, terms, own), out_shape=(ja...]
    dot_general x4 -> x0, matrix products: 2.65 us -> none  [the longest x2 1.93 us: left_apply(): jnp.einsum('aij,acjk->acik', left_block, tiles, preferred_element_type=jn...]
  transfers between devices with their start and end apart: 2 -> 11, of which waited for: 2 -> 7; matrix products, arithmetic and copies ran while one was open for 0% -> 0% of each run, Pallas kernels for 0% -> 3%
where the time goes in v1:
time: 41.6 us; the launch traced here: 41.3 us
  starting transfers between devices  22.2 us (53%)
  waiting for transfers between devices  11 us (26%)
  Pallas kernels  3.89 us (9%)
  local copies, waits for them, and re-layouts  2.86 us (7%)
  between operations  1.33 us (3%)
    ppermute x11, starting transfers between devices, move(): lax.ppermute(value, AXES, [(a * terms + b, c * terms + d) for (a, b), (c,...  22.2 us
    ppermute x11, waiting for transfers between devices, move(): lax.ppermute(value, AXES, [(a * terms + b, c * terms + d) for (a, b), (c,...  11 us
    unnamed x10, local copies, waits for them, and re-layouts  2.86 us
    pallas_call x1, Pallas kernels, local(): pl.pallas_call(functools.partial(first_kernel, terms, own), out_shape=(ja...  1.9 us
    pallas_call x1, Pallas kernels, local(): pl.pallas_call(functools.partial(second_kernel, terms, own), out_shape=ja...  1.15 us
    pallas_call x1, Pallas kernels, local(): pl.pallas_call(functools.partial(scale_kernel, float(blocks * n_cols * wi...  0.84 us
  transfers between devices with their start and end apart: 11, of which 7 were waited for; matrix products, arithmetic and copies ran while one was open for 0% of the time, Pallas kernels for 3%

profile of v1, /device:TPU:0, one launch (start us, length us, event | category | flops | bytes accessed | tf_op | source)
XLA Modules:
  0.0 41.3 jit_solution(12014140794659394811)
XLA Ops:
  0.6 3.0 %collective-permute-start.1 = (bf16[1,1,256,256]{3,2,1,0:T(8,128)(2,1)}, bf16[1,1,256,256]{3,2,1,0:T(8,128)(2,1)S(1)}, u32[]{:S(2)}, u32[]{:S(2)}) collective-permute-start(bf16[1,1,256,256]{3,2,1,0:T(8,128)(2,1)} %refs_0_.1), channel_id=1, source_target_pairs={{0,2},{1,3},{2,0},{3,1},{4,6},{5,7},{6,4},{7,5},{8,10},{9,11},{10,... | collective-permute-start | bytes 393224 | tf_op jit(solution)/shard_map/ppermute | solution.py:14
  3.6 0.0 collective-permute-start
  3.6 0.2 collective-permute-start.2
  3.8 2.0 %collective-permute-start.4 = (bf16[1,1,256,256]{3,2,1,0:T(8,128)(2,1)}, bf16[1,1,256,256]{3,2,1,0:T(8,128)(2,1)S(1)}, u32[]{:S(2)}, u32[]{:S(2)}) collective-permute-start(bf16[1,1,256,256]{3,2,1,0:T(8,128)(2,1)} %param.8), channel_id=1, source_target_pairs={{0,4},{1,0},{2,12},{3,8},{4,5},{5,1},{6,13},{7,9},{8,6},{9,2},{10,... | collective-permute-start | bytes 393224 | tf_op jit(solution)/shard_map/ppermute | solution.py:14
  5.9 1.6 %collective-permute-start.3 = (bf16[1,1,256,256]{3,2,1,0:T(8,128)(2,1)}, bf16[1,1,256,256]{3,2,1,0:T(8,128)(2,1)S(1)}, u32[]{:S(2)}, u32[]{:S(2)}) collective-permute-start(bf16[1,1,256,256]{3,2,1,0:T(8,128)(2,1)} %param.8), channel_id=1, source_target_pairs={{0,0},{1,4},{2,8},{3,12},{4,1},{5,5},{6,9},{7,13},{8,2},{9,6},{10,... | collective-permute-start | bytes 393224 | tf_op jit(solution)/shard_map/ppermute | solution.py:14
  7.4 0.4 %collective-permute-done.1.refs_2_ = bf16[1,1,256,256]{3,2,1,0:T(8,128)(2,1)S(1)} collective-permute-done((bf16[1,1,256,256]{3,2,1,0:T(8,128)(2,1)}, bf16[1,1,256,256]{3,2,1,0:T(8,128)(2,1)S(1)}, u32[]{:S(2)}, u32[]{:S(2)}) %collective-permute-start.1) | collective-permute-done | bytes 131104 | tf_op jit(solution)/shard_map/ppermute | solution.py:14
  7.9 5.4 %collective-permute-start.6 = (bf16[1,1,256,256]{3,2,1,0:T(8,128)(2,1)}, bf16[1,1,256,256]{3,2,1,0:T(8,128)(2,1)S(1)}, u32[]{:S(2)}, u32[]{:S(2)}) collective-permute-start(bf16[1,1,256,256]{3,2,1,0:T(8,128)(2,1)} %param.8), channel_id=1, source_target_pairs={{0,12},{1,8},{2,4},{3,0},{4,13},{5,9},{6,5},{7,1},{8,14},{9,10},{1... | collective-permute-start | bytes 393224 | tf_op jit(solution)/shard_map/ppermute | solution.py:14
  13.3 0.0 collective-permute-done.refs_1_
  13.3 0.5 %collective-permute-start.5 = (bf16[1,1,256,256]{3,2,1,0:T(8,128)(2,1)}, bf16[1,1,256,256]{3,2,1,0:T(8,128)(2,1)S(1)}, u32[]{:S(2)}, u32[]{:S(2)}) collective-permute-start(bf16[1,1,256,256]{3,2,1,0:T(8,128)(2,1)} %param.8), channel_id=1, source_target_pairs={{0,8},{1,12},{2,0},{3,4},{4,9},{5,13},{6,1},{7,5},{8,10},{9,14},{1... | collective-permute-start | bytes 393224 | tf_op jit(solution)/shard_map/ppermute | solution.py:14
  14.5 0.0 copy-start.3
  14.5 0.0 copy-start.4
  14.5 0.1 pad_add_fusion.place
  14.6 0.0 collective-permute-done.2.refs_3_
  14.6 0.0 collective-permute-done.4.refs_5_
  14.6 0.0 collective-permute-done.3.refs_4_
  14.6 2.9 %collective-permute-done.6.refs_7_ = bf16[1,1,256,256]{3,2,1,0:T(8,128)(2,1)S(1)} collective-permute-done((bf16[1,1,256,256]{3,2,1,0:T(8,128)(2,1)}, bf16[1,1,256,256]{3,2,1,0:T(8,128)(2,1)S(1)}, u32[]{:S(2)}, u32[]{:S(2)}) %collective-permute-start.6) | collective-permute-done | bytes 131104 | tf_op jit(solution)/shard_map/ppermute | solution.py:14
  17.5 2.7 %collective-permute-done.5.refs_6_ = bf16[1,1,256,256]{3,2,1,0:T(8,128)(2,1)S(1)} collective-permute-done((bf16[1,1,256,256]{3,2,1,0:T(8,128)(2,1)}, bf16[1,1,256,256]{3,2,1,0:T(8,128)(2,1)S(1)}, u32[]{:S(2)}, u32[]{:S(2)}) %collective-permute-start.5) | collective-permute-done | bytes 131104 | tf_op jit(solution)/shard_map/ppermute | solution.py:14
  20.2 0.0 copy-done.3
  20.2 1.0 %copy-done = bf16[1,4,256,256]{3,2,1,0:T(8,128)(2,1)S(1)} copy-done((bf16[1,4,256,256]{3,2,1,0:T(8,128)(2,1)S(1)}, bf16[1,4,256,256]{3,2,1,0:T(8,128)(2,1)}, u32[]{:S(2)}) %copy-start) | copy-done | bytes 524312
  21.3 0.9 %copy-done.1 = bf16[1,1,256,256]{3,2,1,0:T(8,128)(2,1)S(1)} copy-done((bf16[1,1,256,256]{3,2,1,0:T(8,128)(2,1)S(1)}, bf16[1,1,256,256]{3,2,1,0:T(8,128)(2,1)}, u32[]{:S(2)}) %copy-start.1) | copy-done | bytes 131096
  22.2 1.9 %shard_map.77 = (bf16[1,1,256,256]{3,2,1,0:T(8,128)(2,1)}, bf16[4,256,256]{2,1,0:T(8,128)(2,1)S(1)}, bf16[4,256,256]{2,1,0:T(8,128)(2,1)S(1)}, f32[8,256]{1,0:T(8,128)S(1)}) custom-call(s32[2]{0:T(128)S(1)} %pad_add_fusion.place, s32[1]{0:T(128)S(6)} %copy.8.rows, s32[4]{0:T(128)S(1)} %copy-done.3, s32[1,4]{1,0:T(1,128)S(1)} %copy-done.4, ...), custom_call_target="tpu_custom_call" | custom-call | tf_op jit(solution)/shard_map/pallas_call | solution.py:105
  24.1 0.9 %collective-permute-start.7 = (f32[8,256]{1,0:T(8,128)S(1)}, f32[8,256]{1,0:T(8,128)S(1)}, u32[]{:S(2)}, u32[]{:S(2)}) collective-permute-start(f32[8,256]{1,0:T(8,128)S(1)} %get-tuple-element.9), channel_id=1, source_target_pairs={{0,1},{1,0},{2,3},{3,2},{4,5},{5,4},{6,7},{7,6},{8,9},{9,8},{10,11... | collective-permute-start | bytes 24584 | tf_op jit(solution)/shard_map/ppermute | solution.py:14
  25.0 0.8 %collective-permute-done.7 = f32[8,256]{1,0:T(8,128)S(1)} collective-permute-done((f32[8,256]{1,0:T(8,128)S(1)}, f32[8,256]{1,0:T(8,128)S(1)}, u32[]{:S(2)}, u32[]{:S(2)}) %collective-permute-start.7) | collective-permute-done | bytes 8224 | tf_op jit(solution)/shard_map/ppermute | solution.py:14
  25.9 4.8 %collective-permute-start.8 = (f32[8,256]{1,0:T(8,128)S(1)}, f32[8,256]{1,0:T(8,128)S(1)}, u32[]{:S(2)}, u32[]{:S(2)}) collective-permute-start(f32[8,256]{1,0:T(8,128)S(1)} %add.12), channel_id=1, source_target_pairs={{0,2},{1,3},{2,0},{3,1},{4,6},{5,7},{6,4},{7,5},{8,10},{9,11},{10,... | collective-permute-start | bytes 24584 | tf_op jit(solution)/shard_map/ppermute | solution.py:14
  30.7 1.6 %collective-permute-done.8 = f32[8,256]{1,0:T(8,128)S(1)} collective-permute-done((f32[8,256]{1,0:T(8,128)S(1)}, f32[8,256]{1,0:T(8,128)S(1)}, u32[]{:S(2)}, u32[]{:S(2)}) %collective-permute-start.8) | collective-permute-done | bytes 8224 | tf_op jit(solution)/shard_map/ppermute | solution.py:14
  32.3 1.2 %collective-permute-start.9 = (f32[8,256]{1,0:T(8,128)S(1)}, f32[8,256]{1,0:T(8,128)S(1)}, u32[]{:S(2)}, u32[]{:S(2)}) collective-permute-start(f32[8,256]{1,0:T(8,128)S(1)} %add.13), channel_id=1, source_target_pairs={{0,4},{1,5},{2,6},{3,7},{4,0},{5,1},{6,2},{7,3},{8,12},{9,13},{10,... | collective-permute-start | bytes 24584 | tf_op jit(solution)/shard_map/ppermute | solution.py:14
  33.5 2.4 %collective-permute-done.9 = f32[8,256]{1,0:T(8,128)S(1)} collective-permute-done((f32[8,256]{1,0:T(8,128)S(1)}, f32[8,256]{1,0:T(8,128)S(1)}, u32[]{:S(2)}, u32[]{:S(2)}) %collective-permute-start.9) | collective-permute-done | bytes 8224 | tf_op jit(solution)/shard_map/ppermute | solution.py:14
  35.9 2.4 %collective-permute-start.10 = (f32[8,256]{1,0:T(8,128)S(1)}, f32[8,256]{1,0:T(8,128)S(1)}, u32[]{:S(2)}, u32[]{:S(2)}) collective-permute-start(f32[8,256]{1,0:T(8,128)S(1)} %add.14), channel_id=1, source_target_pairs={{0,8},{1,9},{2,10},{3,11},{4,12},{5,13},{6,14},{7,15},{8,0},{9,1},... | collective-permute-start | bytes 24584 | tf_op jit(solution)/shard_map/ppermute | solution.py:14
  38.4 0.9 %copy-done.2 = bf16[1,1,256,256]{3,2,1,0:T(8,128)(2,1)S(1)} copy-done((bf16[1,1,256,256]{3,2,1,0:T(8,128)(2,1)S(1)}, bf16[1,1,256,256]{3,2,1,0:T(8,128)(2,1)}, u32[]{:S(2)}) %copy-start.2) | copy-done | bytes 131096
  39.3 1.2 %shard_map.78.raw = f32[1,1,256,256]{3,2,1,0:T(8,128)S(1)} custom-call(s32[2]{0:T(128)S(1)} %pad_add_fusion.place, s32[1]{0:T(128)S(6)} %copy.8.rows, s32[4]{0:T(128)S(1)} %copy-done.3, s32[1,4]{1,0:T(1,128)S(1)} %copy-done.4, bf16[1,1,256,256]{3,2,1,0:T(8,128)(2,1)S(1)} %copy-done.2, bf16[4,256,256]{2,1,0:T(8,128)(2,1)S(1)} %get-tuple-element.7.left, ...), custom_call_target="tpu_custom_call" | custom-call | tf_op jit(solution)/shard_map/pallas_call | solution.py:118
  40.4 0.1 collective-permute-done.10
  40.5 0.8 %shard_map.79 = bf16[1,1,256,256]{3,2,1,0:T(8,128)(2,1)} custom-call(f32[1,1,256,256]{3,2,1,0:T(8,128)S(1)} %shard_map.78.raw, f32[8,256]{1,0:T(8,128)S(1)} %add.15.norm), custom_call_target="tpu_custom_call" | custom-call | tf_op jit(solution)/shard_map/pallas_call | solution.py:127
  (8 shorter events, 0.0 us)
Async XLA Ops:
  0.6 7.2 %collective-permute-start.1 = (bf16[1,1,256,256]{3,2,1,0:T(8,128)(2,1)}, bf16[1,1,256,256]{3,2,1,0:T(8,128)(2,1)S(1)}, u32[]{:S(2)}, u32[]{:S(2)}) collective-permute-start(bf16[1,1,256,256]{3,2,1,0:T(8,128)(2,1)} %refs_0_.1), channel_id=1, source_target_pairs={{0,2},{1,3},{2,0},{3,1},{4,6},{5,7},{6,4},{7,5},{8,10},{9,11},{10,... | collective-permute-start | bytes 393224 | tf_op jit(solution)/shard_map/ppermute | solution.py:14
  3.6 9.7 %collective-permute-start = (bf16[1,1,256,256]{3,2,1,0:T(8,128)(2,1)}, bf16[1,1,256,256]{3,2,1,0:T(8,128)(2,1)S(1)}, u32[]{:S(2)}, u32[]{:S(2)}) collective-permute-start(bf16[1,1,256,256]{3,2,1,0:T(8,128)(2,1)} %refs_0_.1), channel_id=1, source_target_pairs={{0,1},{1,0},{2,3},{3,2},{4,5},{5,4},{6,7},{7,6},{8,9},{9,8},{10,11... | collective-permute-start | bytes 393224 | tf_op jit(solution)/shard_map/ppermute | solution.py:14
  3.6 10.9 %collective-permute-start.2 = (bf16[1,1,256,256]{3,2,1,0:T(8,128)(2,1)}, bf16[1,1,256,256]{3,2,1,0:T(8,128)(2,1)S(1)}, u32[]{:S(2)}, u32[]{:S(2)}) collective-permute-start(bf16[1,1,256,256]{3,2,1,0:T(8,128)(2,1)} %refs_0_.1), channel_id=1, source_target_pairs={{0,3},{1,2},{2,1},{3,0},{4,7},{5,6},{6,5},{7,4},{8,11},{9,10},{10,... | collective-permute-start | bytes 393224 | tf_op jit(solution)/shard_map/ppermute | solution.py:14
  3.8 10.7 %collective-permute-start.4 = (bf16[1,1,256,256]{3,2,1,0:T(8,128)(2,1)}, bf16[1,1,256,256]{3,2,1,0:T(8,128)(2,1)S(1)}, u32[]{:S(2)}, u32[]{:S(2)}) collective-permute-start(bf16[1,1,256,256]{3,2,1,0:T(8,128)(2,1)} %param.8), channel_id=1, source_target_pairs={{0,4},{1,0},{2,12},{3,8},{4,5},{5,1},{6,13},{7,9},{8,6},{9,2},{10,... | collective-permute-start | bytes 393224 | tf_op jit(solution)/shard_map/ppermute | solution.py:14
  5.9 8.7 %collective-permute-start.3 = (bf16[1,1,256,256]{3,2,1,0:T(8,128)(2,1)}, bf16[1,1,256,256]{3,2,1,0:T(8,128)(2,1)S(1)}, u32[]{:S(2)}, u32[]{:S(2)}) collective-permute-start(bf16[1,1,256,256]{3,2,1,0:T(8,128)(2,1)} %param.8), channel_id=1, source_target_pairs={{0,0},{1,4},{2,8},{3,12},{4,1},{5,5},{6,9},{7,13},{8,2},{9,6},{10,... | collective-permute-start | bytes 393224 | tf_op jit(solution)/shard_map/ppermute | solution.py:14
  7.9 9.7 %collective-permute-start.6 = (bf16[1,1,256,256]{3,2,1,0:T(8,128)(2,1)}, bf16[1,1,256,256]{3,2,1,0:T(8,128)(2,1)S(1)}, u32[]{:S(2)}, u32[]{:S(2)}) collective-permute-start(bf16[1,1,256,256]{3,2,1,0:T(8,128)(2,1)} %param.8), channel_id=1, source_target_pairs={{0,12},{1,8},{2,4},{3,0},{4,13},{5,9},{6,5},{7,1},{8,14},{9,10},{1... | collective-permute-start | bytes 393224 | tf_op jit(solution)/shard_map/ppermute | solution.py:14
  13.3 6.9 %collective-permute-start.5 = (bf16[1,1,256,256]{3,2,1,0:T(8,128)(2,1)}, bf16[1,1,256,256]{3,2,1,0:T(8,128)(2,1)S(1)}, u32[]{:S(2)}, u32[]{:S(2)}) collective-permute-start(bf16[1,1,256,256]{3,2,1,0:T(8,128)(2,1)} %param.8), channel_id=1, source_target_pairs={{0,8},{1,12},{2,0},{3,4},{4,9},{5,13},{6,1},{7,5},{8,10},{9,14},{1... | collective-permute-start | bytes 393224 | tf_op jit(solution)/shard_map/ppermute | solution.py:14
  14.5 5.8 %copy-start.3 = (s32[4]{0:T(128)S(1)}, s32[4]{0:T(128)}, u32[]{:S(2)}) copy-start(s32[4]{0:T(128)} %cols.3) | copy-start | bytes 52
  14.5 5.7 %copy-start.4 = (s32[1,4]{1,0:T(1,128)S(1)}, s32[1,4]{1,0:T(1,128)}, u32[]{:S(2)}) copy-start(s32[1,4]{1,0:T(1,128)} %live.3) | copy-start | bytes 52
  20.2 1.0 %copy-start = (bf16[1,4,256,256]{3,2,1,0:T(8,128)(2,1)S(1)}, bf16[1,4,256,256]{3,2,1,0:T(8,128)(2,1)}, u32[]{:S(2)}) copy-start(bf16[1,4,256,256]{3,2,1,0:T(8,128)(2,1)} %tiles.1) | copy-start | bytes 1572868
  21.3 0.9 %copy-start.1 = (bf16[1,1,256,256]{3,2,1,0:T(8,128)(2,1)S(1)}, bf16[1,1,256,256]{3,2,1,0:T(8,128)(2,1)}, u32[]{:S(2)}) copy-start(bf16[1,1,256,256]{3,2,1,0:T(8,128)(2,1)} %refs_0_.1) | copy-start | bytes 393220
  24.1 1.8 %collective-permute-start.7 = (f32[8,256]{1,0:T(8,128)S(1)}, f32[8,256]{1,0:T(8,128)S(1)}, u32[]{:S(2)}, u32[]{:S(2)}) collective-permute-start(f32[8,256]{1,0:T(8,128)S(1)} %get-tuple-element.9), channel_id=1, source_target_pairs={{0,1},{1,0},{2,3},{3,2},{4,5},{5,4},{6,7},{7,6},{8,9},{9,8},{10,11... | collective-permute-start | bytes 24584 | tf_op jit(solution)/shard_map/ppermute | solution.py:14
  25.9 6.4 %collective-permute-start.8 = (f32[8,256]{1,0:T(8,128)S(1)}, f32[8,256]{1,0:T(8,128)S(1)}, u32[]{:S(2)}, u32[]{:S(2)}) collective-permute-start(f32[8,256]{1,0:T(8,128)S(1)} %add.12), channel_id=1, source_target_pairs={{0,2},{1,3},{2,0},{3,1},{4,6},{5,7},{6,4},{7,5},{8,10},{9,11},{10,... | collective-permute-start | bytes 24584 | tf_op jit(solution)/shard_map/ppermute | solution.py:14
  32.3 3.7 %collective-permute-start.9 = (f32[8,256]{1,0:T(8,128)S(1)}, f32[8,256]{1,0:T(8,128)S(1)}, u32[]{:S(2)}, u32[]{:S(2)}) collective-permute-start(f32[8,256]{1,0:T(8,128)S(1)} %add.13), channel_id=1, source_target_pairs={{0,4},{1,5},{2,6},{3,7},{4,0},{5,1},{6,2},{7,3},{8,12},{9,13},{10,... | collective-permute-start | bytes 24584 | tf_op jit(solution)/shard_map/ppermute | solution.py:14
  35.9 4.5 %collective-permute-start.10 = (f32[8,256]{1,0:T(8,128)S(1)}, f32[8,256]{1,0:T(8,128)S(1)}, u32[]{:S(2)}, u32[]{:S(2)}) collective-permute-start(f32[8,256]{1,0:T(8,128)S(1)} %add.14), channel_id=1, source_target_pairs={{0,8},{1,9},{2,10},{3,11},{4,12},{5,13},{6,14},{7,15},{8,0},{9,1},... | collective-permute-start | bytes 24584 | tf_op jit(solution)/shard_map/ppermute | solution.py:14
  38.4 0.9 %copy-start.2 = (bf16[1,1,256,256]{3,2,1,0:T(8,128)(2,1)S(1)}, bf16[1,1,256,256]{3,2,1,0:T(8,128)(2,1)}, u32[]{:S(2)}) copy-start(bf16[1,1,256,256]{3,2,1,0:T(8,128)(2,1)} %get-tuple-element.4.image) | copy-start | bytes 393220

commit v2 on v1

v2 whole, which is shorter than its diff:
```python
import functools

import jax
import jax.numpy as jnp
import numpy as np
from jax import lax
from jax.experimental import pallas as pl
from jax.experimental.pallas import tpu as pltpu
from jax.sharding import PartitionSpec as P

AXES = ("blk", "term")


def move(value, pairs, terms):
    return lax.ppermute(
        value, AXES, [(a * terms + b, c * terms + d) for (a, b), (c, d) in pairs]
    )


def right_routes(blocks, terms, own):
    half = blocks // 2
    steps, arrives = [], np.zeros((blocks, terms, blocks), np.int32)
    for k in range(blocks):
        pairs = []
        for c in range(blocks):
            for t in range(terms):
                i = (c % own) * terms + t
                a = ((i % 2) * half + i // 2) ^ k
                arrives[a, c // own, k] = i
                if (c, t) != (a, c // own):
                    pairs.append(((c, t), (a, c // own)))
        steps.append(pairs)
    return steps, arrives


def keep_mask(width, rows, cols, live):
    at_row = lax.broadcasted_iota(jnp.int32, (width, width), 0)
    at_col = lax.broadcasted_iota(jnp.int32, (width, width), 1)
    return (at_row < rows) & (at_col < cols) & (live == 1)


def dot(a, b):
    return jnp.dot(a, b, preferred_element_type=jnp.float32)


def left_kernel(terms, own, place, rows, cols, live, two_site, *refs):
    lefts, (products, tiles, sem) = refs[:terms], refs[terms:]
    blk, term = place[0], place[1]
    width = tiles.shape[-1]
    copy = pltpu.make_async_copy(two_site.at[0, pl.ds(term * own, own)], tiles, sem)
    copy.start()
    copy.wait()
    for o in range(own):
        col = term * own + o
        keep = keep_mask(width, rows[0], cols[col], live[0, col])
        start = jnp.where(keep, tiles[o], jnp.zeros((), tiles.dtype))
        for m in range(terms):
            products[o, term ^ m] = dot(lefts[m][0, 0], start).astype(jnp.bfloat16)


def right_sum(terms, own, place, arrives, products, mine, rights, total):
    total[...] = jnp.zeros_like(total)
    for k, right in enumerate(rights):
        o, t = arrives[k] // terms, arrives[k] % terms
        total[o] += dot(products[o, t], right[0, 0])

    @pl.when(place[0] // own == place[1])
    def _():
        o = place[0] % own
        total[o] += dot(products[o, place[1]], mine[0, 0])


def first_kernel(terms, own, place, arrives, rows, cols, live, products, mine, *refs):
    rights, (image, partial, total) = refs[:-3], refs[-3:]
    width = total.shape[-1]
    right_sum(terms, own, place, arrives, products, mine, rights, total)
    partial[...] = jnp.zeros_like(partial)
    for o in range(own):
        col = place[1] * own + o
        keep = keep_mask(width, rows[0], cols[col], live[0, col])
        out = jnp.where(keep, total[o], 0.0).astype(jnp.bfloat16)
        image[0, o] = out
        out = out.astype(jnp.float32)
        squares = jnp.sum((out * out).reshape(-1, 8, width), axis=0)
        for lane in range(0, width, 128):
            partial[...] += squares[:, lane : lane + 128]


def second_kernel(terms, own, place, arrives, rows, cols, live, image, mine, *refs):
    lefts, rights = refs[:terms], refs[terms:-4]
    final, raw, products, total = refs[-4:]
    width = total.shape[-1]
    final[...] = image[...]
    for o in range(own):
        for m in range(terms):
            products[o, place[1] ^ m] = dot(lefts[m][0, 0], image[0, o]).astype(jnp.bfloat16)
    right_sum(terms, own, place, arrives, products, mine, rights, total)
    for o in range(own):
        col = place[1] * own + o
        keep = keep_mask(width, rows[0], cols[col], live[0, col])
        raw[0, o] = jnp.where(keep, total[o], 0.0)


def scale_kernel(count, raw, norm, other, image):
    norm_sum = jnp.sum(norm[...] + other[...])
    image[...] = (raw[...] * lax.rsqrt(norm_sum / count + 1e-06)).astype(jnp.bfloat16)


def local(blocks, terms, two_site, left_env, right_env, row_size, col_size, block_live):
    width = two_site.shape[2]
    n_cols = two_site.shape[1]
    own = n_cols // terms
    vmem, smem = pl.BlockSpec(memory_space=pltpu.VMEM), pl.BlockSpec(memory_space=pltpu.SMEM)
    anywhere = pl.BlockSpec(memory_space=pl.ANY)
    params = pltpu.CompilerParams(vmem_limit_bytes=32 * 1024 * 1024)
    blk, term = lax.axis_index("blk"), lax.axis_index("term")
    place = jnp.stack([blk, term]).astype(jnp.int32)
    everyone = [(a, t) for a in range(blocks) for t in range(terms)]

    steps, table = right_routes(blocks, terms, own)
    arrives = jnp.asarray(table)[blk, term]
    rights = [move(right_env, pairs, terms) for pairs in steps]
    lefts = [left_env]
    for m in range(1, terms):
        if m % 2 == 0:
            lefts.append(move(left_env, [((a, t), (a, t ^ m)) for a, t in everyone], terms))
        else:
            lefts.append(move(lefts[m - 1], [((a, t), (a, t ^ 1)) for a, t in everyone], terms))

    tile = (own, width, width)
    dots = own * terms * 2 * width**3
    products = pl.pallas_call(
        functools.partial(left_kernel, terms, own),
        out_shape=jax.ShapeDtypeStruct((own, terms, width, width), jnp.bfloat16),
        in_specs=[smem] * 4 + [anywhere] + [vmem] * terms,
        out_specs=vmem,
        scratch_shapes=[pltpu.VMEM(tile, jnp.bfloat16), pltpu.SemaphoreType.DMA],
        compiler_params=params,
        cost_estimate=pl.CostEstimate(flops=dots, bytes_accessed=8 * width * width, transcendentals=0),
    )(place, row_size, col_size, block_live, two_site, *lefts)

    first, partial = pl.pallas_call(
        functools.partial(first_kernel, terms, own),
        out_shape=(
            jax.ShapeDtypeStruct((1,) + tile, jnp.bfloat16),
            jax.ShapeDtypeStruct((8, 128), jnp.float32),
        ),
        in_specs=[smem] * 5 + [vmem] * (2 + blocks),
        out_specs=(vmem,) * 2,
        scratch_shapes=[pltpu.VMEM(tile, jnp.float32)],
        compiler_params=params,
        cost_estimate=pl.CostEstimate(flops=dots, bytes_accessed=8 * width * width, transcendentals=0),
    )(place, arrives, row_size, col_size, block_live, products, right_env, *rights)

    first_image, raw = pl.pallas_call(
        functools.partial(second_kernel, terms, own),
        out_shape=(
            jax.ShapeDtypeStruct((1,) + tile, jnp.bfloat16),
            jax.ShapeDtypeStruct((1,) + tile, jnp.float32),
        ),
        in_specs=[smem] * 5 + [vmem] * (2 + terms + blocks),
        out_specs=(vmem,) * 2,
        scratch_shapes=[
            pltpu.VMEM((own, terms, width, width), jnp.bfloat16),
            pltpu.VMEM(tile, jnp.float32),
        ],
        compiler_params=params,
        cost_estimate=pl.CostEstimate(flops=2 * dots, bytes_accessed=8 * width * width, transcendentals=0),
    )(place, arrives, row_size, col_size, block_live, first, right_env, *lefts, *rights)

    other = jnp.zeros_like(partial)
    flips = [(0, 1 << s) for s in range((terms - 1).bit_length())]
    flips += [(1 << s, 0) for s in range((blocks - 1).bit_length())]
    norm = partial
    for da, dt in flips:
        norm = norm + other
        other = move(norm, [((a, t), (a ^ da, t ^ dt)) for a, t in everyone], terms)

    second_image = pl.pallas_call(
        functools.partial(scale_kernel, float(blocks * n_cols * width * width)),
        out_shape=jax.ShapeDtypeStruct((1,) + tile, jnp.bfloat16),
        in_specs=[vmem] * 3,
        out_specs=vmem,
        compiler_params=params,
    )(raw, norm, other)
    return first_image, second_image


def solution(mesh):
    return jax.shard_map(
        functools.partial(local, mesh.shape["blk"], mesh.shape["term"]),
        mesh=mesh,
        in_specs=(
            P(("runs", "blk"), None, None, None),
            P(("runs", "term"), "blk", None, None),
            P(("runs", "term"), "blk", None, None),
            P(("runs", "blk")),
            P("runs"),
            P(("runs", "blk"), None),
        ),
        out_specs=(P(("runs", "blk"), "term", None, None), P(("runs", "blk"), "term", None, None)),
        check_vma=False,
    )
```

time: 41.6 us -> 36.3 us (0.87)
  waiting for transfers between devices: 11 us -> 4.71 us
  Pallas kernels: 3.89 us -> 5.12 us
    ppermute x11, waiting for transfers between devices: 11 us -> 4.71 us  [move(): lax.ppermute(value, AXES, [(a * terms + b, c * terms + d) for (a, b), (c,...]
    pallas_call x1 -> x2, Pallas kernels: 1.15 us -> 3.12 us  [the longest x1 2.02 us: local(): pl.pallas_call(functools.partial(second_kernel, terms, own), out_shape=(j...]
    unnamed x10 -> x12, local copies, waits for them, and re-layouts: 2.86 us -> 1.96 us
    pallas_call x1, Pallas kernels: 1.9 us -> 1.17 us  [local(): pl.pallas_call(functools.partial(first_kernel, terms, own), out_shape=(ja...]
    squeeze x0 -> x1, local copies, waits for them, and re-layouts: none -> 0.7 us  [local(): arrives = jnp.asarray(table)[blk, term]]
  transfers between devices with their start and end apart: 11 -> 11, of which waited for: 7 -> 3; matrix products, arithmetic and copies ran while one was open for 0% -> 2% of each run, Pallas kernels for 3% -> 9%
where the time goes in v2:
time: 36.3 us; the launch traced here: 36.1 us
  starting transfers between devices  22.1 us (61%)
  Pallas kernels  5.12 us (14%)
  waiting for transfers between devices  4.71 us (13%)
  local copies, waits for them, and re-layouts  2.66 us (7%)
  between operations  1.42 us (4%)
    ppermute x11, starting transfers between devices, move(): lax.ppermute(value, AXES, [(a * terms + b, c * terms + d) for (a, b), (c,...  22.1 us
    ppermute x11, waiting for transfers between devices, move(): lax.ppermute(value, AXES, [(a * terms + b, c * terms + d) for (a, b), (c,...  4.71 us
    pallas_call x1, Pallas kernels, local(): pl.pallas_call(functools.partial(second_kernel, terms, own), out_shape=(j...  2.02 us
    unnamed x12, local copies, waits for them, and re-layouts  1.96 us
    pallas_call x1, Pallas kernels, local(): pl.pallas_call(functools.partial(first_kernel, terms, own), out_shape=(ja...  1.17 us
    pallas_call x1, Pallas kernels, local(): pl.pallas_call(functools.partial(left_kernel, terms, own), out_shape=jax....  1.1 us
    pallas_call x1, Pallas kernels, local(): pl.pallas_call(functools.partial(scale_kernel, float(blocks * n_cols * wi...  0.83 us
  transfers between devices with their start and end apart: 11, of which 3 were waited for; matrix products, arithmetic and copies ran while one was open for 2% of the time, Pallas kernels for 9%

profile of v2, /device:TPU:0, one launch (start us, length us, event | category | flops | bytes accessed | tf_op | source)
XLA Modules:
  0.0 36.1 jit_solution(14256093653578877457)
XLA Ops:
  0.6 3.0 %collective-permute-start.1 = (bf16[1,1,256,256]{3,2,1,0:T(8,128)(2,1)}, bf16[1,1,256,256]{3,2,1,0:T(8,128)(2,1)S(1)}, u32[]{:S(2)}, u32[]{:S(2)}) collective-permute-start(bf16[1,1,256,256]{3,2,1,0:T(8,128)(2,1)} %refs_0_.3), channel_id=1, source_target_pairs={{0,2},{1,3},{2,0},{3,1},{4,6},{5,7},{6,4},{7,5},{8,10},{9,11},{10,... | collective-permute-start | bytes 393224 | tf_op jit(solution)/shard_map/ppermute | solution.py:15
  3.6 0.0 collective-permute-start
  3.6 5.5 %collective-permute-start.6 = (bf16[1,1,256,256]{3,2,1,0:T(8,128)(2,1)}, bf16[1,1,256,256]{3,2,1,0:T(8,128)(2,1)S(1)}, u32[]{:S(2)}, u32[]{:S(2)}) collective-permute-start(bf16[1,1,256,256]{3,2,1,0:T(8,128)(2,1)} %mine.3), channel_id=1, source_target_pairs={{0,12},{1,4},{2,8},{3,0},{4,13},{6,9},{7,1},{8,14},{9,6},{11,2},{1... | collective-permute-start | bytes 393224 | tf_op jit(solution)/shard_map/ppermute | solution.py:15
  9.1 0.6 %collective-permute-start.5 = (bf16[1,1,256,256]{3,2,1,0:T(8,128)(2,1)}, bf16[1,1,256,256]{3,2,1,0:T(8,128)(2,1)S(1)}, u32[]{:S(2)}, u32[]{:S(2)}) collective-permute-start(bf16[1,1,256,256]{3,2,1,0:T(8,128)(2,1)} %mine.3), channel_id=1, source_target_pairs={{0,8},{1,0},{2,12},{3,4},{4,9},{5,1},{6,13},{7,5},{8,10},{9,2},{10... | collective-permute-start | bytes 393224 | tf_op jit(solution)/shard_map/ppermute | solution.py:15
  9.7 0.2 collective-permute-start.4
  10.0 0.0 collective-permute-done.1.refs_2_
  10.0 0.7 %collective-permute-start.3 = (bf16[1,1,256,256]{3,2,1,0:T(8,128)(2,1)}, bf16[1,1,256,256]{3,2,1,0:T(8,128)(2,1)S(1)}, u32[]{:S(2)}, u32[]{:S(2)}) collective-permute-start(bf16[1,1,256,256]{3,2,1,0:T(8,128)(2,1)} %mine.3), channel_id=1, source_target_pairs={{1,8},{2,4},{3,12},{4,1},{5,9},{6,5},{7,13},{8,2},{9,10},{10,6},{1... | collective-permute-start | bytes 393224 | tf_op jit(solution)/shard_map/ppermute | solution.py:15
  10.6 0.0 collective-permute-done.refs_1_
  10.6 3.7 %collective-permute-start.2 = (bf16[1,1,256,256]{3,2,1,0:T(8,128)(2,1)S(1)}, bf16[1,1,256,256]{3,2,1,0:T(8,128)(2,1)S(1)}, u32[]{:S(2)}, u32[]{:S(2)}) collective-permute-start(bf16[1,1,256,256]{3,2,1,0:T(8,128)(2,1)S(1)} %collective-permute-done.1.refs_2_), channel_id=1, source_target_pairs={{0,1},{1,0},{2,3},{3,2},{4,5},{5,4},{6,7},{7,6},{8,9},{9,8},{10,11... | collective-permute-start | bytes 393224 | tf_op jit(solution)/shard_map/ppermute | solution.py:15
  14.4 0.1 pad_add_fusion.place
  15.1 0.0 copy-start.4
  15.1 0.0 copy-start.5
  15.1 0.7 %dynamic-slice_bitcast_fusion.arrives = s32[4]{0:T(128)S(1)} fusion(s32[4,4,4]{2,1,0:T(4,128)} %constant.13.clone, s32[]{:T(128)S(6)} %select_n.6, s32[]{:T(128)S(6)} %select_n.7), kind=kLoop, calls=%fused_computation.1 | loop fusion | bytes 40 | tf_op jit(solution)/shard_map/squeeze | solution.py:121
  15.8 0.0 collective-permute-done.2.refs_3_
  15.8 0.0 copy-start
  15.8 0.9 %copy-done = bf16[1,1,256,256]{3,2,1,0:T(8,128)(2,1)S(1)} copy-done((bf16[1,1,256,256]{3,2,1,0:T(8,128)(2,1)S(1)}, bf16[1,1,256,256]{3,2,1,0:T(8,128)(2,1)}, u32[]{:S(2)}) %copy-start) | copy-done | bytes 131096
  16.7 1.0 %copy-done.3 = bf16[1,4,256,256]{3,2,1,0:T(8,128)(2,1)S(1)} copy-done((bf16[1,4,256,256]{3,2,1,0:T(8,128)(2,1)S(1)}, bf16[1,4,256,256]{3,2,1,0:T(8,128)(2,1)}, u32[]{:S(2)}) %copy-start.3) | copy-done | bytes 524312
  17.8 1.1 %shard_map.86.products = bf16[1,4,256,256]{3,2,1,0:T(8,128)(2,1)S(1)} custom-call(s32[2]{0:T(128)S(1)} %pad_add_fusion.place, s32[1]{0:T(128)S(6)} %copy.9.rows, s32[4]{0:T(128)S(1)} %copy-done.4, s32[1,4]{1,0:T(1,128)S(1)} %copy-done.5, bf16[1,4,256,256]{3,2,1,0:T(8,128)(2,1)S(1)} %copy-done.3, bf16[1,1,256,256]{3,2,1,0:T(8,128)(2,1)S(1)} %copy-done, ...), custom_call_target="tpu_custom_call" | custom-call | flops 134217728 | bytes 524288 | tf_op jit(solution)/shard_map/pallas_call | solution.py:132
  18.9 0.0 copy-start.1
  18.9 0.0 collective-permute-done.5.refs_2_.refs_6_
  18.9 0.0 collective-permute-done.4.refs_1_.refs_5_
  19.0 1.2 %shard_map.87 = (bf16[1,1,256,256]{3,2,1,0:T(8,128)(2,1)S(1)}, f32[8,128]{1,0:T(8,128)S(1)}) custom-call(s32[2]{0:T(128)S(1)} %pad_add_fusion.place, s32[4]{0:T(128)S(1)} %dynamic-slice_bitcast_fusion.arrives, s32[1]{0:T(128)S(6)} %copy.9.rows, s32[4]{0:T(128)S(1)} %copy-done.4, s32[1,4]{1,0:T(1,128)S(1)} %copy-done.5, ...), custom_call_target="tpu_custom_call" | custom-call | flops 134217728 | bytes 524288 | tf_op jit(solution)/shard_map/pallas_call | solution.py:142
  20.1 0.1 collective-permute-start.7
  20.2 1.2 %collective-permute-done.7 = f32[8,128]{1,0:T(8,128)S(1)} collective-permute-done((f32[8,128]{1,0:T(8,128)S(1)}, f32[8,128]{1,0:T(8,128)S(1)}, u32[]{:S(2)}, u32[]{:S(2)}) %collective-permute-start.7) | collective-permute-done | bytes 4128 | tf_op jit(solution)/shard_map/ppermute | solution.py:15
  21.4 3.7 %collective-permute-start.8 = (f32[8,128]{1,0:T(8,128)S(1)}, f32[8,128]{1,0:T(8,128)S(1)}, u32[]{:S(2)}, u32[]{:S(2)}) collective-permute-start(f32[8,128]{1,0:T(8,128)S(1)} %add.17), channel_id=1, source_target_pairs={{0,2},{1,3},{2,0},{3,1},{4,6},{5,7},{6,4},{7,5},{8,10},{9,11},{10,... | collective-permute-start | bytes 12296 | tf_op jit(solution)/shard_map/ppermute | solution.py:15
  25.0 1.6 %collective-permute-done.8 = f32[8,128]{1,0:T(8,128)S(1)} collective-permute-done((f32[8,128]{1,0:T(8,128)S(1)}, f32[8,128]{1,0:T(8,128)S(1)}, u32[]{:S(2)}, u32[]{:S(2)}) %collective-permute-start.8) | collective-permute-done | bytes 4128 | tf_op jit(solution)/shard_map/ppermute | solution.py:15
  26.6 1.7 %collective-permute-start.9 = (f32[8,128]{1,0:T(8,128)S(1)}, f32[8,128]{1,0:T(8,128)S(1)}, u32[]{:S(2)}, u32[]{:S(2)}) collective-permute-start(f32[8,128]{1,0:T(8,128)S(1)} %add.18), channel_id=1, source_target_pairs={{0,4},{1,5},{2,6},{3,7},{4,0},{5,1},{6,2},{7,3},{8,12},{9,13},{10,... | collective-permute-start | bytes 12296 | tf_op jit(solution)/shard_map/ppermute | solution.py:15
  28.3 1.9 %collective-permute-done.9 = f32[8,128]{1,0:T(8,128)S(1)} collective-permute-done((f32[8,128]{1,0:T(8,128)S(1)}, f32[8,128]{1,0:T(8,128)S(1)}, u32[]{:S(2)}, u32[]{:S(2)}) %collective-permute-start.9) | collective-permute-done | bytes 4128 | tf_op jit(solution)/shard_map/ppermute | solution.py:15
  30.2 3.0 %collective-permute-start.10 = (f32[8,128]{1,0:T(8,128)S(1)}, f32[8,128]{1,0:T(8,128)S(1)}, u32[]{:S(2)}, u32[]{:S(2)}) collective-permute-start(f32[8,128]{1,0:T(8,128)S(1)} %add.19.norm), channel_id=1, source_target_pairs={{0,8},{1,9},{2,10},{3,11},{4,12},{5,13},{6,14},{7,15},{8,0},{9,1},... | collective-permute-start | bytes 12296 | tf_op jit(solution)/shard_map/ppermute | solution.py:15
  33.2 2.0 %shard_map.88 = (bf16[1,1,256,256]{3,2,1,0:T(8,128)(2,1)}, f32[1,1,256,256]{3,2,1,0:T(8,128)S(1)}) custom-call(s32[2]{0:T(128)S(1)} %pad_add_fusion.place, s32[4]{0:T(128)S(1)} %dynamic-slice_bitcast_fusion.arrives, s32[1]{0:T(128)S(6)} %copy.9.rows, s32[4]{0:T(128)S(1)} %copy-done.4, s32[1,4]{1,0:T(1,128)S(1)} %copy-done.5, ...), custom_call_target="tpu_custom_call" | custom-call | flops 268435456 | bytes 524288 | tf_op jit(solution)/shard_map/pallas_call | solution.py:155
  35.2 0.0 collective-permute-done.10.other
  35.2 0.8 %shard_map.89 = bf16[1,1,256,256]{3,2,1,0:T(8,128)(2,1)} custom-call(f32[1,1,256,256]{3,2,1,0:T(8,128)S(1)} %get-tuple-element.8.raw, f32[8,128]{1,0:T(8,128)S(1)} %add.19.norm, f32[8,128]{1,0:T(8,128)S(1)} %collective-permute-done.10.other), custom_call_target="tpu_custom_call" | custom-call | tf_op jit(solution)/shard_map/pallas_call | solution.py:179
  (11 shorter events, 0.0 us)
Async XLA Ops:
  0.6 9.3 %collective-permute-start.1 = (bf16[1,1,256,256]{3,2,1,0:T(8,128)(2,1)}, bf16[1,1,256,256]{3,2,1,0:T(8,128)(2,1)S(1)}, u32[]{:S(2)}, u32[]{:S(2)}) collective-permute-start(bf16[1,1,256,256]{3,2,1,0:T(8,128)(2,1)} %refs_0_.3), channel_id=1, source_target_pairs={{0,2},{1,3},{2,0},{3,1},{4,6},{5,7},{6,4},{7,5},{8,10},{9,11},{10,... | collective-permute-start | bytes 393224 | tf_op jit(solution)/shard_map/ppermute | solution.py:15
  3.6 7.0 %collective-permute-start = (bf16[1,1,256,256]{3,2,1,0:T(8,128)(2,1)}, bf16[1,1,256,256]{3,2,1,0:T(8,128)(2,1)S(1)}, u32[]{:S(2)}, u32[]{:S(2)}) collective-permute-start(bf16[1,1,256,256]{3,2,1,0:T(8,128)(2,1)} %refs_0_.3), channel_id=1, source_target_pairs={{0,1},{1,0},{2,3},{3,2},{4,5},{5,4},{6,7},{7,6},{8,9},{9,8},{10,11... | collective-permute-start | bytes 393224 | tf_op jit(solution)/shard_map/ppermute | solution.py:15
  3.6 15.3 %collective-permute-start.6 = (bf16[1,1,256,256]{3,2,1,0:T(8,128)(2,1)}, bf16[1,1,256,256]{3,2,1,0:T(8,128)(2,1)S(1)}, u32[]{:S(2)}, u32[]{:S(2)}) collective-permute-start(bf16[1,1,256,256]{3,2,1,0:T(8,128)(2,1)} %mine.3), channel_id=1, source_target_pairs={{0,12},{1,4},{2,8},{3,0},{4,13},{6,9},{7,1},{8,14},{9,6},{11,2},{1... | collective-permute-start | bytes 393224 | tf_op jit(solution)/shard_map/ppermute | solution.py:15
  9.1 9.8 %collective-permute-start.5 = (bf16[1,1,256,256]{3,2,1,0:T(8,128)(2,1)}, bf16[1,1,256,256]{3,2,1,0:T(8,128)(2,1)S(1)}, u32[]{:S(2)}, u32[]{:S(2)}) collective-permute-start(bf16[1,1,256,256]{3,2,1,0:T(8,128)(2,1)} %mine.3), channel_id=1, source_target_pairs={{0,8},{1,0},{2,12},{3,4},{4,9},{5,1},{6,13},{7,5},{8,10},{9,2},{10... | collective-permute-start | bytes 393224 | tf_op jit(solution)/shard_map/ppermute | solution.py:15
  9.7 9.2 %collective-permute-start.4 = (bf16[1,1,256,256]{3,2,1,0:T(8,128)(2,1)}, bf16[1,1,256,256]{3,2,1,0:T(8,128)(2,1)S(1)}, u32[]{:S(2)}, u32[]{:S(2)}) collective-permute-start(bf16[1,1,256,256]{3,2,1,0:T(8,128)(2,1)} %mine.3), channel_id=1, source_target_pairs={{0,4},{1,12},{2,0},{3,8},{4,5},{5,13},{6,1},{7,9},{8,6},{9,14},{10... | collective-permute-start | bytes 393224 | tf_op jit(solution)/shard_map/ppermute | solution.py:15
  10.0 9.0 %collective-permute-start.3 = (bf16[1,1,256,256]{3,2,1,0:T(8,128)(2,1)}, bf16[1,1,256,256]{3,2,1,0:T(8,128)(2,1)S(1)}, u32[]{:S(2)}, u32[]{:S(2)}) collective-permute-start(bf16[1,1,256,256]{3,2,1,0:T(8,128)(2,1)} %mine.3), channel_id=1, source_target_pairs={{1,8},{2,4},{3,12},{4,1},{5,9},{6,5},{7,13},{8,2},{9,10},{10,6},{1... | collective-permute-start | bytes 393224 | tf_op jit(solution)/shard_map/ppermute | solution.py:15
  10.6 5.2 %collective-permute-start.2 = (bf16[1,1,256,256]{3,2,1,0:T(8,128)(2,1)S(1)}, bf16[1,1,256,256]{3,2,1,0:T(8,128)(2,1)S(1)}, u32[]{:S(2)}, u32[]{:S(2)}) collective-permute-start(bf16[1,1,256,256]{3,2,1,0:T(8,128)(2,1)S(1)} %collective-permute-done.1.refs_2_), channel_id=1, source_target_pairs={{0,1},{1,0},{2,3},{3,2},{4,5},{5,4},{6,7},{7,6},{8,9},{9,8},{10,11... | collective-permute-start | bytes 393224 | tf_op jit(solution)/shard_map/ppermute | solution.py:15
  15.1 0.7 %copy-start.4 = (s32[4]{0:T(128)S(1)}, s32[4]{0:T(128)}, u32[]{:S(2)}) copy-start(s32[4]{0:T(128)} %cols.5) | copy-start | bytes 52
  15.1 0.7 %copy-start.5 = (s32[1,4]{1,0:T(1,128)S(1)}, s32[1,4]{1,0:T(1,128)}, u32[]{:S(2)}) copy-start(s32[1,4]{1,0:T(1,128)} %live.5) | copy-start | bytes 52
  15.8 0.9 %copy-start = (bf16[1,1,256,256]{3,2,1,0:T(8,128)(2,1)S(1)}, bf16[1,1,256,256]{3,2,1,0:T(8,128)(2,1)}, u32[]{:S(2)}) copy-start(bf16[1,1,256,256]{3,2,1,0:T(8,128)(2,1)} %refs_0_.3) | copy-start | bytes 393220
  16.7 1.0 %copy-start.3 = (bf16[1,4,256,256]{3,2,1,0:T(8,128)(2,1)S(1)}, bf16[1,4,256,256]{3,2,1,0:T(8,128)(2,1)}, u32[]{:S(2)}) copy-start(bf16[1,4,256,256]{3,2,1,0:T(8,128)(2,1)} %two_site.1) | copy-start | bytes 1572868
  17.8 1.2 %copy-start.2 = (bf16[1,1,256,256]{3,2,1,0:T(8,128)(2,1)S(1)}, bf16[1,1,256,256]{3,2,1,0:T(8,128)(2,1)}, u32[]{:S(2)}) copy-start(bf16[1,1,256,256]{3,2,1,0:T(8,128)(2,1)} %mine.3) | copy-start | bytes 393220
  18.9 14.3 %copy-start.1 = (bf16[1,1,256,256]{3,2,1,0:T(8,128)(2,1)S(1)}, bf16[1,1,256,256]{3,2,1,0:T(8,128)(2,1)}, u32[]{:S(2)}) copy-start(bf16[1,1,256,256]{3,2,1,0:T(8,128)(2,1)} %refs_0_.3) | copy-start | bytes 393220
  20.1 1.2 %collective-permute-start.7 = (f32[8,128]{1,0:T(8,128)S(1)}, f32[8,128]{1,0:T(8,128)S(1)}, u32[]{:S(2)}, u32[]{:S(2)}) collective-permute-start(f32[8,128]{1,0:T(8,128)S(1)} %get-tuple-element.9), channel_id=1, source_target_pairs={{0,1},{1,0},{2,3},{3,2},{4,5},{5,4},{6,7},{7,6},{8,9},{9,8},{10,11... | collective-permute-start | bytes 12296 | tf_op jit(solution)/shard_map/ppermute | solution.py:15
  21.4 5.2 %collective-permute-start.8 = (f32[8,128]{1,0:T(8,128)S(1)}, f32[8,128]{1,0:T(8,128)S(1)}, u32[]{:S(2)}, u32[]{:S(2)}) collective-permute-start(f32[8,128]{1,0:T(8,128)S(1)} %add.17), channel_id=1, source_target_pairs={{0,2},{1,3},{2,0},{3,1},{4,6},{5,7},{6,4},{7,5},{8,10},{9,11},{10,... | collective-permute-start | bytes 12296 | tf_op jit(solution)/shard_map/ppermute | solution.py:15
  26.6 3.6 %collective-permute-start.9 = (f32[8,128]{1,0:T(8,128)S(1)}, f32[8,128]{1,0:T(8,128)S(1)}, u32[]{:S(2)}, u32[]{:S(2)}) collective-permute-start(f32[8,128]{1,0:T(8,128)S(1)} %add.18), channel_id=1, source_target_pairs={{0,4},{1,5},{2,6},{3,7},{4,0},{5,1},{6,2},{7,3},{8,12},{9,13},{10,... | collective-permute-start | bytes 12296 | tf_op jit(solution)/shard_map/ppermute | solution.py:15
  30.2 5.0 %collective-permute-start.10 = (f32[8,128]{1,0:T(8,128)S(1)}, f32[8,128]{1,0:T(8,128)S(1)}, u32[]{:S(2)}, u32[]{:S(2)}) collective-permute-start(f32[8,128]{1,0:T(8,128)S(1)} %add.19.norm), channel_id=1, source_target_pairs={{0,8},{1,9},{2,10},{3,11},{4,12},{5,13},{6,14},{7,15},{8,0},{9,1},... | collective-permute-start | bytes 12296 | tf_op jit(solution)/shard_map/ppermute | solution.py:15

commit v3 on v0

v3 whole, which is shorter than its diff:
```python
import functools

import jax
import jax.numpy as jnp
from jax import lax
from jax.experimental import pallas as pl
from jax.experimental.pallas import tpu as pltpu
from jax.sharding import PartitionSpec as P

AXES = ("blk", "term")


def move(value, pairs, terms):
    return lax.ppermute(
        value, AXES, [(a * terms + b, c * terms + d) for (a, b), (c, d) in pairs]
    )


def source_number(blocks, blk, step):
    half = blocks // 2
    place = blk ^ step
    return (place % half) * 2 + place // half


def right_routes(blocks, terms, own):
    steps = []
    for k in range(blocks):
        pairs = []
        for a in range(blocks):
            for group in range(terms):
                i = source_number(blocks, a, k)
                source = (group * own + i // terms, i % terms)
                if source != (a, group):
                    pairs.append((source, (a, group)))
        steps.append(pairs)
    return steps


def dot(a, b):
    return jnp.dot(a, b, preferred_element_type=jnp.float32)


def early_kernel(blocks, terms, own, two_site, rows, cols, live, *refs):
    rights, (start, keep, products, tiles, rows_at, cols_at, live_at, sems) = refs[:-8], refs[-8:]
    blk, term = lax.axis_index("blk"), lax.axis_index("term")
    width = tiles.shape[-1]
    copies = [
        pltpu.make_async_copy(two_site.at[0, pl.ds(term * own, own)], tiles, sems.at[0]),
        pltpu.make_async_copy(rows, rows_at, sems.at[1]),
        pltpu.make_async_copy(cols, cols_at, sems.at[2]),
        pltpu.make_async_copy(live, live_at, sems.at[3]),
    ]
    for copy in copies:
        copy.start()
    for copy in copies:
        copy.wait()
    at_row = lax.broadcasted_iota(jnp.int32, (width, width), 0)
    at_col = lax.broadcasted_iota(jnp.int32, (width, width), 1)
    for o in range(own):
        col = term * own + o
        mask = (at_row < rows_at[0]) & (at_col < cols_at[col]) & (live_at[0, col] == 1)
        start[o] = jnp.where(mask, tiles[o], jnp.zeros((), tiles.dtype))
        keep[o] = jnp.where(mask, 1.0, 0.0)
    for k, right in enumerate(rights):
        o = source_number(blocks, blk, k) // terms
        products[k] = dot(start[o], right[0, 0]).astype(jnp.bfloat16)


def finish(blocks, terms, own, tile, keep, mine, lefts, rights, early, products):
    blk, term = lax.axis_index("blk"), lax.axis_index("term")
    for k in range(blocks):
        i = source_number(blocks, blk, k)
        if k < blocks - len(rights):
            products[i] = early[k]
        else:
            right = rights[k - blocks + len(rights)]
            products[i] = dot(tile[i // terms], right[0, 0]).astype(jnp.bfloat16)

    @pl.when(blk // own == term)
    def _():
        o = blk % own
        products[o * terms + term] = dot(tile[o], mine[0, 0]).astype(jnp.bfloat16)

    sums = []
    for o in range(own):
        total = sum(dot(left[0, 0], products[o * terms + (term ^ m)]) for m, left in enumerate(lefts))
        sums.append(jnp.where(keep[o] != 0.0, total, 0.0))
    return sums


def first_kernel(blocks, terms, own, start, keep, early, mine, *refs):
    lefts, rights, (image, partial, products) = refs[:terms], refs[terms:-3], refs[-3:]
    width = start.shape[-1]
    squares = jnp.zeros((8, width), jnp.float32)
    for o, total in enumerate(finish(blocks, terms, own, start, keep, mine, lefts, rights, early, products)):
        out = total.astype(jnp.bfloat16)
        image[o] = out
        out = out.astype(jnp.float32)
        squares += jnp.sum((out * out).reshape(-1, 8, width), axis=0)
    partial[...] = sum(squares[:, lane : lane + 128] for lane in range(0, width, 128))


def second_kernel(blocks, terms, own, image, keep, mine, *refs):
    lefts, rights, (final, raw, products) = refs[:terms], refs[terms:-3], refs[-3:]
    final[0] = image[...]
    for o, total in enumerate(finish(blocks, terms, own, image, keep, mine, lefts, rights, None, products)):
        raw[0, o] = total


def scale_kernel(count, raw, norm, other, image):
    norm_sum = jnp.sum(norm[...] + other[...])
    image[...] = (raw[...] * lax.rsqrt(norm_sum / count + 1e-06)).astype(jnp.bfloat16)


def cost(dots, width):
    return pl.CostEstimate(flops=dots * 2 * width**3, bytes_accessed=8 * width**2, transcendentals=0)


def local(blocks, terms, two_site, left_env, right_env, row_size, col_size, block_live):
    width = two_site.shape[2]
    n_cols = two_site.shape[1]
    own = n_cols // terms
    vmem, hbm = pl.BlockSpec(memory_space=pltpu.VMEM), pl.BlockSpec(memory_space=pltpu.HBM)
    params = pltpu.CompilerParams(vmem_limit_bytes=32 * 1024 * 1024)
    everyone = [(a, t) for a in range(blocks) for t in range(terms)]

    rights = [move(right_env, pairs, terms) for pairs in right_routes(blocks, terms, own)]
    lefts = [left_env] + [None] * (terms - 1)
    for m in list(range(1, terms, 2)) + list(range(2, terms, 2)):
        source, hop = (left_env, m) if m % 2 else (lefts[m + 1], 1)
        lefts[m] = move(source, [((a, t), (a, t ^ hop)) for a, t in everyone], terms)

    tile = (own, width, width)
    early = blocks // 2
    start, keep, products = pl.pallas_call(
        functools.partial(early_kernel, blocks, terms, own),
        out_shape=(
            jax.ShapeDtypeStruct(tile, jnp.bfloat16),
            jax.ShapeDtypeStruct(tile, jnp.float32),
            jax.ShapeDtypeStruct((early, width, width), jnp.bfloat16),
        ),
        in_specs=[hbm] * 4 + [vmem] * early,
        out_specs=(vmem,) * 3,
        scratch_shapes=[
            pltpu.VMEM(tile, jnp.bfloat16),
            pltpu.SMEM(row_size.shape, jnp.int32),
            pltpu.SMEM(col_size.shape, jnp.int32),
            pltpu.SMEM(block_live.shape, jnp.int32),
            pltpu.SemaphoreType.DMA((4,)),
        ],
        compiler_params=params,
        cost_estimate=cost(early, width),
    )(two_site, row_size, col_size, block_live, *rights[:early])

    work = [pltpu.VMEM((blocks, width, width), jnp.bfloat16)]
    first, partial = pl.pallas_call(
        functools.partial(first_kernel, blocks, terms, own),
        out_shape=(
            jax.ShapeDtypeStruct(tile, jnp.bfloat16),
            jax.ShapeDtypeStruct((8, 128), jnp.float32),
        ),
        in_specs=[vmem] * (4 + terms + blocks - early),
        out_specs=(vmem,) * 2,
        scratch_shapes=work,
        compiler_params=params,
        cost_estimate=cost(2 * blocks - early, width),
    )(start, keep, products, right_env, *lefts, *rights[early:])

    first_image, raw = pl.pallas_call(
        functools.partial(second_kernel, blocks, terms, own),
        out_shape=(
            jax.ShapeDtypeStruct((1,) + tile, jnp.bfloat16),
            jax.ShapeDtypeStruct((1,) + tile, jnp.float32),
        ),
        in_specs=[vmem] * (3 + terms + blocks),
        out_specs=(vmem,) * 2,
        scratch_shapes=work,
        compiler_params=params,
        cost_estimate=cost(2 * blocks, width),
    )(first, keep, right_env, *lefts, *rights)

    flips = [(0, 1)] + [(0, 1 | 1 << s) for s in range(1, (terms - 1).bit_length())]
    flips += [(1 << s, 1) for s in range((blocks - 1).bit_length())]
    norm, other = partial, None
    for da, dt in flips:
        norm = norm if other is None else norm + other
        other = move(norm, [((a, t), (a ^ da, t ^ dt)) for a, t in everyone], terms)

    second_image = pl.pallas_call(
        functools.partial(scale_kernel, float(blocks * n_cols * width * width)),
        out_shape=jax.ShapeDtypeStruct((1,) + tile, jnp.bfloat16),
        in_specs=[vmem] * 3,
        out_specs=vmem,
        compiler_params=params,
    )(raw, norm, other)
    return first_image, second_image


def solution(mesh):
    return jax.shard_map(
        functools.partial(local, mesh.shape["blk"], mesh.shape["term"]),
        mesh=mesh,
        in_specs=(
            P(("runs", "blk"), None, None, None),
            P(("runs", "term"), "blk", None, None),
            P(("runs", "term"), "blk", None, None),
            P(("runs", "blk")),
            P("runs"),
            P(("runs", "blk"), None),
        ),
        out_specs=(P(("runs", "blk"), "term", None, None), P(("runs", "blk"), "term", None, None)),
        check_vma=False,
    )
```

time: 176 us -> 33.3 us (0.19)
  blocking collectives: 112 us -> 0 us
  waiting for transfers between devices: 41.2 us -> 5.48 us
  starting transfers between devices: 0.08 us -> 21.2 us
  between operations: 15.5 us -> 1.43 us
  Pallas kernels: 0 us -> 3.89 us
  other arithmetic: 3.49 us -> 0.01 us
  matrix products: 2.65 us -> 0 us
    all_to_all x4 -> x0, blocking collectives: 72.4 us -> none  [the longest x2 38.4 us: finish(): lax.all_to_all(left_part, 'blk', split_axis=1, concat_axis=0, tiled=True)]
    reduce_scatter x2 -> x0, waiting for transfers between devices: 41.2 us -> none  [finish(): lax.psum_scatter(partial_rows.astype(jnp.float32).astype(jnp.bfloat16), '...]
    psum x1 -> x0, blocking collectives: 32.9 us -> none  [local(): norm_sum = lax.psum(local_sum, ('blk', 'term'))]
    ppermute x0 -> x11, starting transfers between devices: none -> 21.2 us  [move(): lax.ppermute(value, AXES, [(a * terms + b, c * terms + d) for (a, b), (c,...]
    all_gather x1 -> x0, blocking collectives: 6.51 us -> none  [local(): lax.all_gather(unit, 'term', axis=1, tiled=True)]
    ppermute x0 -> x11, waiting for transfers between devices: none -> 5.48 us  [move(): lax.ppermute(value, AXES, [(a * terms + b, c * terms + d) for (a, b), (c,...]
    pallas_call x0 -> x4, Pallas kernels: none -> 3.89 us  [the longest x1 1.29 us: local(): pl.pallas_call(functools.partial(second_kernel, blocks, terms, own), out_...]
    dot_general x4 -> x0, matrix products: 2.65 us -> none  [the longest x2 1.93 us: left_apply(): jnp.einsum('aij,acjk->acik', left_block, tiles, preferred_element_type=jn...]
  transfers between devices with their start and end apart: 2 -> 11, of which waited for: 2 -> 5; matrix products, arithmetic and copies ran while one was open for 0% -> 0% of each run, Pallas kernels for 0% -> 7%
where the time goes in v3:
time: 33.3 us; the launch traced here: 33.1 us
  starting transfers between devices  21.2 us (64%)
  waiting for transfers between devices  5.48 us (16%)
  Pallas kernels  3.89 us (12%)
  between operations  1.43 us (4%)
  local copies, waits for them, and re-layouts  1.12 us (3%)
    ppermute x11, starting transfers between devices, move(): lax.ppermute(value, AXES, [(a * terms + b, c * terms + d) for (a, b), (c,...  21.2 us
    ppermute x11, waiting for transfers between devices, move(): lax.ppermute(value, AXES, [(a * terms + b, c * terms + d) for (a, b), (c,...  5.48 us
    pallas_call x1, Pallas kernels, local(): pl.pallas_call(functools.partial(second_kernel, blocks, terms, own), out_...  1.29 us
    unnamed x10, local copies, waits for them, and re-layouts  1.12 us
    pallas_call x1, Pallas kernels, local(): pl.pallas_call(functools.partial(early_kernel, blocks, terms, own), out_s...  1.03 us
    pallas_call x1, Pallas kernels, local(): pl.pallas_call(functools.partial(scale_kernel, float(blocks * n_cols * wi...  0.83 us
    pallas_call x1, Pallas kernels, local(): pl.pallas_call(functools.partial(first_kernel, blocks, terms, own), out_s...  0.73 us
  transfers between devices with their start and end apart: 11, of which 5 were waited for; matrix products, arithmetic and copies ran while one was open for 0% of the time, Pallas kernels for 7%

profile of v3, /device:TPU:0, one launch (start us, length us, event | category | flops | bytes accessed | tf_op | source)
XLA Modules:
  0.0 33.1 jit_solution(2011028925958538453)
XLA Ops:
  0.6 0.0 copy-start.4
  0.6 0.0 copy-start.3
  0.7 2.4 %collective-permute-start.3 = (bf16[1,1,256,256]{3,2,1,0:T(8,128)(2,1)}, bf16[1,1,256,256]{3,2,1,0:T(8,128)(2,1)S(1)}, u32[]{:S(2)}, u32[]{:S(2)}) collective-permute-start(bf16[1,1,256,256]{3,2,1,0:T(8,128)(2,1)} %refs_0_.3), channel_id=1, source_target_pairs={{0,3},{1,2},{2,1},{3,0},{4,7},{5,6},{6,5},{7,4},{8,11},{9,10},{10,... | collective-permute-start | bytes 393224 | tf_op jit(solution)/shard_map/ppermute | solution.py:14
  3.1 1.6 %collective-permute-start.1 = (bf16[1,1,256,256]{3,2,1,0:T(8,128)(2,1)}, bf16[1,1,256,256]{3,2,1,0:T(8,128)(2,1)S(1)}, u32[]{:S(2)}, u32[]{:S(2)}) collective-permute-start(bf16[1,1,256,256]{3,2,1,0:T(8,128)(2,1)} %mine.3), channel_id=1, source_target_pairs={{2,0},{6,1},{10,2},{14,3},{0,4},{4,5},{8,6},{12,7},{3,8},{7,9},{11... | collective-permute-start | bytes 393224 | tf_op jit(solution)/shard_map/ppermute | solution.py:14
  4.7 0.7 %collective-permute-start = (bf16[1,1,256,256]{3,2,1,0:T(8,128)(2,1)}, bf16[1,1,256,256]{3,2,1,0:T(8,128)(2,1)S(1)}, u32[]{:S(2)}, u32[]{:S(2)}) collective-permute-start(bf16[1,1,256,256]{3,2,1,0:T(8,128)(2,1)} %mine.3), channel_id=1, source_target_pairs={{4,1},{8,2},{12,3},{2,4},{6,5},{10,6},{14,7},{1,8},{5,9},{9,10},{1... | collective-permute-start | bytes 393224 | tf_op jit(solution)/shard_map/ppermute | solution.py:14
  5.3 3.5 %collective-permute-start.2 = (bf16[1,1,256,256]{3,2,1,0:T(8,128)(2,1)}, bf16[1,1,256,256]{3,2,1,0:T(8,128)(2,1)S(1)}, u32[]{:S(2)}, u32[]{:S(2)}) collective-permute-start(bf16[1,1,256,256]{3,2,1,0:T(8,128)(2,1)} %refs_0_.3), channel_id=1, source_target_pairs={{0,1},{1,0},{2,3},{3,2},{4,5},{5,4},{6,7},{7,6},{8,9},{9,8},{10,11... | collective-permute-start | bytes 393224 | tf_op jit(solution)/shard_map/ppermute | solution.py:14
  8.8 5.2 %collective-permute-start.6 = (bf16[1,1,256,256]{3,2,1,0:T(8,128)(2,1)}, bf16[1,1,256,256]{3,2,1,0:T(8,128)(2,1)S(1)}, u32[]{:S(2)}, u32[]{:S(2)}) collective-permute-start(bf16[1,1,256,256]{3,2,1,0:T(8,128)(2,1)} %mine.3), channel_id=1, source_target_pairs={{3,0},{7,1},{11,2},{15,3},{1,4},{9,6},{13,7},{2,8},{6,9},{14,11},{... | collective-permute-start | bytes 393224 | tf_op jit(solution)/shard_map/ppermute | solution.py:14
  14.0 0.0 collective-permute-done.3.refs_3_
  14.0 0.1 collective-permute-start.5
  14.1 0.0 collective-permute-done.1.refs_1_.refs_5_
  14.1 0.5 %collective-permute-start.4 = (bf16[1,1,256,256]{3,2,1,0:T(8,128)(2,1)S(1)}, bf16[1,1,256,256]{3,2,1,0:T(8,128)(2,1)S(1)}, u32[]{:S(2)}, u32[]{:S(2)}) collective-permute-start(bf16[1,1,256,256]{3,2,1,0:T(8,128)(2,1)S(1)} %collective-permute-done.3.refs_3_), channel_id=1, source_target_pairs={{0,1},{1,0},{2,3},{3,2},{4,5},{5,4},{6,7},{7,6},{8,9},{9,8},{10,11... | collective-permute-start | bytes 393224 | tf_op jit(solution)/shard_map/ppermute | solution.py:14
  15.3 0.0 copy-start
  15.3 0.0 copy-start.1
  15.3 0.0 collective-permute-done.refs_0_.refs_4_
  15.3 0.0 copy-done.4
  15.3 1.1 %copy-done.2 = bf16[1,4,256,256]{3,2,1,0:T(8,128)(2,1)S(1)} copy-done((bf16[1,4,256,256]{3,2,1,0:T(8,128)(2,1)S(1)}, bf16[1,4,256,256]{3,2,1,0:T(8,128)(2,1)}, u32[]{:S(2)}) %copy-start.2) | copy-done | bytes 524312
  16.4 1.0 %shard_map.77 = (bf16[1,256,256]{2,1,0:T(8,128)(2,1)S(1)}, f32[1,256,256]{2,1,0:T(8,128)S(1)}, bf16[2,256,256]{2,1,0:T(8,128)(2,1)S(1)}) custom-call(bf16[1,4,256,256]{3,2,1,0:T(8,128)(2,1)S(1)} %copy-done.2, s32[1]{0:T(128)S(6)} %copy.8.rows, s32[4]{0:T(128)S(1)} %copy-done.3, s32[1,4]{1,0:T(1,128)S(1)} %copy-done.4, ...), custom_call_target="tpu_custom_call" | custom-call | flops 67108864 | bytes 524288 | tf_op jit(solution)/shard_map/pallas_call | solution.py:135
  17.5 0.0 collective-permute-done.2.refs_1_
  17.5 0.0 collective-permute-done.6.refs_5_.refs_7_
  17.5 0.8 %collective-permute-done.5.refs_4_.refs_6_ = bf16[1,1,256,256]{3,2,1,0:T(8,128)(2,1)S(1)} collective-permute-done((bf16[1,1,256,256]{3,2,1,0:T(8,128)(2,1)}, bf16[1,1,256,256]{3,2,1,0:T(8,128)(2,1)S(1)}, u32[]{:S(2)}, u32[]{:S(2)}) %collective-permute-start.5) | collective-permute-done | bytes 131104 | tf_op jit(solution)/shard_map/ppermute | solution.py:14
  18.3 0.0 collective-permute-done.4.refs_2_
  18.3 0.7 %shard_map.78 = (bf16[1,256,256]{2,1,0:T(8,128)(2,1)S(1)}, f32[8,128]{1,0:T(8,128)S(1)}) custom-call(bf16[1,256,256]{2,1,0:T(8,128)(2,1)S(1)} %get-tuple-element.9.start, f32[1,256,256]{2,1,0:T(8,128)S(1)} %get-tuple-element.10.keep, bf16[2,256,256]{2,1,0:T(8,128)(2,1)S(1)} %get-tuple-element.11.early, bf16[1,1,256,256]{3,2,1,0:T(8,128)(2,1)S(1)} %copy-done, ...), custom_call_target="tpu_custom_call" | custom-call | flops 201326592 | bytes 524288 | tf_op jit(solution)/shard_map/pallas_call | solution.py:156
  19.0 0.1 collective-permute-start.7
  19.1 1.2 %collective-permute-done.7 = f32[8,128]{1,0:T(8,128)S(1)} collective-permute-done((f32[8,128]{1,0:T(8,128)S(1)}, f32[8,128]{1,0:T(8,128)S(1)}, u32[]{:S(2)}, u32[]{:S(2)}) %collective-permute-start.7) | collective-permute-done | bytes 4128 | tf_op jit(solution)/shard_map/ppermute | solution.py:14
  20.2 3.7 %collective-permute-start.8 = (f32[8,128]{1,0:T(8,128)S(1)}, f32[8,128]{1,0:T(8,128)S(1)}, u32[]{:S(2)}, u32[]{:S(2)}) collective-permute-start(f32[8,128]{1,0:T(8,128)S(1)} %add.9), channel_id=1, source_target_pairs={{0,3},{1,2},{2,1},{3,0},{4,7},{5,6},{6,5},{7,4},{8,11},{9,10},{10,... | collective-permute-start | bytes 12296 | tf_op jit(solution)/shard_map/ppermute | solution.py:14
  24.0 1.3 %collective-permute-done.8 = f32[8,128]{1,0:T(8,128)S(1)} collective-permute-done((f32[8,128]{1,0:T(8,128)S(1)}, f32[8,128]{1,0:T(8,128)S(1)}, u32[]{:S(2)}, u32[]{:S(2)}) %collective-permute-start.8) | collective-permute-done | bytes 4128 | tf_op jit(solution)/shard_map/ppermute | solution.py:14
  25.3 1.0 %collective-permute-start.9 = (f32[8,128]{1,0:T(8,128)S(1)}, f32[8,128]{1,0:T(8,128)S(1)}, u32[]{:S(2)}, u32[]{:S(2)}) collective-permute-start(f32[8,128]{1,0:T(8,128)S(1)} %add.10), channel_id=1, source_target_pairs={{0,5},{1,4},{2,7},{3,6},{4,1},{5,0},{6,3},{7,2},{8,13},{9,12},{10,... | collective-permute-start | bytes 12296 | tf_op jit(solution)/shard_map/ppermute | solution.py:14
  26.3 2.0 %collective-permute-done.9 = f32[8,128]{1,0:T(8,128)S(1)} collective-permute-done((f32[8,128]{1,0:T(8,128)S(1)}, f32[8,128]{1,0:T(8,128)S(1)}, u32[]{:S(2)}, u32[]{:S(2)}) %collective-permute-start.9) | collective-permute-done | bytes 4128 | tf_op jit(solution)/shard_map/ppermute | solution.py:14
  28.3 2.5 %collective-permute-start.10 = (f32[8,128]{1,0:T(8,128)S(1)}, f32[8,128]{1,0:T(8,128)S(1)}, u32[]{:S(2)}, u32[]{:S(2)}) collective-permute-start(f32[8,128]{1,0:T(8,128)S(1)} %add.11.norm), channel_id=1, source_target_pairs={{0,9},{1,8},{2,11},{3,10},{4,13},{5,12},{6,15},{7,14},{8,1},{9,0},... | collective-permute-start | bytes 12296 | tf_op jit(solution)/shard_map/ppermute | solution.py:14
  30.8 1.3 %shard_map.79 = (bf16[1,1,256,256]{3,2,1,0:T(8,128)(2,1)}, f32[1,1,256,256]{3,2,1,0:T(8,128)S(1)}) custom-call(bf16[1,256,256]{2,1,0:T(8,128)(2,1)S(1)} %get-tuple-element.12.image, f32[1,256,256]{2,1,0:T(8,128)S(1)} %get-tuple-element.10.keep, bf16[1,1,256,256]{3,2,1,0:T(8,128)(2,1)S(1)} %copy-done, bf16[1,1,256,256]{3,2,1,0:T(8,128)(2,1)S(1)} %copy-done.1, ...), custom_call_target="tpu_custom_call" | custom-call | flops 268435456 | bytes 524288 | tf_op jit(solution)/shard_map/pallas_call | solution.py:169
  32.1 0.2 collective-permute-done.10.other
  32.3 0.8 %shard_map.80 = bf16[1,1,256,256]{3,2,1,0:T(8,128)(2,1)} custom-call(f32[1,1,256,256]{3,2,1,0:T(8,128)S(1)} %get-tuple-element.14.raw, f32[8,128]{1,0:T(8,128)S(1)} %add.11.norm, f32[8,128]{1,0:T(8,128)S(1)} %collective-permute-done.10.other), custom_call_target="tpu_custom_call" | custom-call | tf_op jit(solution)/shard_map/pallas_call | solution.py:189
  (7 shorter events, 0.0 us)
Async XLA Ops:
  0.6 14.7 %copy-start.4 = (s32[1,4]{1,0:T(1,128)S(1)}, s32[1,4]{1,0:T(1,128)}, u32[]{:S(2)}) copy-start(s32[1,4]{1,0:T(1,128)} %live.1) | copy-start | bytes 52
  0.6 14.7 %copy-start.3 = (s32[4]{0:T(128)S(1)}, s32[4]{0:T(128)}, u32[]{:S(2)}) copy-start(s32[4]{0:T(128)} %cols.1) | copy-start | bytes 52
  0.7 13.4 %collective-permute-start.3 = (bf16[1,1,256,256]{3,2,1,0:T(8,128)(2,1)}, bf16[1,1,256,256]{3,2,1,0:T(8,128)(2,1)S(1)}, u32[]{:S(2)}, u32[]{:S(2)}) collective-permute-start(bf16[1,1,256,256]{3,2,1,0:T(8,128)(2,1)} %refs_0_.3), channel_id=1, source_target_pairs={{0,3},{1,2},{2,1},{3,0},{4,7},{5,6},{6,5},{7,4},{8,11},{9,10},{10,... | collective-permute-start | bytes 393224 | tf_op jit(solution)/shard_map/ppermute | solution.py:14
  3.1 11.0 %collective-permute-start.1 = (bf16[1,1,256,256]{3,2,1,0:T(8,128)(2,1)}, bf16[1,1,256,256]{3,2,1,0:T(8,128)(2,1)S(1)}, u32[]{:S(2)}, u32[]{:S(2)}) collective-permute-start(bf16[1,1,256,256]{3,2,1,0:T(8,128)(2,1)} %mine.3), channel_id=1, source_target_pairs={{2,0},{6,1},{10,2},{14,3},{0,4},{4,5},{8,6},{12,7},{3,8},{7,9},{11... | collective-permute-start | bytes 393224 | tf_op jit(solution)/shard_map/ppermute | solution.py:14
  4.7 10.6 %collective-permute-start = (bf16[1,1,256,256]{3,2,1,0:T(8,128)(2,1)}, bf16[1,1,256,256]{3,2,1,0:T(8,128)(2,1)S(1)}, u32[]{:S(2)}, u32[]{:S(2)}) collective-permute-start(bf16[1,1,256,256]{3,2,1,0:T(8,128)(2,1)} %mine.3), channel_id=1, source_target_pairs={{4,1},{8,2},{12,3},{2,4},{6,5},{10,6},{14,7},{1,8},{5,9},{9,10},{1... | collective-permute-start | bytes 393224 | tf_op jit(solution)/shard_map/ppermute | solution.py:14
  5.3 12.1 %collective-permute-start.2 = (bf16[1,1,256,256]{3,2,1,0:T(8,128)(2,1)}, bf16[1,1,256,256]{3,2,1,0:T(8,128)(2,1)S(1)}, u32[]{:S(2)}, u32[]{:S(2)}) collective-permute-start(bf16[1,1,256,256]{3,2,1,0:T(8,128)(2,1)} %refs_0_.3), channel_id=1, source_target_pairs={{0,1},{1,0},{2,3},{3,2},{4,5},{5,4},{6,7},{7,6},{8,9},{9,8},{10,11... | collective-permute-start | bytes 393224 | tf_op jit(solution)/shard_map/ppermute | solution.py:14
  8.8 8.7 %collective-permute-start.6 = (bf16[1,1,256,256]{3,2,1,0:T(8,128)(2,1)}, bf16[1,1,256,256]{3,2,1,0:T(8,128)(2,1)S(1)}, u32[]{:S(2)}, u32[]{:S(2)}) collective-permute-start(bf16[1,1,256,256]{3,2,1,0:T(8,128)(2,1)} %mine.3), channel_id=1, source_target_pairs={{3,0},{7,1},{11,2},{15,3},{1,4},{9,6},{13,7},{2,8},{6,9},{14,11},{... | collective-permute-start | bytes 393224 | tf_op jit(solution)/shard_map/ppermute | solution.py:14
  14.0 4.2 %collective-permute-start.5 = (bf16[1,1,256,256]{3,2,1,0:T(8,128)(2,1)}, bf16[1,1,256,256]{3,2,1,0:T(8,128)(2,1)S(1)}, u32[]{:S(2)}, u32[]{:S(2)}) collective-permute-start(bf16[1,1,256,256]{3,2,1,0:T(8,128)(2,1)} %mine.3), channel_id=1, source_target_pairs={{1,0},{5,1},{9,2},{13,3},{3,4},{7,5},{11,6},{15,7},{0,8},{4,9},{8,... | collective-permute-start | bytes 393224 | tf_op jit(solution)/shard_map/ppermute | solution.py:14
  14.1 4.1 %collective-permute-start.4 = (bf16[1,1,256,256]{3,2,1,0:T(8,128)(2,1)S(1)}, bf16[1,1,256,256]{3,2,1,0:T(8,128)(2,1)S(1)}, u32[]{:S(2)}, u32[]{:S(2)}) collective-permute-start(bf16[1,1,256,256]{3,2,1,0:T(8,128)(2,1)S(1)} %collective-permute-done.3.refs_3_), channel_id=1, source_target_pairs={{0,1},{1,0},{2,3},{3,2},{4,5},{5,4},{6,7},{7,6},{8,9},{9,8},{10,11... | collective-permute-start | bytes 393224 | tf_op jit(solution)/shard_map/ppermute | solution.py:14
  15.3 3.0 %copy-start = (bf16[1,1,256,256]{3,2,1,0:T(8,128)(2,1)S(1)}, bf16[1,1,256,256]{3,2,1,0:T(8,128)(2,1)}, u32[]{:S(2)}) copy-start(bf16[1,1,256,256]{3,2,1,0:T(8,128)(2,1)} %mine.3) | copy-start | bytes 393220
  15.3 3.0 %copy-start.1 = (bf16[1,1,256,256]{3,2,1,0:T(8,128)(2,1)S(1)}, bf16[1,1,256,256]{3,2,1,0:T(8,128)(2,1)}, u32[]{:S(2)}) copy-start(bf16[1,1,256,256]{3,2,1,0:T(8,128)(2,1)} %refs_0_.3) | copy-start | bytes 393220
  15.3 1.1 %copy-start.2 = (bf16[1,4,256,256]{3,2,1,0:T(8,128)(2,1)S(1)}, bf16[1,4,256,256]{3,2,1,0:T(8,128)(2,1)}, u32[]{:S(2)}) copy-start(bf16[1,4,256,256]{3,2,1,0:T(8,128)(2,1)} %two_site.1) | copy-start | bytes 1572868
  19.0 1.2 %collective-permute-start.7 = (f32[8,128]{1,0:T(8,128)S(1)}, f32[8,128]{1,0:T(8,128)S(1)}, u32[]{:S(2)}, u32[]{:S(2)}) collective-permute-start(f32[8,128]{1,0:T(8,128)S(1)} %get-tuple-element.15), channel_id=1, source_target_pairs={{0,1},{1,0},{2,3},{3,2},{4,5},{5,4},{6,7},{7,6},{8,9},{9,8},{10,11... | collective-permute-start | bytes 12296 | tf_op jit(solution)/shard_map/ppermute | solution.py:14
  20.2 5.0 %collective-permute-start.8 = (f32[8,128]{1,0:T(8,128)S(1)}, f32[8,128]{1,0:T(8,128)S(1)}, u32[]{:S(2)}, u32[]{:S(2)}) collective-permute-start(f32[8,128]{1,0:T(8,128)S(1)} %add.9), channel_id=1, source_target_pairs={{0,3},{1,2},{2,1},{3,0},{4,7},{5,6},{6,5},{7,4},{8,11},{9,10},{10,... | collective-permute-start | bytes 12296 | tf_op jit(solution)/shard_map/ppermute | solution.py:14
  25.3 3.0 %collective-permute-start.9 = (f32[8,128]{1,0:T(8,128)S(1)}, f32[8,128]{1,0:T(8,128)S(1)}, u32[]{:S(2)}, u32[]{:S(2)}) collective-permute-start(f32[8,128]{1,0:T(8,128)S(1)} %add.10), channel_id=1, source_target_pairs={{0,5},{1,4},{2,7},{3,6},{4,1},{5,0},{6,3},{7,2},{8,13},{9,12},{10,... | collective-permute-start | bytes 12296 | tf_op jit(solution)/shard_map/ppermute | solution.py:14
  28.3 3.9 %collective-permute-start.10 = (f32[8,128]{1,0:T(8,128)S(1)}, f32[8,128]{1,0:T(8,128)S(1)}, u32[]{:S(2)}, u32[]{:S(2)}) collective-permute-start(f32[8,128]{1,0:T(8,128)S(1)} %add.11.norm), channel_id=1, source_target_pairs={{0,9},{1,8},{2,11},{3,10},{4,13},{5,12},{6,15},{7,14},{8,1},{9,0},... | collective-permute-start | bytes 12296 | tf_op jit(solution)/shard_map/ppermute | solution.py:14

commit v4 on v3

--- a/solution.py
+++ b/solution.py
@@ -16,9 +16,17 @@
     )
 
 
-def source_number(blocks, blk, step):
+ORDERS = ((2, 0, 1, 3), (1, 3, 0, 2), (1, 3, 0, 2), (0, 2, 3, 1))
+
+
+def source_number(blocks, own, blk, term, step):
+    place = blk ^ step
+    if blocks == 4 and own == 1:
+        packed = sum(i << (8 * g + 2 * p) for g, order in enumerate(ORDERS) for i, p in enumerate(order))
+        if not isinstance(place, int):
+            packed = jnp.int32(packed - (packed >> 31 << 32))
+        return (packed >> (8 * term + 2 * place)) & 3
     half = blocks // 2
-    place = blk ^ step
     return (place % half) * 2 + place // half
 
 
@@ -28,7 +36,7 @@
         pairs = []
         for a in range(blocks):
             for group in range(terms):
-                i = source_number(blocks, a, k)
+                i = source_number(blocks, own, a, group, k)
                 source = (group * own + i // terms, i % terms)
                 if source != (a, group):
                     pairs.append((source, (a, group)))
@@ -62,14 +70,14 @@
         start[o] = jnp.where(mask, tiles[o], jnp.zeros((), tiles.dtype))
         keep[o] = jnp.where(mask, 1.0, 0.0)
     for k, right in enumerate(rights):
-        o = source_number(blocks, blk, k) // terms
+        o = source_number(blocks, own, blk, term, k) // terms
         products[k] = dot(start[o], right[0, 0]).astype(jnp.bfloat16)
 
 
 def finish(blocks, terms, own, tile, keep, mine, lefts, rights, early, products):
     blk, term = lax.axis_index("blk"), lax.axis_index("term")
     for k in range(blocks):
-        i = source_number(blocks, blk, k)
+        i = source_number(blocks, own, blk, term, k)
         if k < blocks - len(rights):
             products[i] = early[k]
         else:

time: 33.3 us -> 31.6 us (0.949)
  starting transfers between devices: 21.2 us -> 18.8 us
  waiting for transfers between devices: 5.48 us -> 6.28 us
    ppermute x11, starting transfers between devices: 21.2 us -> 18.8 us  [move(): lax.ppermute(value, AXES, [(a * terms + b, c * terms + d) for (a, b), (c,...]
    ppermute x11, waiting for transfers between devices: 5.48 us -> 6.28 us  [move(): lax.ppermute(value, AXES, [(a * terms + b, c * terms + d) for (a, b), (c,...]
  transfers between devices with their start and end apart: 11 -> 11, of which waited for: 5 -> 6; matrix products, arithmetic and copies ran while one was open for 0% -> 0% of each run, Pallas kernels for 7% -> 7%
where the time goes in v4:
time: 31.6 us; the launch traced here: 31.4 us
  starting transfers between devices  18.8 us (59%)
  waiting for transfers between devices  6.28 us (20%)
  Pallas kernels  3.83 us (12%)
  between operations  1.43 us (5%)
  local copies, waits for them, and re-layouts  1.12 us (4%)
    ppermute x11, starting transfers between devices, move(): lax.ppermute(value, AXES, [(a * terms + b, c * terms + d) for (a, b), (c,...  18.8 us
    ppermute x11, waiting for transfers between devices, move(): lax.ppermute(value, AXES, [(a * terms + b, c * terms + d) for (a, b), (c,...  6.28 us
    pallas_call x1, Pallas kernels, local(): pl.pallas_call(functools.partial(second_kernel, blocks, terms, own), out_...  1.26 us
    unnamed x10, local copies, waits for them, and re-layouts  1.12 us
    pallas_call x1, Pallas kernels, local(): pl.pallas_call(functools.partial(early_kernel, blocks, terms, own), out_s...  1.03 us
    pallas_call x1, Pallas kernels, local(): pl.pallas_call(functools.partial(scale_kernel, float(blocks * n_cols * wi...  0.83 us
    pallas_call x1, Pallas kernels, local(): pl.pallas_call(functools.partial(first_kernel, blocks, terms, own), out_s...  0.71 us
  transfers between devices with their start and end apart: 11, of which 6 were waited for; matrix products, arithmetic and copies ran while one was open for 0% of the time, Pallas kernels for 7%

profile of v4, /device:TPU:0, one launch (start us, length us, event | category | flops | bytes accessed | tf_op | source)
XLA Modules:
  0.0 31.4 jit_solution(100407423194624168)
XLA Ops:
  0.6 0.0 copy-start.4
  0.6 0.0 copy-start.3
  0.7 2.4 %collective-permute-start.3 = (bf16[1,1,256,256]{3,2,1,0:T(8,128)(2,1)}, bf16[1,1,256,256]{3,2,1,0:T(8,128)(2,1)S(1)}, u32[]{:S(2)}, u32[]{:S(2)}) collective-permute-start(bf16[1,1,256,256]{3,2,1,0:T(8,128)(2,1)} %refs_0_.3), channel_id=1, source_target_pairs={{0,3},{1,2},{2,1},{3,0},{4,7},{5,6},{6,5},{7,4},{8,11},{9,10},{10,... | collective-permute-start | bytes 393224 | tf_op jit(solution)/shard_map/ppermute | solution.py:14
  3.1 3.6 %collective-permute-start.1 = (bf16[1,1,256,256]{3,2,1,0:T(8,128)(2,1)}, bf16[1,1,256,256]{3,2,1,0:T(8,128)(2,1)S(1)}, u32[]{:S(2)}, u32[]{:S(2)}) collective-permute-start(bf16[1,1,256,256]{3,2,1,0:T(8,128)(2,1)} %mine.3), channel_id=1, source_target_pairs={{2,0},{4,1},{8,2},{15,3},{1,4},{6,5},{10,6},{12,7},{3,8},{5,9},{9,... | collective-permute-start | bytes 393224 | tf_op jit(solution)/shard_map/ppermute | solution.py:14
  6.7 0.0 collective-permute-start
  6.7 0.5 %collective-permute-start.2 = (bf16[1,1,256,256]{3,2,1,0:T(8,128)(2,1)}, bf16[1,1,256,256]{3,2,1,0:T(8,128)(2,1)S(1)}, u32[]{:S(2)}, u32[]{:S(2)}) collective-permute-start(bf16[1,1,256,256]{3,2,1,0:T(8,128)(2,1)} %refs_0_.3), channel_id=1, source_target_pairs={{0,1},{1,0},{2,3},{3,2},{4,5},{5,4},{6,7},{7,6},{8,9},{9,8},{10,11... | collective-permute-start | bytes 393224 | tf_op jit(solution)/shard_map/ppermute | solution.py:14
  7.2 0.7 %collective-permute-start.6 = (bf16[1,1,256,256]{3,2,1,0:T(8,128)(2,1)}, bf16[1,1,256,256]{3,2,1,0:T(8,128)(2,1)S(1)}, u32[]{:S(2)}, u32[]{:S(2)}) collective-permute-start(bf16[1,1,256,256]{3,2,1,0:T(8,128)(2,1)} %mine.3), channel_id=1, source_target_pairs={{3,0},{5,1},{9,2},{14,3},{0,4},{7,5},{11,6},{13,7},{2,8},{4,9},{8,... | collective-permute-start | bytes 393224 | tf_op jit(solution)/shard_map/ppermute | solution.py:14
  7.9 0.7 %collective-permute-done.3.refs_3_ = bf16[1,1,256,256]{3,2,1,0:T(8,128)(2,1)S(1)} collective-permute-done((bf16[1,1,256,256]{3,2,1,0:T(8,128)(2,1)}, bf16[1,1,256,256]{3,2,1,0:T(8,128)(2,1)S(1)}, u32[]{:S(2)}, u32[]{:S(2)}) %collective-permute-start.3) | collective-permute-done | bytes 131104 | tf_op jit(solution)/shard_map/ppermute | solution.py:14
  8.6 0.7 %collective-permute-start.5 = (bf16[1,1,256,256]{3,2,1,0:T(8,128)(2,1)}, bf16[1,1,256,256]{3,2,1,0:T(8,128)(2,1)S(1)}, u32[]{:S(2)}, u32[]{:S(2)}) collective-permute-start(bf16[1,1,256,256]{3,2,1,0:T(8,128)(2,1)} %mine.3), channel_id=1, source_target_pairs={{7,1},{11,2},{13,3},{3,4},{9,6},{14,7},{1,8},{6,9},{12,11},{2,12},... | collective-permute-start | bytes 393224 | tf_op jit(solution)/shard_map/ppermute | solution.py:14
  9.2 0.4 %collective-permute-done.1.refs_1_.refs_5_ = bf16[1,1,256,256]{3,2,1,0:T(8,128)(2,1)S(1)} collective-permute-done((bf16[1,1,256,256]{3,2,1,0:T(8,128)(2,1)}, bf16[1,1,256,256]{3,2,1,0:T(8,128)(2,1)S(1)}, u32[]{:S(2)}, u32[]{:S(2)}) %collective-permute-start.1) | collective-permute-done | bytes 131104 | tf_op jit(solution)/shard_map/ppermute | solution.py:14
  9.6 3.2 %collective-permute-start.4 = (bf16[1,1,256,256]{3,2,1,0:T(8,128)(2,1)S(1)}, bf16[1,1,256,256]{3,2,1,0:T(8,128)(2,1)S(1)}, u32[]{:S(2)}, u32[]{:S(2)}) collective-permute-start(bf16[1,1,256,256]{3,2,1,0:T(8,128)(2,1)S(1)} %collective-permute-done.3.refs_3_), channel_id=1, source_target_pairs={{0,1},{1,0},{2,3},{3,2},{4,5},{5,4},{6,7},{7,6},{8,9},{9,8},{10,11... | collective-permute-start | bytes 393224 | tf_op jit(solution)/shard_map/ppermute | solution.py:14
  13.5 0.0 copy-start
  13.5 0.0 copy-start.1
  13.5 0.0 collective-permute-done.refs_0_.refs_4_
  13.5 0.0 copy-done.4
  13.5 1.1 %copy-done.2 = bf16[1,4,256,256]{3,2,1,0:T(8,128)(2,1)S(1)} copy-done((bf16[1,4,256,256]{3,2,1,0:T(8,128)(2,1)S(1)}, bf16[1,4,256,256]{3,2,1,0:T(8,128)(2,1)}, u32[]{:S(2)}) %copy-start.2) | copy-done | bytes 524312
  14.6 1.0 %shard_map.77 = (bf16[1,256,256]{2,1,0:T(8,128)(2,1)S(1)}, f32[1,256,256]{2,1,0:T(8,128)S(1)}, bf16[2,256,256]{2,1,0:T(8,128)(2,1)S(1)}) custom-call(bf16[1,4,256,256]{3,2,1,0:T(8,128)(2,1)S(1)} %copy-done.2, s32[1]{0:T(128)S(6)} %copy.8.rows, s32[4]{0:T(128)S(1)} %copy-done.3, s32[1,4]{1,0:T(1,128)S(1)} %copy-done.4, ...), custom_call_target="tpu_custom_call" | custom-call | flops 67108864 | bytes 524288 | tf_op jit(solution)/shard_map/pallas_call | solution.py:143
  15.7 0.0 collective-permute-done.2.refs_1_
  15.7 0.0 collective-permute-done.6.refs_5_.refs_7_
  15.7 0.0 collective-permute-done.5.refs_4_.refs_6_
  15.7 0.0 collective-permute-done.4.refs_2_
  15.7 0.7 %shard_map.78 = (bf16[1,256,256]{2,1,0:T(8,128)(2,1)S(1)}, f32[8,128]{1,0:T(8,128)S(1)}) custom-call(bf16[1,256,256]{2,1,0:T(8,128)(2,1)S(1)} %get-tuple-element.9.start, f32[1,256,256]{2,1,0:T(8,128)S(1)} %get-tuple-element.10.keep, bf16[2,256,256]{2,1,0:T(8,128)(2,1)S(1)} %get-tuple-element.11.early, bf16[1,1,256,256]{3,2,1,0:T(8,128)(2,1)S(1)} %copy-done, ...), custom_call_target="tpu_custom_call" | custom-call | flops 201326592 | bytes 524288 | tf_op jit(solution)/shard_map/pallas_call | solution.py:164
  16.4 2.4 %collective-permute-start.7 = (f32[8,128]{1,0:T(8,128)S(1)}, f32[8,128]{1,0:T(8,128)S(1)}, u32[]{:S(2)}, u32[]{:S(2)}) collective-permute-start(f32[8,128]{1,0:T(8,128)S(1)} %get-tuple-element.15), channel_id=1, source_target_pairs={{0,1},{1,0},{2,3},{3,2},{4,5},{5,4},{6,7},{7,6},{8,9},{9,8},{10,11... | collective-permute-start | bytes 12296 | tf_op jit(solution)/shard_map/ppermute | solution.py:14
  18.9 0.8 %collective-permute-done.7 = f32[8,128]{1,0:T(8,128)S(1)} collective-permute-done((f32[8,128]{1,0:T(8,128)S(1)}, f32[8,128]{1,0:T(8,128)S(1)}, u32[]{:S(2)}, u32[]{:S(2)}) %collective-permute-start.7) | collective-permute-done | bytes 4128 | tf_op jit(solution)/shard_map/ppermute | solution.py:14
  19.7 2.6 %collective-permute-start.8 = (f32[8,128]{1,0:T(8,128)S(1)}, f32[8,128]{1,0:T(8,128)S(1)}, u32[]{:S(2)}, u32[]{:S(2)}) collective-permute-start(f32[8,128]{1,0:T(8,128)S(1)} %add.9), channel_id=1, source_target_pairs={{0,3},{1,2},{2,1},{3,0},{4,7},{5,6},{6,5},{7,4},{8,11},{9,10},{10,... | collective-permute-start | bytes 12296 | tf_op jit(solution)/shard_map/ppermute | solution.py:14
  22.3 1.3 %collective-permute-done.8 = f32[8,128]{1,0:T(8,128)S(1)} collective-permute-done((f32[8,128]{1,0:T(8,128)S(1)}, f32[8,128]{1,0:T(8,128)S(1)}, u32[]{:S(2)}, u32[]{:S(2)}) %collective-permute-start.8) | collective-permute-done | bytes 4128 | tf_op jit(solution)/shard_map/ppermute | solution.py:14
  23.6 0.0 collective-permute-start.9
  23.6 3.0 %collective-permute-done.9 = f32[8,128]{1,0:T(8,128)S(1)} collective-permute-done((f32[8,128]{1,0:T(8,128)S(1)}, f32[8,128]{1,0:T(8,128)S(1)}, u32[]{:S(2)}, u32[]{:S(2)}) %collective-permute-start.9) | collective-permute-done | bytes 4128 | tf_op jit(solution)/shard_map/ppermute | solution.py:14
  26.7 2.6 %collective-permute-start.10 = (f32[8,128]{1,0:T(8,128)S(1)}, f32[8,128]{1,0:T(8,128)S(1)}, u32[]{:S(2)}, u32[]{:S(2)}) collective-permute-start(f32[8,128]{1,0:T(8,128)S(1)} %add.11.norm), channel_id=1, source_target_pairs={{0,9},{1,8},{2,11},{3,10},{4,13},{5,12},{6,15},{7,14},{8,1},{9,0},... | collective-permute-start | bytes 12296 | tf_op jit(solution)/shard_map/ppermute | solution.py:14
  29.3 1.3 %shard_map.79 = (bf16[1,1,256,256]{3,2,1,0:T(8,128)(2,1)}, f32[1,1,256,256]{3,2,1,0:T(8,128)S(1)}) custom-call(bf16[1,256,256]{2,1,0:T(8,128)(2,1)S(1)} %get-tuple-element.12.image, f32[1,256,256]{2,1,0:T(8,128)S(1)} %get-tuple-element.10.keep, bf16[1,1,256,256]{3,2,1,0:T(8,128)(2,1)S(1)} %copy-done, bf16[1,1,256,256]{3,2,1,0:T(8,128)(2,1)S(1)} %copy-done.1, ...), custom_call_target="tpu_custom_call" | custom-call | flops 268435456 | bytes 524288 | tf_op jit(solution)/shard_map/pallas_call | solution.py:177
  30.5 0.1 collective-permute-done.10.other
  30.6 0.8 %shard_map.80 = bf16[1,1,256,256]{3,2,1,0:T(8,128)(2,1)} custom-call(f32[1,1,256,256]{3,2,1,0:T(8,128)S(1)} %get-tuple-element.14.raw, f32[8,128]{1,0:T(8,128)S(1)} %add.11.norm, f32[8,128]{1,0:T(8,128)S(1)} %collective-permute-done.10.other), custom_call_target="tpu_custom_call" | custom-call | tf_op jit(solution)/shard_map/pallas_call | solution.py:197
  (7 shorter events, 0.0 us)
Async XLA Ops:
  0.6 12.9 %copy-start.4 = (s32[1,4]{1,0:T(1,128)S(1)}, s32[1,4]{1,0:T(1,128)}, u32[]{:S(2)}) copy-start(s32[1,4]{1,0:T(1,128)} %live.1) | copy-start | bytes 52
  0.6 12.9 %copy-start.3 = (s32[4]{0:T(128)S(1)}, s32[4]{0:T(128)}, u32[]{:S(2)}) copy-start(s32[4]{0:T(128)} %cols.1) | copy-start | bytes 52
  0.7 7.9 %collective-permute-start.3 = (bf16[1,1,256,256]{3,2,1,0:T(8,128)(2,1)}, bf16[1,1,256,256]{3,2,1,0:T(8,128)(2,1)S(1)}, u32[]{:S(2)}, u32[]{:S(2)}) collective-permute-start(bf16[1,1,256,256]{3,2,1,0:T(8,128)(2,1)} %refs_0_.3), channel_id=1, source_target_pairs={{0,3},{1,2},{2,1},{3,0},{4,7},{5,6},{6,5},{7,4},{8,11},{9,10},{10,... | collective-permute-start | bytes 393224 | tf_op jit(solution)/shard_map/ppermute | solution.py:14
  3.1 6.5 %collective-permute-start.1 = (bf16[1,1,256,256]{3,2,1,0:T(8,128)(2,1)}, bf16[1,1,256,256]{3,2,1,0:T(8,128)(2,1)S(1)}, u32[]{:S(2)}, u32[]{:S(2)}) collective-permute-start(bf16[1,1,256,256]{3,2,1,0:T(8,128)(2,1)} %mine.3), channel_id=1, source_target_pairs={{2,0},{4,1},{8,2},{15,3},{1,4},{6,5},{10,6},{12,7},{3,8},{5,9},{9,... | collective-permute-start | bytes 393224 | tf_op jit(solution)/shard_map/ppermute | solution.py:14
  6.7 6.8 %collective-permute-start = (bf16[1,1,256,256]{3,2,1,0:T(8,128)(2,1)}, bf16[1,1,256,256]{3,2,1,0:T(8,128)(2,1)S(1)}, u32[]{:S(2)}, u32[]{:S(2)}) collective-permute-start(bf16[1,1,256,256]{3,2,1,0:T(8,128)(2,1)} %mine.3), channel_id=1, source_target_pairs={{1,0},{6,1},{10,2},{12,3},{2,4},{4,5},{8,6},{15,7},{0,8},{7,9},{11... | collective-permute-start | bytes 393224 | tf_op jit(solution)/shard_map/ppermute | solution.py:14
  6.7 9.0 %collective-permute-start.2 = (bf16[1,1,256,256]{3,2,1,0:T(8,128)(2,1)}, bf16[1,1,256,256]{3,2,1,0:T(8,128)(2,1)S(1)}, u32[]{:S(2)}, u32[]{:S(2)}) collective-permute-start(bf16[1,1,256,256]{3,2,1,0:T(8,128)(2,1)} %refs_0_.3), channel_id=1, source_target_pairs={{0,1},{1,0},{2,3},{3,2},{4,5},{5,4},{6,7},{7,6},{8,9},{9,8},{10,11... | collective-permute-start | bytes 393224 | tf_op jit(solution)/shard_map/ppermute | solution.py:14
  7.2 8.5 %collective-permute-start.6 = (bf16[1,1,256,256]{3,2,1,0:T(8,128)(2,1)}, bf16[1,1,256,256]{3,2,1,0:T(8,128)(2,1)S(1)}, u32[]{:S(2)}, u32[]{:S(2)}) collective-permute-start(bf16[1,1,256,256]{3,2,1,0:T(8,128)(2,1)} %mine.3), channel_id=1, source_target_pairs={{3,0},{5,1},{9,2},{14,3},{0,4},{7,5},{11,6},{13,7},{2,8},{4,9},{8,... | collective-permute-start | bytes 393224 | tf_op jit(solution)/shard_map/ppermute | solution.py:14
  8.6 7.1 %collective-permute-start.5 = (bf16[1,1,256,256]{3,2,1,0:T(8,128)(2,1)}, bf16[1,1,256,256]{3,2,1,0:T(8,128)(2,1)S(1)}, u32[]{:S(2)}, u32[]{:S(2)}) collective-permute-start(bf16[1,1,256,256]{3,2,1,0:T(8,128)(2,1)} %mine.3), channel_id=1, source_target_pairs={{7,1},{11,2},{13,3},{3,4},{9,6},{14,7},{1,8},{6,9},{12,11},{2,12},... | collective-permute-start | bytes 393224 | tf_op jit(solution)/shard_map/ppermute | solution.py:14
  9.6 6.1 %collective-permute-start.4 = (bf16[1,1,256,256]{3,2,1,0:T(8,128)(2,1)S(1)}, bf16[1,1,256,256]{3,2,1,0:T(8,128)(2,1)S(1)}, u32[]{:S(2)}, u32[]{:S(2)}) collective-permute-start(bf16[1,1,256,256]{3,2,1,0:T(8,128)(2,1)S(1)} %collective-permute-done.3.refs_3_), channel_id=1, source_target_pairs={{0,1},{1,0},{2,3},{3,2},{4,5},{5,4},{6,7},{7,6},{8,9},{9,8},{10,11... | collective-permute-start | bytes 393224 | tf_op jit(solution)/shard_map/ppermute | solution.py:14
  13.5 2.2 %copy-start = (bf16[1,1,256,256]{3,2,1,0:T(8,128)(2,1)S(1)}, bf16[1,1,256,256]{3,2,1,0:T(8,128)(2,1)}, u32[]{:S(2)}) copy-start(bf16[1,1,256,256]{3,2,1,0:T(8,128)(2,1)} %mine.3) | copy-start | bytes 393220
  13.5 2.2 %copy-start.1 = (bf16[1,1,256,256]{3,2,1,0:T(8,128)(2,1)S(1)}, bf16[1,1,256,256]{3,2,1,0:T(8,128)(2,1)}, u32[]{:S(2)}) copy-start(bf16[1,1,256,256]{3,2,1,0:T(8,128)(2,1)} %refs_0_.3) | copy-start | bytes 393220
  13.5 1.1 %copy-start.2 = (bf16[1,4,256,256]{3,2,1,0:T(8,128)(2,1)S(1)}, bf16[1,4,256,256]{3,2,1,0:T(8,128)(2,1)}, u32[]{:S(2)}) copy-start(bf16[1,4,256,256]{3,2,1,0:T(8,128)(2,1)} %two_site.1) | copy-start | bytes 1572868
  16.4 3.2 %collective-permute-start.7 = (f32[8,128]{1,0:T(8,128)S(1)}, f32[8,128]{1,0:T(8,128)S(1)}, u32[]{:S(2)}, u32[]{:S(2)}) collective-permute-start(f32[8,128]{1,0:T(8,128)S(1)} %get-tuple-element.15), channel_id=1, source_target_pairs={{0,1},{1,0},{2,3},{3,2},{4,5},{5,4},{6,7},{7,6},{8,9},{9,8},{10,11... | collective-permute-start | bytes 12296 | tf_op jit(solution)/shard_map/ppermute | solution.py:14
  19.7 3.9 %collective-permute-start.8 = (f32[8,128]{1,0:T(8,128)S(1)}, f32[8,128]{1,0:T(8,128)S(1)}, u32[]{:S(2)}, u32[]{:S(2)}) collective-permute-start(f32[8,128]{1,0:T(8,128)S(1)} %add.9), channel_id=1, source_target_pairs={{0,3},{1,2},{2,1},{3,0},{4,7},{5,6},{6,5},{7,4},{8,11},{9,10},{10,... | collective-permute-start | bytes 12296 | tf_op jit(solution)/shard_map/ppermute | solution.py:14
  23.6 3.0 %collective-permute-start.9 = (f32[8,128]{1,0:T(8,128)S(1)}, f32[8,128]{1,0:T(8,128)S(1)}, u32[]{:S(2)}, u32[]{:S(2)}) collective-permute-start(f32[8,128]{1,0:T(8,128)S(1)} %add.10), channel_id=1, source_target_pairs={{0,5},{1,4},{2,7},{3,6},{4,1},{5,0},{6,3},{7,2},{8,13},{9,12},{10,... | collective-permute-start | bytes 12296 | tf_op jit(solution)/shard_map/ppermute | solution.py:14
  26.7 3.9 %collective-permute-start.10 = (f32[8,128]{1,0:T(8,128)S(1)}, f32[8,128]{1,0:T(8,128)S(1)}, u32[]{:S(2)}, u32[]{:S(2)}) collective-permute-start(f32[8,128]{1,0:T(8,128)S(1)} %add.11.norm), channel_id=1, source_target_pairs={{0,9},{1,8},{2,11},{3,10},{4,13},{5,12},{6,15},{7,14},{8,1},{9,0},... | collective-permute-start | bytes 12296 | tf_op jit(solution)/shard_map/ppermute | solution.py:14

commit v5 on v4

--- a/solution.py
+++ b/solution.py
@@ -17,6 +17,11 @@
 
 
 ORDERS = ((2, 0, 1, 3), (1, 3, 0, 2), (1, 3, 0, 2), (0, 2, 3, 1))
+STEPS = (2, 3, 1, 0)
+
+
+def steps_of(blocks, own):
+    return STEPS if blocks == 4 and own == 1 else range(blocks)
 
 
 def source_number(blocks, own, blk, term, step):
@@ -31,26 +36,25 @@
 
 
 def right_routes(blocks, terms, own):
-    steps = []
-    for k in range(blocks):
+    routes = []
+    for step in steps_of(blocks, own):
         pairs = []
         for a in range(blocks):
             for group in range(terms):
-                i = source_number(blocks, own, a, group, k)
+                i = source_number(blocks, own, a, group, step)
                 source = (group * own + i // terms, i % terms)
                 if source != (a, group):
                     pairs.append((source, (a, group)))
-        steps.append(pairs)
-    return steps
+        routes.append(pairs)
+    return routes
 
 
 def dot(a, b):
     return jnp.dot(a, b, preferred_element_type=jnp.float32)
 
 
-def early_kernel(blocks, terms, own, two_site, rows, cols, live, *refs):
-    rights, (start, keep, products, tiles, rows_at, cols_at, live_at, sems) = refs[:-8], refs[-8:]
-    blk, term = lax.axis_index("blk"), lax.axis_index("term")
+def start_kernel(own, two_site, rows, cols, live, start, keep, tiles, rows_at, cols_at, live_at, sems):
+    term = lax.axis_index("term")
     width = tiles.shape[-1]
     copies = [
         pltpu.make_async_copy(two_site.at[0, pl.ds(term * own, own)], tiles, sems.at[0]),
@@ -69,20 +73,13 @@
         mask = (at_row < rows_at[0]) & (at_col < cols_at[col]) & (live_at[0, col] == 1)
         start[o] = jnp.where(mask, tiles[o], jnp.zeros((), tiles.dtype))
         keep[o] = jnp.where(mask, 1.0, 0.0)
-    for k, right in enumerate(rights):
-        o = source_number(blocks, own, blk, term, k) // terms
-        products[k] = dot(start[o], right[0, 0]).astype(jnp.bfloat16)
-
-
-def finish(blocks, terms, own, tile, keep, mine, lefts, rights, early, products):
+
+
+def apply_tiles(blocks, terms, own, tile, keep, mine, lefts, rights, products):
     blk, term = lax.axis_index("blk"), lax.axis_index("term")
-    for k in range(blocks):
-        i = source_number(blocks, own, blk, term, k)
-        if k < blocks - len(rights):
-            products[i] = early[k]
-        else:
-            right = rights[k - blocks + len(rights)]
-            products[i] = dot(tile[i // terms], right[0, 0]).astype(jnp.bfloat16)
+    for step, right in zip(steps_of(blocks, own), rights):
+        i = source_number(blocks, own, blk, term, step)
+        products[i] = dot(tile[i // terms], right[0, 0]).astype(jnp.bfloat16)
 
     @pl.when(blk // own == term)
     def _():
@@ -96,11 +93,11 @@
     return sums
 
 
-def first_kernel(blocks, terms, own, start, keep, early, mine, *refs):
+def first_kernel(blocks, terms, own, start, keep, mine, *refs):
     lefts, rights, (image, partial, products) = refs[:terms], refs[terms:-3], refs[-3:]
     width = start.shape[-1]
     squares = jnp.zeros((8, width), jnp.float32)
-    for o, total in enumerate(finish(blocks, terms, own, start, keep, mine, lefts, rights, early, products)):
+    for o, total in enumerate(apply_tiles(blocks, terms, own, start, keep, mine, lefts, rights, products)):
         out = total.astype(jnp.bfloat16)
         image[o] = out
         out = out.astype(jnp.float32)
@@ -111,7 +108,7 @@
 def second_kernel(blocks, terms, own, image, keep, mine, *refs):
     lefts, rights, (final, raw, products) = refs[:terms], refs[terms:-3], refs[-3:]
     final[0] = image[...]
-    for o, total in enumerate(finish(blocks, terms, own, image, keep, mine, lefts, rights, None, products)):
+    for o, total in enumerate(apply_tiles(blocks, terms, own, image, keep, mine, lefts, rights, products)):
         raw[0, o] = total
 
 
@@ -139,16 +136,14 @@
         lefts[m] = move(source, [((a, t), (a, t ^ hop)) for a, t in everyone], terms)
 
     tile = (own, width, width)
-    early = blocks // 2
-    start, keep, products = pl.pallas_call(
-        functools.partial(early_kernel, blocks, terms, own),
+    start, keep = pl.pallas_call(
+        functools.partial(start_kernel, own),
         out_shape=(
             jax.ShapeDtypeStruct(tile, jnp.bfloat16),
             jax.ShapeDtypeStruct(tile, jnp.float32),
-            jax.ShapeDtypeStruct((early, width, width), jnp.bfloat16),
         ),
-        in_specs=[hbm] * 4 + [vmem] * early,
-        out_specs=(vmem,) * 3,
+        in_specs=[hbm] * 4,
+        out_specs=(vmem,) * 2,
         scratch_shapes=[
             pltpu.VMEM(tile, jnp.bfloat16),
             pltpu.SMEM(row_size.shape, jnp.int32),
@@ -157,35 +152,30 @@
             pltpu.SemaphoreType.DMA((4,)),
         ],
         compiler_params=params,
-        cost_estimate=cost(early, width),
-    )(two_site, row_size, col_size, block_live, *rights[:early])
-
-    work = [pltpu.VMEM((blocks, width, width), jnp.bfloat16)]
-    first, partial = pl.pallas_call(
-        functools.partial(first_kernel, blocks, terms, own),
-        out_shape=(
-            jax.ShapeDtypeStruct(tile, jnp.bfloat16),
-            jax.ShapeDtypeStruct((8, 128), jnp.float32),
-        ),
-        in_specs=[vmem] * (4 + terms + blocks - early),
-        out_specs=(vmem,) * 2,
-        scratch_shapes=work,
-        compiler_params=params,
-        cost_estimate=cost(2 * blocks - early, width),
-    )(start, keep, products, right_env, *lefts, *rights[early:])
-
-    first_image, raw = pl.pallas_call(
-        functools.partial(second_kernel, blocks, terms, own),
-        out_shape=(
-            jax.ShapeDtypeStruct((1,) + tile, jnp.bfloat16),
-            jax.ShapeDtypeStruct((1,) + tile, jnp.float32),
-        ),
-        in_specs=[vmem] * (3 + terms + blocks),
-        out_specs=(vmem,) * 2,
-        scratch_shapes=work,
-        compiler_params=params,
-        cost_estimate=cost(2 * blocks, width),
-    )(first, keep, right_env, *lefts, *rights)
+        cost_estimate=cost(0, width),
+    )(two_site, row_size, col_size, block_live)
+
+    def apply_call(kernel, operand, outs):
+        return pl.pallas_call(
+            functools.partial(kernel, blocks, terms, own),
+            out_shape=outs,
+            in_specs=[vmem] * (3 + terms + blocks),
+            out_specs=(vmem,) * 2,
+            scratch_shapes=[pltpu.VMEM((blocks, width, width), jnp.bfloat16)],
+            compiler_params=params,
+            cost_estimate=cost(2 * blocks, width),
+        )(operand, keep, right_env, *lefts, *rights)
+
+    first, partial = apply_call(
+        first_kernel,
+        start,
+        (jax.ShapeDtypeStruct(tile, jnp.bfloat16), jax.ShapeDtypeStruct((8, 128), jnp.float32)),
+    )
+    first_image, raw = apply_call(
+        second_kernel,
+        first,
+        (jax.ShapeDtypeStruct((1,) + tile, jnp.bfloat16), jax.ShapeDtypeStruct((1,) + tile, jnp.float32)),
+    )
 
     flips = [(0, 1)] + [(0, 1 | 1 << s) for s in range(1, (terms - 1).bit_length())]
     flips += [(1 << s, 1) for s in range((blocks - 1).bit_length())]

time: 31.6 us -> 31.1 us (0.984)
  waiting for transfers between devices: 6.28 us -> 3.73 us
  starting transfers between devices: 18.8 us -> 21 us
    ppermute x11, waiting for transfers between devices: 6.28 us -> 3.73 us  [move(): lax.ppermute(value, AXES, [(a * terms + b, c * terms + d) for (a, b), (c,...]
    ppermute x11, starting transfers between devices: 18.8 us -> 21 us  [move(): lax.ppermute(value, AXES, [(a * terms + b, c * terms + d) for (a, b), (c,...]
  transfers between devices with their start and end apart: 11 -> 11, of which waited for: 6 -> 4; matrix products, arithmetic and copies ran while one was open for 0% -> 0% of each run, Pallas kernels for 7% -> 7%
where the time goes in v5:
time: 31.1 us; the launch traced here: 30.9 us
  starting transfers between devices  21 us (68%)
  waiting for transfers between devices  3.73 us (12%)
  Pallas kernels  3.73 us (12%)
  between operations  1.41 us (5%)
  local copies, waits for them, and re-layouts  1.08 us (3%)
    ppermute x11, starting transfers between devices, move(): lax.ppermute(value, AXES, [(a * terms + b, c * terms + d) for (a, b), (c,...  21 us
    ppermute x11, waiting for transfers between devices, move(): lax.ppermute(value, AXES, [(a * terms + b, c * terms + d) for (a, b), (c,...  3.73 us
    pallas_call x2, Pallas kernels, apply_call(): pl.pallas_call(functools.partial(kernel, blocks, terms, own), out_shape=o...  2.03 us
    unnamed x10, local copies, waits for them, and re-layouts  1.08 us
    pallas_call x1, Pallas kernels, local(): pl.pallas_call(functools.partial(start_kernel, own), out_shape=(jax.Shape...  0.86 us
    pallas_call x1, Pallas kernels, local(): pl.pallas_call(functools.partial(scale_kernel, float(blocks * n_cols * wi...  0.83 us
  transfers between devices with their start and end apart: 11, of which 4 were waited for; matrix products, arithmetic and copies ran while one was open for 0% of the time, Pallas kernels for 7%

profile of v5, /device:TPU:0, one launch (start us, length us, event | category | flops | bytes accessed | tf_op | source)
XLA Modules:
  0.0 30.9 jit_solution(5004514646139834252)
XLA Ops:
  0.6 0.0 copy-start.4
  0.6 0.0 copy-start.3
  0.7 2.4 %collective-permute-start.1 = (bf16[1,1,256,256]{3,2,1,0:T(8,128)(2,1)}, bf16[1,1,256,256]{3,2,1,0:T(8,128)(2,1)S(1)}, u32[]{:S(2)}, u32[]{:S(2)}) collective-permute-start(bf16[1,1,256,256]{3,2,1,0:T(8,128)(2,1)} %refs_0_.3), channel_id=1, source_target_pairs={{0,3},{1,2},{2,1},{3,0},{4,7},{5,6},{6,5},{7,4},{8,11},{9,10},{10,... | collective-permute-start | bytes 393224 | tf_op jit(solution)/shard_map/ppermute | solution.py:14
  3.1 0.7 %collective-permute-start = (bf16[1,1,256,256]{3,2,1,0:T(8,128)(2,1)}, bf16[1,1,256,256]{3,2,1,0:T(8,128)(2,1)S(1)}, u32[]{:S(2)}, u32[]{:S(2)}) collective-permute-start(bf16[1,1,256,256]{3,2,1,0:T(8,128)(2,1)} %refs_0_.3), channel_id=1, source_target_pairs={{0,1},{1,0},{2,3},{3,2},{4,5},{5,4},{6,7},{7,6},{8,9},{9,8},{10,11... | collective-permute-start | bytes 393224 | tf_op jit(solution)/shard_map/ppermute | solution.py:14
  3.8 2.6 %collective-permute-start.6 = (bf16[1,1,256,256]{3,2,1,0:T(8,128)(2,1)}, bf16[1,1,256,256]{3,2,1,0:T(8,128)(2,1)S(1)}, u32[]{:S(2)}, u32[]{:S(2)}) collective-permute-start(bf16[1,1,256,256]{3,2,1,0:T(8,128)(2,1)} %mine.3), channel_id=1, source_target_pairs={{1,0},{6,1},{10,2},{12,3},{2,4},{4,5},{8,6},{15,7},{0,8},{7,9},{11... | collective-permute-start | bytes 393224 | tf_op jit(solution)/shard_map/ppermute | solution.py:14
  6.4 1.0 %collective-permute-start.5 = (bf16[1,1,256,256]{3,2,1,0:T(8,128)(2,1)}, bf16[1,1,256,256]{3,2,1,0:T(8,128)(2,1)S(1)}, u32[]{:S(2)}, u32[]{:S(2)}) collective-permute-start(bf16[1,1,256,256]{3,2,1,0:T(8,128)(2,1)} %mine.3), channel_id=1, source_target_pairs={{2,0},{4,1},{8,2},{15,3},{1,4},{6,5},{10,6},{12,7},{3,8},{5,9},{9,... | collective-permute-start | bytes 393224 | tf_op jit(solution)/shard_map/ppermute | solution.py:14
  7.4 0.0 collective-permute-start.4
  7.4 0.0 collective-permute-done.1.refs_3_
  7.4 0.7 %collective-permute-start.3 = (bf16[1,1,256,256]{3,2,1,0:T(8,128)(2,1)}, bf16[1,1,256,256]{3,2,1,0:T(8,128)(2,1)S(1)}, u32[]{:S(2)}, u32[]{:S(2)}) collective-permute-start(bf16[1,1,256,256]{3,2,1,0:T(8,128)(2,1)} %mine.3), channel_id=1, source_target_pairs={{7,1},{11,2},{13,3},{3,4},{9,6},{14,7},{1,8},{6,9},{12,11},{2,12},... | collective-permute-start | bytes 393224 | tf_op jit(solution)/shard_map/ppermute | solution.py:14
  8.0 0.0 collective-permute-done.refs_1_
  8.1 6.2 %collective-permute-start.2 = (bf16[1,1,256,256]{3,2,1,0:T(8,128)(2,1)S(1)}, bf16[1,1,256,256]{3,2,1,0:T(8,128)(2,1)S(1)}, u32[]{:S(2)}, u32[]{:S(2)}) collective-permute-start(bf16[1,1,256,256]{3,2,1,0:T(8,128)(2,1)S(1)} %collective-permute-done.1.refs_3_), channel_id=1, source_target_pairs={{0,1},{1,0},{2,3},{3,2},{4,5},{5,4},{6,7},{7,6},{8,9},{9,8},{10,11... | collective-permute-start | bytes 393224 | tf_op jit(solution)/shard_map/ppermute | solution.py:14
  14.9 0.0 copy-done.4
  14.9 0.0 copy-done.3
  14.9 1.0 %copy-done.2 = bf16[1,4,256,256]{3,2,1,0:T(8,128)(2,1)S(1)} copy-done((bf16[1,4,256,256]{3,2,1,0:T(8,128)(2,1)S(1)}, bf16[1,4,256,256]{3,2,1,0:T(8,128)(2,1)}, u32[]{:S(2)}) %copy-start.2) | copy-done | bytes 524312
  15.9 0.9 %shard_map.77 = (bf16[1,256,256]{2,1,0:T(8,128)(2,1)S(1)}, f32[1,256,256]{2,1,0:T(8,128)S(1)}) custom-call(bf16[1,4,256,256]{3,2,1,0:T(8,128)(2,1)S(1)} %copy-done.2, s32[1]{0:T(128)S(6)} %copy.8.rows, s32[4]{0:T(128)S(1)} %copy-done.3, s32[1,4]{1,0:T(1,128)S(1)} %copy-done.4), custom_call_target="tpu_custom_call" | custom-call | bytes 524288 | tf_op jit(solution)/shard_map/pallas_call | solution.py:139
  16.8 0.0 collective-permute-done.6.refs_7_
  16.8 0.0 collective-permute-done.5.refs_6_
  16.8 0.0 collective-permute-done.4.refs_5_
  16.8 0.0 collective-permute-done.3.refs_4_
  16.8 0.0 collective-permute-done.2.refs_2_
  16.9 0.0 copy-done.1
  16.9 0.8 %shard_map.78 = (bf16[1,256,256]{2,1,0:T(8,128)(2,1)S(1)}, f32[8,128]{1,0:T(8,128)S(1)}) custom-call(bf16[1,256,256]{2,1,0:T(8,128)(2,1)S(1)} %get-tuple-element.8.start, f32[1,256,256]{2,1,0:T(8,128)S(1)} %get-tuple-element.9.keep, bf16[1,1,256,256]{3,2,1,0:T(8,128)(2,1)S(1)} %copy-done, bf16[1,1,256,256]{3,2,1,0:T(8,128)(2,1)S(1)} %copy-done.1, ...), custom_call_target="tpu_custom_call" | custom-call | flops 268435456 | bytes 524288 | tf_op jit(solution)/shard_map/pallas_call | solution.py:159
  17.7 1.5 %collective-permute-start.7 = (f32[8,128]{1,0:T(8,128)S(1)}, f32[8,128]{1,0:T(8,128)S(1)}, u32[]{:S(2)}, u32[]{:S(2)}) collective-permute-start(f32[8,128]{1,0:T(8,128)S(1)} %get-tuple-element.13), channel_id=1, source_target_pairs={{0,1},{1,0},{2,3},{3,2},{4,5},{5,4},{6,7},{7,6},{8,9},{9,8},{10,11... | collective-permute-start | bytes 12296 | tf_op jit(solution)/shard_map/ppermute | solution.py:14
  19.1 0.8 %collective-permute-done.7 = f32[8,128]{1,0:T(8,128)S(1)} collective-permute-done((f32[8,128]{1,0:T(8,128)S(1)}, f32[8,128]{1,0:T(8,128)S(1)}, u32[]{:S(2)}, u32[]{:S(2)}) %collective-permute-start.7) | collective-permute-done | bytes 4128 | tf_op jit(solution)/shard_map/ppermute | solution.py:14
  20.0 1.6 %collective-permute-start.8 = (f32[8,128]{1,0:T(8,128)S(1)}, f32[8,128]{1,0:T(8,128)S(1)}, u32[]{:S(2)}, u32[]{:S(2)}) collective-permute-start(f32[8,128]{1,0:T(8,128)S(1)} %add.9), channel_id=1, source_target_pairs={{0,3},{1,2},{2,1},{3,0},{4,7},{5,6},{6,5},{7,4},{8,11},{9,10},{10,... | collective-permute-start | bytes 12296 | tf_op jit(solution)/shard_map/ppermute | solution.py:14
  21.5 1.5 %collective-permute-done.8 = f32[8,128]{1,0:T(8,128)S(1)} collective-permute-done((f32[8,128]{1,0:T(8,128)S(1)}, f32[8,128]{1,0:T(8,128)S(1)}, u32[]{:S(2)}, u32[]{:S(2)}) %collective-permute-start.8) | collective-permute-done | bytes 4128 | tf_op jit(solution)/shard_map/ppermute | solution.py:14
  23.0 1.7 %collective-permute-start.9 = (f32[8,128]{1,0:T(8,128)S(1)}, f32[8,128]{1,0:T(8,128)S(1)}, u32[]{:S(2)}, u32[]{:S(2)}) collective-permute-start(f32[8,128]{1,0:T(8,128)S(1)} %add.10), channel_id=1, source_target_pairs={{0,5},{1,4},{2,7},{3,6},{4,1},{5,0},{6,3},{7,2},{8,13},{9,12},{10,... | collective-permute-start | bytes 12296 | tf_op jit(solution)/shard_map/ppermute | solution.py:14
  24.7 1.3 %collective-permute-done.9 = f32[8,128]{1,0:T(8,128)S(1)} collective-permute-done((f32[8,128]{1,0:T(8,128)S(1)}, f32[8,128]{1,0:T(8,128)S(1)}, u32[]{:S(2)}, u32[]{:S(2)}) %collective-permute-start.9) | collective-permute-done | bytes 4128 | tf_op jit(solution)/shard_map/ppermute | solution.py:14
  26.1 2.7 %collective-permute-start.10 = (f32[8,128]{1,0:T(8,128)S(1)}, f32[8,128]{1,0:T(8,128)S(1)}, u32[]{:S(2)}, u32[]{:S(2)}) collective-permute-start(f32[8,128]{1,0:T(8,128)S(1)} %add.11.norm), channel_id=1, source_target_pairs={{0,9},{1,8},{2,11},{3,10},{4,13},{5,12},{6,15},{7,14},{8,1},{9,0},... | collective-permute-start | bytes 12296 | tf_op jit(solution)/shard_map/ppermute | solution.py:14
  28.8 1.3 %shard_map.79 = (bf16[1,1,256,256]{3,2,1,0:T(8,128)(2,1)}, f32[1,1,256,256]{3,2,1,0:T(8,128)S(1)}) custom-call(bf16[1,256,256]{2,1,0:T(8,128)(2,1)S(1)} %get-tuple-element.10.image, f32[1,256,256]{2,1,0:T(8,128)S(1)} %get-tuple-element.9.keep, bf16[1,1,256,256]{3,2,1,0:T(8,128)(2,1)S(1)} %copy-done, bf16[1,1,256,256]{3,2,1,0:T(8,128)(2,1)S(1)} %copy-done.1, ...), custom_call_target="tpu_custom_call" | custom-call | flops 268435456 | bytes 524288 | tf_op jit(solution)/shard_map/pallas_call | solution.py:159
  30.0 0.1 collective-permute-done.10.other
  30.1 0.8 %shard_map.80 = bf16[1,1,256,256]{3,2,1,0:T(8,128)(2,1)} custom-call(f32[1,1,256,256]{3,2,1,0:T(8,128)S(1)} %get-tuple-element.12.raw, f32[8,128]{1,0:T(8,128)S(1)} %add.11.norm, f32[8,128]{1,0:T(8,128)S(1)} %collective-permute-done.10.other), custom_call_target="tpu_custom_call" | custom-call | tf_op jit(solution)/shard_map/pallas_call | solution.py:187
  (7 shorter events, 0.0 us)
Async XLA Ops:
  0.6 14.2 %copy-start.4 = (s32[1,4]{1,0:T(1,128)S(1)}, s32[1,4]{1,0:T(1,128)}, u32[]{:S(2)}) copy-start(s32[1,4]{1,0:T(1,128)} %live.1) | copy-start | bytes 52
  0.6 14.2 %copy-start.3 = (s32[4]{0:T(128)S(1)}, s32[4]{0:T(128)}, u32[]{:S(2)}) copy-start(s32[4]{0:T(128)} %cols.1) | copy-start | bytes 52
  0.7 6.7 %collective-permute-start.1 = (bf16[1,1,256,256]{3,2,1,0:T(8,128)(2,1)}, bf16[1,1,256,256]{3,2,1,0:T(8,128)(2,1)S(1)}, u32[]{:S(2)}, u32[]{:S(2)}) collective-permute-start(bf16[1,1,256,256]{3,2,1,0:T(8,128)(2,1)} %refs_0_.3), channel_id=1, source_target_pairs={{0,3},{1,2},{2,1},{3,0},{4,7},{5,6},{6,5},{7,4},{8,11},{9,10},{10,... | collective-permute-start | bytes 393224 | tf_op jit(solution)/shard_map/ppermute | solution.py:14
  3.1 5.0 %collective-permute-start = (bf16[1,1,256,256]{3,2,1,0:T(8,128)(2,1)}, bf16[1,1,256,256]{3,2,1,0:T(8,128)(2,1)S(1)}, u32[]{:S(2)}, u32[]{:S(2)}) collective-permute-start(bf16[1,1,256,256]{3,2,1,0:T(8,128)(2,1)} %refs_0_.3), channel_id=1, source_target_pairs={{0,1},{1,0},{2,3},{3,2},{4,5},{5,4},{6,7},{7,6},{8,9},{9,8},{10,11... | collective-permute-start | bytes 393224 | tf_op jit(solution)/shard_map/ppermute | solution.py:14
  3.8 13.0 %collective-permute-start.6 = (bf16[1,1,256,256]{3,2,1,0:T(8,128)(2,1)}, bf16[1,1,256,256]{3,2,1,0:T(8,128)(2,1)S(1)}, u32[]{:S(2)}, u32[]{:S(2)}) collective-permute-start(bf16[1,1,256,256]{3,2,1,0:T(8,128)(2,1)} %mine.3), channel_id=1, source_target_pairs={{1,0},{6,1},{10,2},{12,3},{2,4},{4,5},{8,6},{15,7},{0,8},{7,9},{11... | collective-permute-start | bytes 393224 | tf_op jit(solution)/shard_map/ppermute | solution.py:14
  6.4 10.5 %collective-permute-start.5 = (bf16[1,1,256,256]{3,2,1,0:T(8,128)(2,1)}, bf16[1,1,256,256]{3,2,1,0:T(8,128)(2,1)S(1)}, u32[]{:S(2)}, u32[]{:S(2)}) collective-permute-start(bf16[1,1,256,256]{3,2,1,0:T(8,128)(2,1)} %mine.3), channel_id=1, source_target_pairs={{2,0},{4,1},{8,2},{15,3},{1,4},{6,5},{10,6},{12,7},{3,8},{5,9},{9,... | collective-permute-start | bytes 393224 | tf_op jit(solution)/shard_map/ppermute | solution.py:14
  7.4 9.4 %collective-permute-start.4 = (bf16[1,1,256,256]{3,2,1,0:T(8,128)(2,1)}, bf16[1,1,256,256]{3,2,1,0:T(8,128)(2,1)S(1)}, u32[]{:S(2)}, u32[]{:S(2)}) collective-permute-start(bf16[1,1,256,256]{3,2,1,0:T(8,128)(2,1)} %mine.3), channel_id=1, source_target_pairs={{3,0},{5,1},{9,2},{14,3},{0,4},{7,5},{11,6},{13,7},{2,8},{4,9},{8,... | collective-permute-start | bytes 393224 | tf_op jit(solution)/shard_map/ppermute | solution.py:14
  7.4 9.5 %collective-permute-start.3 = (bf16[1,1,256,256]{3,2,1,0:T(8,128)(2,1)}, bf16[1,1,256,256]{3,2,1,0:T(8,128)(2,1)S(1)}, u32[]{:S(2)}, u32[]{:S(2)}) collective-permute-start(bf16[1,1,256,256]{3,2,1,0:T(8,128)(2,1)} %mine.3), channel_id=1, source_target_pairs={{7,1},{11,2},{13,3},{3,4},{9,6},{14,7},{1,8},{6,9},{12,11},{2,12},... | collective-permute-start | bytes 393224 | tf_op jit(solution)/shard_map/ppermute | solution.py:14
  8.1 8.8 %collective-permute-start.2 = (bf16[1,1,256,256]{3,2,1,0:T(8,128)(2,1)S(1)}, bf16[1,1,256,256]{3,2,1,0:T(8,128)(2,1)S(1)}, u32[]{:S(2)}, u32[]{:S(2)}) collective-permute-start(bf16[1,1,256,256]{3,2,1,0:T(8,128)(2,1)S(1)} %collective-permute-done.1.refs_3_), channel_id=1, source_target_pairs={{0,1},{1,0},{2,3},{3,2},{4,5},{5,4},{6,7},{7,6},{8,9},{9,8},{10,11... | collective-permute-start | bytes 393224 | tf_op jit(solution)/shard_map/ppermute | solution.py:14
  14.9 1.0 %copy-start.2 = (bf16[1,4,256,256]{3,2,1,0:T(8,128)(2,1)S(1)}, bf16[1,4,256,256]{3,2,1,0:T(8,128)(2,1)}, u32[]{:S(2)}) copy-start(bf16[1,4,256,256]{3,2,1,0:T(8,128)(2,1)} %two_site.1) | copy-start | bytes 1572868
  15.9 0.9 %copy-start = (bf16[1,1,256,256]{3,2,1,0:T(8,128)(2,1)S(1)}, bf16[1,1,256,256]{3,2,1,0:T(8,128)(2,1)}, u32[]{:S(2)}) copy-start(bf16[1,1,256,256]{3,2,1,0:T(8,128)(2,1)} %mine.3) | copy-start | bytes 393220
  15.9 1.0 %copy-start.1 = (bf16[1,1,256,256]{3,2,1,0:T(8,128)(2,1)S(1)}, bf16[1,1,256,256]{3,2,1,0:T(8,128)(2,1)}, u32[]{:S(2)}) copy-start(bf16[1,1,256,256]{3,2,1,0:T(8,128)(2,1)} %refs_0_.3) | copy-start | bytes 393220
  17.7 2.3 %collective-permute-start.7 = (f32[8,128]{1,0:T(8,128)S(1)}, f32[8,128]{1,0:T(8,128)S(1)}, u32[]{:S(2)}, u32[]{:S(2)}) collective-permute-start(f32[8,128]{1,0:T(8,128)S(1)} %get-tuple-element.13), channel_id=1, source_target_pairs={{0,1},{1,0},{2,3},{3,2},{4,5},{5,4},{6,7},{7,6},{8,9},{9,8},{10,11... | collective-permute-start | bytes 12296 | tf_op jit(solution)/shard_map/ppermute | solution.py:14
  20.0 3.0 %collective-permute-start.8 = (f32[8,128]{1,0:T(8,128)S(1)}, f32[8,128]{1,0:T(8,128)S(1)}, u32[]{:S(2)}, u32[]{:S(2)}) collective-permute-start(f32[8,128]{1,0:T(8,128)S(1)} %add.9), channel_id=1, source_target_pairs={{0,3},{1,2},{2,1},{3,0},{4,7},{5,6},{6,5},{7,4},{8,11},{9,10},{10,... | collective-permute-start | bytes 12296 | tf_op jit(solution)/shard_map/ppermute | solution.py:14
  23.0 3.0 %collective-permute-start.9 = (f32[8,128]{1,0:T(8,128)S(1)}, f32[8,128]{1,0:T(8,128)S(1)}, u32[]{:S(2)}, u32[]{:S(2)}) collective-permute-start(f32[8,128]{1,0:T(8,128)S(1)} %add.10), channel_id=1, source_target_pairs={{0,5},{1,4},{2,7},{3,6},{4,1},{5,0},{6,3},{7,2},{8,13},{9,12},{10,... | collective-permute-start | bytes 12296 | tf_op jit(solution)/shard_map/ppermute | solution.py:14
  26.1 4.0 %collective-permute-start.10 = (f32[8,128]{1,0:T(8,128)S(1)}, f32[8,128]{1,0:T(8,128)S(1)}, u32[]{:S(2)}, u32[]{:S(2)}) collective-permute-start(f32[8,128]{1,0:T(8,128)S(1)} %add.11.norm), channel_id=1, source_target_pairs={{0,9},{1,8},{2,11},{3,10},{4,13},{5,12},{6,15},{7,14},{8,1},{9,0},... | collective-permute-start | bytes 12296 | tf_op jit(solution)/shard_map/ppermute | solution.py:14

commit v6 on v5

--- a/solution.py
+++ b/solution.py
@@ -131,8 +131,10 @@
 
     rights = [move(right_env, pairs, terms) for pairs in right_routes(blocks, terms, own)]
     lefts = [left_env] + [None] * (terms - 1)
-    for m in list(range(1, terms, 2)) + list(range(2, terms, 2)):
+    for m in list(range(3, terms, 2)) + list(range(2, terms, 2)) + [1]:
         source, hop = (left_env, m) if m % 2 else (lefts[m + 1], 1)
+        if m == 1:
+            source, _ = lax.optimization_barrier((left_env, rights[-1]))
         lefts[m] = move(source, [((a, t), (a, t ^ hop)) for a, t in everyone], terms)
 
     tile = (own, width, width)

time: 31.1 us -> 30.4 us (0.977)
  starting transfers between devices: 21 us -> 17.1 us
  waiting for transfers between devices: 3.73 us -> 6.92 us
    ppermute x11, starting transfers between devices: 21 us -> 17.1 us  [move(): lax.ppermute(value, AXES, [(a * terms + b, c * terms + d) for (a, b), (c,...]
    ppermute x11, waiting for transfers between devices: 3.73 us -> 6.92 us  [move(): lax.ppermute(value, AXES, [(a * terms + b, c * terms + d) for (a, b), (c,...]
  transfers between devices with their start and end apart: 11 -> 11, of which waited for: 4 -> 7; matrix products, arithmetic and copies ran while one was open for 0% -> 0% of each run, Pallas kernels for 7% -> 7%
where the time goes in v6:
time: 30.4 us; the launch traced here: 30.2 us
  starting transfers between devices  17.1 us (56%)
  waiting for transfers between devices  6.92 us (23%)
  Pallas kernels  3.74 us (12%)
  between operations  1.39 us (5%)
  local copies, waits for them, and re-layouts  1.05 us (3%)
    ppermute x11, starting transfers between devices, move(): lax.ppermute(value, AXES, [(a * terms + b, c * terms + d) for (a, b), (c,...  17.1 us
    ppermute x11, waiting for transfers between devices, move(): lax.ppermute(value, AXES, [(a * terms + b, c * terms + d) for (a, b), (c,...  6.92 us
    pallas_call x2, Pallas kernels, apply_call(): pl.pallas_call(functools.partial(kernel, blocks, terms, own), out_shape=o...  2.04 us
    unnamed x10, local copies, waits for them, and re-layouts  1.05 us
    pallas_call x1, Pallas kernels, local(): pl.pallas_call(functools.partial(start_kernel, own), out_shape=(jax.Shape...  0.86 us
    pallas_call x1, Pallas kernels, local(): pl.pallas_call(functools.partial(scale_kernel, float(blocks * n_cols * wi...  0.83 us
  transfers between devices with their start and end apart: 11, of which 7 were waited for; matrix products, arithmetic and copies ran while one was open for 0% of the time, Pallas kernels for 7%

profile of v6, /device:TPU:0, one launch (start us, length us, event | category | flops | bytes accessed | tf_op | source)
XLA Modules:
  0.0 30.2 jit_solution(8744580520057455837)
XLA Ops:
  0.6 0.0 copy-start.4
  0.6 0.0 copy-start.3
  0.7 4.1 %collective-permute-start = (bf16[1,1,256,256]{3,2,1,0:T(8,128)(2,1)}, bf16[1,1,256,256]{3,2,1,0:T(8,128)(2,1)S(1)}, u32[]{:S(2)}, u32[]{:S(2)}) collective-permute-start(bf16[1,1,256,256]{3,2,1,0:T(8,128)(2,1)} %mine.3), channel_id=1, source_target_pairs={{1,0},{6,1},{10,2},{12,3},{2,4},{4,5},{8,6},{15,7},{0,8},{7,9},{11... | collective-permute-start | bytes 393224 | tf_op jit(solution)/shard_map/ppermute | solution.py:14
  4.7 2.2 %collective-permute-start.2 = (bf16[1,1,256,256]{3,2,1,0:T(8,128)(2,1)}, bf16[1,1,256,256]{3,2,1,0:T(8,128)(2,1)S(1)}, u32[]{:S(2)}, u32[]{:S(2)}) collective-permute-start(bf16[1,1,256,256]{3,2,1,0:T(8,128)(2,1)} %refs_0_.3), channel_id=1, source_target_pairs={{0,3},{1,2},{2,1},{3,0},{4,7},{5,6},{6,5},{7,4},{8,11},{9,10},{10,... | collective-permute-start | bytes 393224 | tf_op jit(solution)/shard_map/ppermute | solution.py:14
  6.9 0.0 collective-permute-start.6
  6.9 0.0 collective-permute-start.5
  6.9 0.7 %collective-permute-start.4 = (bf16[1,1,256,256]{3,2,1,0:T(8,128)(2,1)}, bf16[1,1,256,256]{3,2,1,0:T(8,128)(2,1)S(1)}, u32[]{:S(2)}, u32[]{:S(2)}) collective-permute-start(bf16[1,1,256,256]{3,2,1,0:T(8,128)(2,1)} %mine.3), channel_id=1, source_target_pairs={{7,1},{11,2},{13,3},{3,4},{9,6},{14,7},{1,8},{6,9},{12,11},{2,12},... | collective-permute-start | bytes 393224 | tf_op jit(solution)/shard_map/ppermute | solution.py:14
  7.6 0.8 %collective-permute-done.refs_7_ = bf16[1,1,256,256]{3,2,1,0:T(8,128)(2,1)S(1)} collective-permute-done((bf16[1,1,256,256]{3,2,1,0:T(8,128)(2,1)}, bf16[1,1,256,256]{3,2,1,0:T(8,128)(2,1)S(1)}, u32[]{:S(2)}, u32[]{:S(2)}) %collective-permute-start) | collective-permute-done | bytes 131104 | tf_op jit(solution)/shard_map/ppermute | solution.py:14
  8.4 2.2 %collective-permute-done.2.refs_3_ = bf16[1,1,256,256]{3,2,1,0:T(8,128)(2,1)S(1)} collective-permute-done((bf16[1,1,256,256]{3,2,1,0:T(8,128)(2,1)}, bf16[1,1,256,256]{3,2,1,0:T(8,128)(2,1)S(1)}, u32[]{:S(2)}, u32[]{:S(2)}) %collective-permute-start.2) | collective-permute-done | bytes 131104 | tf_op jit(solution)/shard_map/ppermute | solution.py:14
  10.6 0.5 %collective-permute-start.3 = (bf16[1,1,256,256]{3,2,1,0:T(8,128)(2,1)S(1)}, bf16[1,1,256,256]{3,2,1,0:T(8,128)(2,1)S(1)}, u32[]{:S(2)}, u32[]{:S(2)}) collective-permute-start(bf16[1,1,256,256]{3,2,1,0:T(8,128)(2,1)S(1)} %collective-permute-done.2.refs_3_), channel_id=1, source_target_pairs={{0,1},{1,0},{2,3},{3,2},{4,5},{5,4},{6,7},{7,6},{8,9},{9,8},{10,11... | collective-permute-start | bytes 393224 | tf_op jit(solution)/shard_map/ppermute | solution.py:14
  11.1 0.1 collective-permute-start.1
  11.9 0.0 copy-done.4
  11.9 1.0 %copy-done.2 = bf16[1,4,256,256]{3,2,1,0:T(8,128)(2,1)S(1)} copy-done((bf16[1,4,256,256]{3,2,1,0:T(8,128)(2,1)S(1)}, bf16[1,4,256,256]{3,2,1,0:T(8,128)(2,1)}, u32[]{:S(2)}) %copy-start.2) | copy-done | bytes 524312
  12.9 0.9 %shard_map.77 = (bf16[1,256,256]{2,1,0:T(8,128)(2,1)S(1)}, f32[1,256,256]{2,1,0:T(8,128)S(1)}) custom-call(bf16[1,4,256,256]{3,2,1,0:T(8,128)(2,1)S(1)} %copy-done.2, s32[1]{0:T(128)S(6)} %copy.8.rows, s32[4]{0:T(128)S(1)} %copy-done.3, s32[1,4]{1,0:T(1,128)S(1)} %copy-done.4), custom_call_target="tpu_custom_call" | custom-call | bytes 524288 | tf_op jit(solution)/shard_map/pallas_call | solution.py:141
  13.8 0.0 collective-permute-done.6.refs_6_
  13.8 0.2 collective-permute-done.5.refs_5_
  14.0 0.0 collective-permute-done.4.refs_4_
  14.0 0.0 collective-permute-done.3.refs_2_
  14.0 0.0 collective-permute-done.1.refs_1_
  14.0 0.0 copy-done
  14.0 0.0 copy-done.1
  14.0 0.8 %shard_map.78 = (bf16[1,256,256]{2,1,0:T(8,128)(2,1)S(1)}, f32[8,128]{1,0:T(8,128)S(1)}) custom-call(bf16[1,256,256]{2,1,0:T(8,128)(2,1)S(1)} %get-tuple-element.9.start, f32[1,256,256]{2,1,0:T(8,128)S(1)} %get-tuple-element.10.keep, bf16[1,1,256,256]{3,2,1,0:T(8,128)(2,1)S(1)} %copy-done, bf16[1,1,256,256]{3,2,1,0:T(8,128)(2,1)S(1)} %copy-done.1, ...), custom_call_target="tpu_custom_call" | custom-call | flops 268435456 | bytes 524288 | tf_op jit(solution)/shard_map/pallas_call | solution.py:161
  14.8 2.2 %collective-permute-start.7 = (f32[8,128]{1,0:T(8,128)S(1)}, f32[8,128]{1,0:T(8,128)S(1)}, u32[]{:S(2)}, u32[]{:S(2)}) collective-permute-start(f32[8,128]{1,0:T(8,128)S(1)} %get-tuple-element.15), channel_id=1, source_target_pairs={{0,1},{1,0},{2,3},{3,2},{4,5},{5,4},{6,7},{7,6},{8,9},{9,8},{10,11... | collective-permute-start | bytes 12296 | tf_op jit(solution)/shard_map/ppermute | solution.py:14
  17.0 0.8 %collective-permute-done.7 = f32[8,128]{1,0:T(8,128)S(1)} collective-permute-done((f32[8,128]{1,0:T(8,128)S(1)}, f32[8,128]{1,0:T(8,128)S(1)}, u32[]{:S(2)}, u32[]{:S(2)}) %collective-permute-start.7) | collective-permute-done | bytes 4128 | tf_op jit(solution)/shard_map/ppermute | solution.py:14
  17.9 3.2 %collective-permute-start.8 = (f32[8,128]{1,0:T(8,128)S(1)}, f32[8,128]{1,0:T(8,128)S(1)}, u32[]{:S(2)}, u32[]{:S(2)}) collective-permute-start(f32[8,128]{1,0:T(8,128)S(1)} %add.9), channel_id=1, source_target_pairs={{0,3},{1,2},{2,1},{3,0},{4,7},{5,6},{6,5},{7,4},{8,11},{9,10},{10,... | collective-permute-start | bytes 12296 | tf_op jit(solution)/shard_map/ppermute | solution.py:14
  21.1 1.3 %collective-permute-done.8 = f32[8,128]{1,0:T(8,128)S(1)} collective-permute-done((f32[8,128]{1,0:T(8,128)S(1)}, f32[8,128]{1,0:T(8,128)S(1)}, u32[]{:S(2)}, u32[]{:S(2)}) %collective-permute-start.8) | collective-permute-done | bytes 4128 | tf_op jit(solution)/shard_map/ppermute | solution.py:14
  22.4 1.6 %collective-permute-start.9 = (f32[8,128]{1,0:T(8,128)S(1)}, f32[8,128]{1,0:T(8,128)S(1)}, u32[]{:S(2)}, u32[]{:S(2)}) collective-permute-start(f32[8,128]{1,0:T(8,128)S(1)} %add.10), channel_id=1, source_target_pairs={{0,5},{1,4},{2,7},{3,6},{4,1},{5,0},{6,3},{7,2},{8,13},{9,12},{10,... | collective-permute-start | bytes 12296 | tf_op jit(solution)/shard_map/ppermute | solution.py:14
  24.0 1.4 %collective-permute-done.9 = f32[8,128]{1,0:T(8,128)S(1)} collective-permute-done((f32[8,128]{1,0:T(8,128)S(1)}, f32[8,128]{1,0:T(8,128)S(1)}, u32[]{:S(2)}, u32[]{:S(2)}) %collective-permute-start.9) | collective-permute-done | bytes 4128 | tf_op jit(solution)/shard_map/ppermute | solution.py:14
  25.5 2.6 %collective-permute-start.10 = (f32[8,128]{1,0:T(8,128)S(1)}, f32[8,128]{1,0:T(8,128)S(1)}, u32[]{:S(2)}, u32[]{:S(2)}) collective-permute-start(f32[8,128]{1,0:T(8,128)S(1)} %add.11.norm), channel_id=1, source_target_pairs={{0,9},{1,8},{2,11},{3,10},{4,13},{5,12},{6,15},{7,14},{8,1},{9,0},... | collective-permute-start | bytes 12296 | tf_op jit(solution)/shard_map/ppermute | solution.py:14
  28.0 1.3 %shard_map.79 = (bf16[1,1,256,256]{3,2,1,0:T(8,128)(2,1)}, f32[1,1,256,256]{3,2,1,0:T(8,128)S(1)}) custom-call(bf16[1,256,256]{2,1,0:T(8,128)(2,1)S(1)} %get-tuple-element.12.image, f32[1,256,256]{2,1,0:T(8,128)S(1)} %get-tuple-element.10.keep, bf16[1,1,256,256]{3,2,1,0:T(8,128)(2,1)S(1)} %copy-done, bf16[1,1,256,256]{3,2,1,0:T(8,128)(2,1)S(1)} %copy-done.1, ...), custom_call_target="tpu_custom_call" | custom-call | flops 268435456 | bytes 524288 | tf_op jit(solution)/shard_map/pallas_call | solution.py:161
  29.3 0.1 collective-permute-done.10.other
  29.4 0.8 %shard_map.80 = bf16[1,1,256,256]{3,2,1,0:T(8,128)(2,1)} custom-call(f32[1,1,256,256]{3,2,1,0:T(8,128)S(1)} %get-tuple-element.14.raw, f32[8,128]{1,0:T(8,128)S(1)} %add.11.norm, f32[8,128]{1,0:T(8,128)S(1)} %collective-permute-done.10.other), custom_call_target="tpu_custom_call" | custom-call | tf_op jit(solution)/shard_map/pallas_call | solution.py:189
  (7 shorter events, 0.0 us)
Async XLA Ops:
  0.6 11.2 %copy-start.4 = (s32[1,4]{1,0:T(1,128)S(1)}, s32[1,4]{1,0:T(1,128)}, u32[]{:S(2)}) copy-start(s32[1,4]{1,0:T(1,128)} %live.1) | copy-start | bytes 52
  0.6 11.2 %copy-start.3 = (s32[4]{0:T(128)S(1)}, s32[4]{0:T(128)}, u32[]{:S(2)}) copy-start(s32[4]{0:T(128)} %cols.1) | copy-start | bytes 52
  0.7 7.7 %collective-permute-start = (bf16[1,1,256,256]{3,2,1,0:T(8,128)(2,1)}, bf16[1,1,256,256]{3,2,1,0:T(8,128)(2,1)S(1)}, u32[]{:S(2)}, u32[]{:S(2)}) collective-permute-start(bf16[1,1,256,256]{3,2,1,0:T(8,128)(2,1)} %mine.3), channel_id=1, source_target_pairs={{1,0},{6,1},{10,2},{12,3},{2,4},{4,5},{8,6},{15,7},{0,8},{7,9},{11... | collective-permute-start | bytes 393224 | tf_op jit(solution)/shard_map/ppermute | solution.py:14
  4.7 5.9 %collective-permute-start.2 = (bf16[1,1,256,256]{3,2,1,0:T(8,128)(2,1)}, bf16[1,1,256,256]{3,2,1,0:T(8,128)(2,1)S(1)}, u32[]{:S(2)}, u32[]{:S(2)}) collective-permute-start(bf16[1,1,256,256]{3,2,1,0:T(8,128)(2,1)} %refs_0_.3), channel_id=1, source_target_pairs={{0,3},{1,2},{2,1},{3,0},{4,7},{5,6},{6,5},{7,4},{8,11},{9,10},{10,... | collective-permute-start | bytes 393224 | tf_op jit(solution)/shard_map/ppermute | solution.py:14
  6.9 6.9 %collective-permute-start.6 = (bf16[1,1,256,256]{3,2,1,0:T(8,128)(2,1)}, bf16[1,1,256,256]{3,2,1,0:T(8,128)(2,1)S(1)}, u32[]{:S(2)}, u32[]{:S(2)}) collective-permute-start(bf16[1,1,256,256]{3,2,1,0:T(8,128)(2,1)} %mine.3), channel_id=1, source_target_pairs={{2,0},{4,1},{8,2},{15,3},{1,4},{6,5},{10,6},{12,7},{3,8},{5,9},{9,... | collective-permute-start | bytes 393224 | tf_op jit(solution)/shard_map/ppermute | solution.py:14
  6.9 7.1 %collective-permute-start.5 = (bf16[1,1,256,256]{3,2,1,0:T(8,128)(2,1)}, bf16[1,1,256,256]{3,2,1,0:T(8,128)(2,1)S(1)}, u32[]{:S(2)}, u32[]{:S(2)}) collective-permute-start(bf16[1,1,256,256]{3,2,1,0:T(8,128)(2,1)} %mine.3), channel_id=1, source_target_pairs={{3,0},{5,1},{9,2},{14,3},{0,4},{7,5},{11,6},{13,7},{2,8},{4,9},{8,... | collective-permute-start | bytes 393224 | tf_op jit(solution)/shard_map/ppermute | solution.py:14
  6.9 7.1 %collective-permute-start.4 = (bf16[1,1,256,256]{3,2,1,0:T(8,128)(2,1)}, bf16[1,1,256,256]{3,2,1,0:T(8,128)(2,1)S(1)}, u32[]{:S(2)}, u32[]{:S(2)}) collective-permute-start(bf16[1,1,256,256]{3,2,1,0:T(8,128)(2,1)} %mine.3), channel_id=1, source_target_pairs={{7,1},{11,2},{13,3},{3,4},{9,6},{14,7},{1,8},{6,9},{12,11},{2,12},... | collective-permute-start | bytes 393224 | tf_op jit(solution)/shard_map/ppermute | solution.py:14
  10.6 3.4 %collective-permute-start.3 = (bf16[1,1,256,256]{3,2,1,0:T(8,128)(2,1)S(1)}, bf16[1,1,256,256]{3,2,1,0:T(8,128)(2,1)S(1)}, u32[]{:S(2)}, u32[]{:S(2)}) collective-permute-start(bf16[1,1,256,256]{3,2,1,0:T(8,128)(2,1)S(1)} %collective-permute-done.2.refs_3_), channel_id=1, source_target_pairs={{0,1},{1,0},{2,3},{3,2},{4,5},{5,4},{6,7},{7,6},{8,9},{9,8},{10,11... | collective-permute-start | bytes 393224 | tf_op jit(solution)/shard_map/ppermute | solution.py:14
  11.1 2.9 %collective-permute-start.1 = (bf16[1,1,256,256]{3,2,1,0:T(8,128)(2,1)}, bf16[1,1,256,256]{3,2,1,0:T(8,128)(2,1)S(1)}, u32[]{:S(2)}, u32[]{:S(2)}) collective-permute-start(bf16[1,1,256,256]{3,2,1,0:T(8,128)(2,1)} %refs_0_.3), channel_id=1, source_target_pairs={{0,1},{1,0},{2,3},{3,2},{4,5},{5,4},{6,7},{7,6},{8,9},{9,8},{10,11... | collective-permute-start | bytes 393224 | tf_op jit(solution)/shard_map/ppermute | solution.py:14
  11.9 1.0 %copy-start.2 = (bf16[1,4,256,256]{3,2,1,0:T(8,128)(2,1)S(1)}, bf16[1,4,256,256]{3,2,1,0:T(8,128)(2,1)}, u32[]{:S(2)}) copy-start(bf16[1,4,256,256]{3,2,1,0:T(8,128)(2,1)} %two_site.1) | copy-start | bytes 1572868
  12.9 1.1 %copy-start = (bf16[1,1,256,256]{3,2,1,0:T(8,128)(2,1)S(1)}, bf16[1,1,256,256]{3,2,1,0:T(8,128)(2,1)}, u32[]{:S(2)}) copy-start(bf16[1,1,256,256]{3,2,1,0:T(8,128)(2,1)} %mine.3) | copy-start | bytes 393220
  12.9 1.1 %copy-start.1 = (bf16[1,1,256,256]{3,2,1,0:T(8,128)(2,1)S(1)}, bf16[1,1,256,256]{3,2,1,0:T(8,128)(2,1)}, u32[]{:S(2)}) copy-start(bf16[1,1,256,256]{3,2,1,0:T(8,128)(2,1)} %refs_0_.3) | copy-start | bytes 393220
  14.8 3.0 %collective-permute-start.7 = (f32[8,128]{1,0:T(8,128)S(1)}, f32[8,128]{1,0:T(8,128)S(1)}, u32[]{:S(2)}, u32[]{:S(2)}) collective-permute-start(f32[8,128]{1,0:T(8,128)S(1)} %get-tuple-element.15), channel_id=1, source_target_pairs={{0,1},{1,0},{2,3},{3,2},{4,5},{5,4},{6,7},{7,6},{8,9},{9,8},{10,11... | collective-permute-start | bytes 12296 | tf_op jit(solution)/shard_map/ppermute | solution.py:14
  17.9 4.6 %collective-permute-start.8 = (f32[8,128]{1,0:T(8,128)S(1)}, f32[8,128]{1,0:T(8,128)S(1)}, u32[]{:S(2)}, u32[]{:S(2)}) collective-permute-start(f32[8,128]{1,0:T(8,128)S(1)} %add.9), channel_id=1, source_target_pairs={{0,3},{1,2},{2,1},{3,0},{4,7},{5,6},{6,5},{7,4},{8,11},{9,10},{10,... | collective-permute-start | bytes 12296 | tf_op jit(solution)/shard_map/ppermute | solution.py:14
  22.4 3.0 %collective-permute-start.9 = (f32[8,128]{1,0:T(8,128)S(1)}, f32[8,128]{1,0:T(8,128)S(1)}, u32[]{:S(2)}, u32[]{:S(2)}) collective-permute-start(f32[8,128]{1,0:T(8,128)S(1)} %add.10), channel_id=1, source_target_pairs={{0,5},{1,4},{2,7},{3,6},{4,1},{5,0},{6,3},{7,2},{8,13},{9,12},{10,... | collective-permute-start | bytes 12296 | tf_op jit(solution)/shard_map/ppermute | solution.py:14
  25.5 3.9 %collective-permute-start.10 = (f32[8,128]{1,0:T(8,128)S(1)}, f32[8,128]{1,0:T(8,128)S(1)}, u32[]{:S(2)}, u32[]{:S(2)}) collective-permute-start(f32[8,128]{1,0:T(8,128)S(1)} %add.11.norm), channel_id=1, source_target_pairs={{0,9},{1,8},{2,11},{3,10},{4,13},{5,12},{6,15},{7,14},{8,1},{9,0},... | collective-permute-start | bytes 12296 | tf_op jit(solution)/shard_map/ppermute | solution.py:14

commit v7 on v6

--- a/solution.py
+++ b/solution.py
@@ -16,28 +16,27 @@
     )
 
 
-ORDERS = ((2, 0, 1, 3), (1, 3, 0, 2), (1, 3, 0, 2), (0, 2, 3, 1))
-STEPS = (2, 3, 1, 0)
-
-
-def steps_of(blocks, own):
-    return STEPS if blocks == 4 and own == 1 else range(blocks)
+ROUTES = (
+    ((0, 2, 3, 1), (3, 1, 0, 2), (1, 3, 2, 0), (2, 0, 1, 3)),
+    ((3, 1, 2, 0), (1, 3, 0, 2), (2, 0, 3, 1), (0, 2, 1, 3)),
+    ((3, 1, 2, 0), (1, 3, 0, 2), (0, 2, 1, 3), (2, 0, 3, 1)),
+    ((0, 2, 1, 3), (2, 0, 3, 1), (1, 3, 0, 2), (3, 1, 2, 0)),
+)
 
 
 def source_number(blocks, own, blk, term, step):
-    place = blk ^ step
     if blocks == 4 and own == 1:
-        packed = sum(i << (8 * g + 2 * p) for g, order in enumerate(ORDERS) for i, p in enumerate(order))
-        if not isinstance(place, int):
+        packed = sum(i << (8 * g + 2 * p) for g, r in enumerate(ROUTES) for i, p in enumerate(r[step]))
+        if not isinstance(blk, int):
             packed = jnp.int32(packed - (packed >> 31 << 32))
-        return (packed >> (8 * term + 2 * place)) & 3
-    half = blocks // 2
+        return (packed >> (8 * term + 2 * blk)) & 3
+    half, place = blocks // 2, blk ^ step
     return (place % half) * 2 + place // half
 
 
 def right_routes(blocks, terms, own):
     routes = []
-    for step in steps_of(blocks, own):
+    for step in range(blocks):
         pairs = []
         for a in range(blocks):
             for group in range(terms):
@@ -77,7 +76,7 @@
 
 def apply_tiles(blocks, terms, own, tile, keep, mine, lefts, rights, products):
     blk, term = lax.axis_index("blk"), lax.axis_index("term")
-    for step, right in zip(steps_of(blocks, own), rights):
+    for step, right in enumerate(rights):
         i = source_number(blocks, own, blk, term, step)
         products[i] = dot(tile[i // terms], right[0, 0]).astype(jnp.bfloat16)
 
@@ -181,6 +180,8 @@
 
     flips = [(0, 1)] + [(0, 1 | 1 << s) for s in range(1, (terms - 1).bit_length())]
     flips += [(1 << s, 1) for s in range((blocks - 1).bit_length())]
+    if len(flips) == 4:
+        flips = [flips[i] for i in (1, 3, 0, 2)]
     norm, other = partial, None
     for da, dt in flips:
         norm = norm if other is None else norm + other

time: 30.4 us -> 30.3 us (level)
  waiting for transfers between devices: 6.92 us -> 6.1 us
  starting transfers between devices: 17.1 us -> 17.8 us
    ppermute x11, waiting for transfers between devices: 6.92 us -> 6.1 us  [move(): lax.ppermute(value, AXES, [(a * terms + b, c * terms + d) for (a, b), (c,...]
    ppermute x11, starting transfers between devices: 17.1 us -> 17.8 us  [move(): lax.ppermute(value, AXES, [(a * terms + b, c * terms + d) for (a, b), (c,...]
  transfers between devices with their start and end apart: 11 -> 11, of which waited for: 7 -> 5; matrix products, arithmetic and copies ran while one was open for 0% -> 0% of each run, Pallas kernels for 7% -> 7%
where the time goes in v7:
time: 30.3 us; the launch traced here: 30.1 us
  starting transfers between devices  17.8 us (59%)
  waiting for transfers between devices  6.1 us (20%)
  Pallas kernels  3.74 us (12%)
  between operations  1.41 us (5%)
  local copies, waits for them, and re-layouts  1.08 us (4%)
    ppermute x11, starting transfers between devices, move(): lax.ppermute(value, AXES, [(a * terms + b, c * terms + d) for (a, b), (c,...  17.8 us
    ppermute x11, waiting for transfers between devices, move(): lax.ppermute(value, AXES, [(a * terms + b, c * terms + d) for (a, b), (c,...  6.1 us
    pallas_call x2, Pallas kernels, apply_call(): pl.pallas_call(functools.partial(kernel, blocks, terms, own), out_shape=o...  2.04 us
    unnamed x10, local copies, waits for them, and re-layouts  1.08 us
    pallas_call x1, Pallas kernels, local(): pl.pallas_call(functools.partial(start_kernel, own), out_shape=(jax.Shape...  0.86 us
    pallas_call x1, Pallas kernels, local(): pl.pallas_call(functools.partial(scale_kernel, float(blocks * n_cols * wi...  0.83 us
  transfers between devices with their start and end apart: 11, of which 5 were waited for; matrix products, arithmetic and copies ran while one was open for 0% of the time, Pallas kernels for 7%

profile of v7, /device:TPU:0, one launch (start us, length us, event | category | flops | bytes accessed | tf_op | source)
XLA Modules:
  0.0 30.1 jit_solution(17767473903991519354)
XLA Ops:
  0.6 0.0 copy-start.4
  0.6 0.0 copy-start.3
  0.7 4.1 %collective-permute-start = (bf16[1,1,256,256]{3,2,1,0:T(8,128)(2,1)}, bf16[1,1,256,256]{3,2,1,0:T(8,128)(2,1)S(1)}, u32[]{:S(2)}, u32[]{:S(2)}) collective-permute-start(bf16[1,1,256,256]{3,2,1,0:T(8,128)(2,1)} %mine.3), channel_id=1, source_target_pairs={{1,0},{4,1},{9,2},{15,3},{2,4},{6,5},{11,6},{13,7},{0,8},{5,9},{8,... | collective-permute-start | bytes 393224 | tf_op jit(solution)/shard_map/ppermute | solution.py:14
  4.7 2.2 %collective-permute-start.2 = (bf16[1,1,256,256]{3,2,1,0:T(8,128)(2,1)}, bf16[1,1,256,256]{3,2,1,0:T(8,128)(2,1)S(1)}, u32[]{:S(2)}, u32[]{:S(2)}) collective-permute-start(bf16[1,1,256,256]{3,2,1,0:T(8,128)(2,1)} %refs_0_.3), channel_id=1, source_target_pairs={{0,3},{1,2},{2,1},{3,0},{4,7},{5,6},{6,5},{7,4},{8,11},{9,10},{10,... | collective-permute-start | bytes 393224 | tf_op jit(solution)/shard_map/ppermute | solution.py:14
  6.9 0.0 collective-permute-start.6
  6.9 1.8 %collective-permute-start.5 = (bf16[1,1,256,256]{3,2,1,0:T(8,128)(2,1)}, bf16[1,1,256,256]{3,2,1,0:T(8,128)(2,1)S(1)}, u32[]{:S(2)}, u32[]{:S(2)}) collective-permute-start(bf16[1,1,256,256]{3,2,1,0:T(8,128)(2,1)} %mine.3), channel_id=1, source_target_pairs={{2,0},{6,1},{10,2},{13,3},{1,4},{4,5},{8,6},{15,7},{3,8},{7,9},{11... | collective-permute-start | bytes 393224 | tf_op jit(solution)/shard_map/ppermute | solution.py:14
  8.7 0.7 %collective-permute-start.4 = (bf16[1,1,256,256]{3,2,1,0:T(8,128)(2,1)}, bf16[1,1,256,256]{3,2,1,0:T(8,128)(2,1)S(1)}, u32[]{:S(2)}, u32[]{:S(2)}) collective-permute-start(bf16[1,1,256,256]{3,2,1,0:T(8,128)(2,1)} %mine.3), channel_id=1, source_target_pairs={{7,1},{11,2},{12,3},{3,4},{9,6},{14,7},{1,8},{6,9},{13,11},{2,12},... | collective-permute-start | bytes 393224 | tf_op jit(solution)/shard_map/ppermute | solution.py:14
  9.4 0.0 collective-permute-done.refs_7_
  9.4 1.9 %collective-permute-done.2.refs_3_ = bf16[1,1,256,256]{3,2,1,0:T(8,128)(2,1)S(1)} collective-permute-done((bf16[1,1,256,256]{3,2,1,0:T(8,128)(2,1)}, bf16[1,1,256,256]{3,2,1,0:T(8,128)(2,1)S(1)}, u32[]{:S(2)}, u32[]{:S(2)}) %collective-permute-start.2) | collective-permute-done | bytes 131104 | tf_op jit(solution)/shard_map/ppermute | solution.py:14
  11.3 0.8 %collective-permute-start.3 = (bf16[1,1,256,256]{3,2,1,0:T(8,128)(2,1)S(1)}, bf16[1,1,256,256]{3,2,1,0:T(8,128)(2,1)S(1)}, u32[]{:S(2)}, u32[]{:S(2)}) collective-permute-start(bf16[1,1,256,256]{3,2,1,0:T(8,128)(2,1)S(1)} %collective-permute-done.2.refs_3_), channel_id=1, source_target_pairs={{0,1},{1,0},{2,3},{3,2},{4,5},{5,4},{6,7},{7,6},{8,9},{9,8},{10,11... | collective-permute-start | bytes 393224 | tf_op jit(solution)/shard_map/ppermute | solution.py:14
  12.1 0.1 collective-permute-start.1
  12.8 0.0 copy-done.4
  12.8 0.0 copy-done.3
  12.8 1.0 %copy-done.2 = bf16[1,4,256,256]{3,2,1,0:T(8,128)(2,1)S(1)} copy-done((bf16[1,4,256,256]{3,2,1,0:T(8,128)(2,1)S(1)}, bf16[1,4,256,256]{3,2,1,0:T(8,128)(2,1)}, u32[]{:S(2)}) %copy-start.2) | copy-done | bytes 524312
  13.9 0.9 %shard_map.77 = (bf16[1,256,256]{2,1,0:T(8,128)(2,1)S(1)}, f32[1,256,256]{2,1,0:T(8,128)S(1)}) custom-call(bf16[1,4,256,256]{3,2,1,0:T(8,128)(2,1)S(1)} %copy-done.2, s32[1]{0:T(128)S(6)} %copy.8.rows, s32[4]{0:T(128)S(1)} %copy-done.3, s32[1,4]{1,0:T(1,128)S(1)} %copy-done.4), custom_call_target="tpu_custom_call" | custom-call | bytes 524288 | tf_op jit(solution)/shard_map/pallas_call | solution.py:140
  14.7 0.0 collective-permute-done.6.refs_6_
  14.8 0.0 collective-permute-done.5.refs_5_
  14.8 0.0 collective-permute-done.4.refs_4_
  14.8 0.0 collective-permute-done.3.refs_2_
  14.8 0.0 collective-permute-done.1.refs_1_
  14.8 0.0 copy-done.1
  14.8 0.8 %shard_map.78 = (bf16[1,256,256]{2,1,0:T(8,128)(2,1)S(1)}, f32[8,128]{1,0:T(8,128)S(1)}) custom-call(bf16[1,256,256]{2,1,0:T(8,128)(2,1)S(1)} %get-tuple-element.9.start, f32[1,256,256]{2,1,0:T(8,128)S(1)} %get-tuple-element.10.keep, bf16[1,1,256,256]{3,2,1,0:T(8,128)(2,1)S(1)} %copy-done, bf16[1,1,256,256]{3,2,1,0:T(8,128)(2,1)S(1)} %copy-done.1, ...), custom_call_target="tpu_custom_call" | custom-call | flops 268435456 | bytes 524288 | tf_op jit(solution)/shard_map/pallas_call | solution.py:160
  15.6 3.8 %collective-permute-start.7 = (f32[8,128]{1,0:T(8,128)S(1)}, f32[8,128]{1,0:T(8,128)S(1)}, u32[]{:S(2)}, u32[]{:S(2)}) collective-permute-start(f32[8,128]{1,0:T(8,128)S(1)} %get-tuple-element.15), channel_id=1, source_target_pairs={{0,3},{1,2},{2,1},{3,0},{4,7},{5,6},{6,5},{7,4},{8,11},{9,10},{10,... | collective-permute-start | bytes 12296 | tf_op jit(solution)/shard_map/ppermute | solution.py:14
  19.4 1.3 %collective-permute-done.7 = f32[8,128]{1,0:T(8,128)S(1)} collective-permute-done((f32[8,128]{1,0:T(8,128)S(1)}, f32[8,128]{1,0:T(8,128)S(1)}, u32[]{:S(2)}, u32[]{:S(2)}) %collective-permute-start.7) | collective-permute-done | bytes 4128 | tf_op jit(solution)/shard_map/ppermute | solution.py:14
  20.8 3.0 %collective-permute-start.8 = (f32[8,128]{1,0:T(8,128)S(1)}, f32[8,128]{1,0:T(8,128)S(1)}, u32[]{:S(2)}, u32[]{:S(2)}) collective-permute-start(f32[8,128]{1,0:T(8,128)S(1)} %add.9), channel_id=1, source_target_pairs={{0,9},{1,8},{2,11},{3,10},{4,13},{5,12},{6,15},{7,14},{8,1},{9,0},... | collective-permute-start | bytes 12296 | tf_op jit(solution)/shard_map/ppermute | solution.py:14
  23.8 1.3 %collective-permute-done.8 = f32[8,128]{1,0:T(8,128)S(1)} collective-permute-done((f32[8,128]{1,0:T(8,128)S(1)}, f32[8,128]{1,0:T(8,128)S(1)}, u32[]{:S(2)}, u32[]{:S(2)}) %collective-permute-start.8) | collective-permute-done | bytes 4128 | tf_op jit(solution)/shard_map/ppermute | solution.py:14
  25.1 0.3 %collective-permute-start.9 = (f32[8,128]{1,0:T(8,128)S(1)}, f32[8,128]{1,0:T(8,128)S(1)}, u32[]{:S(2)}, u32[]{:S(2)}) collective-permute-start(f32[8,128]{1,0:T(8,128)S(1)} %add.10), channel_id=1, source_target_pairs={{0,1},{1,0},{2,3},{3,2},{4,5},{5,4},{6,7},{7,6},{8,9},{9,8},{10,11... | collective-permute-start | bytes 12296 | tf_op jit(solution)/shard_map/ppermute | solution.py:14
  25.4 0.8 %collective-permute-done.9 = f32[8,128]{1,0:T(8,128)S(1)} collective-permute-done((f32[8,128]{1,0:T(8,128)S(1)}, f32[8,128]{1,0:T(8,128)S(1)}, u32[]{:S(2)}, u32[]{:S(2)}) %collective-permute-start.9) | collective-permute-done | bytes 4128 | tf_op jit(solution)/shard_map/ppermute | solution.py:14
  26.3 1.1 %collective-permute-start.10 = (f32[8,128]{1,0:T(8,128)S(1)}, f32[8,128]{1,0:T(8,128)S(1)}, u32[]{:S(2)}, u32[]{:S(2)}) collective-permute-start(f32[8,128]{1,0:T(8,128)S(1)} %add.11.norm), channel_id=1, source_target_pairs={{0,5},{1,4},{2,7},{3,6},{4,1},{5,0},{6,3},{7,2},{8,13},{9,12},{10,... | collective-permute-start | bytes 12296 | tf_op jit(solution)/shard_map/ppermute | solution.py:14
  27.3 1.3 %shard_map.79 = (bf16[1,1,256,256]{3,2,1,0:T(8,128)(2,1)}, f32[1,1,256,256]{3,2,1,0:T(8,128)S(1)}) custom-call(bf16[1,256,256]{2,1,0:T(8,128)(2,1)S(1)} %get-tuple-element.12.image, f32[1,256,256]{2,1,0:T(8,128)S(1)} %get-tuple-element.10.keep, bf16[1,1,256,256]{3,2,1,0:T(8,128)(2,1)S(1)} %copy-done, bf16[1,1,256,256]{3,2,1,0:T(8,128)(2,1)S(1)} %copy-done.1, ...), custom_call_target="tpu_custom_call" | custom-call | flops 268435456 | bytes 524288 | tf_op jit(solution)/shard_map/pallas_call | solution.py:160
  28.6 0.7 %collective-permute-done.10.other = f32[8,128]{1,0:T(8,128)S(1)} collective-permute-done((f32[8,128]{1,0:T(8,128)S(1)}, f32[8,128]{1,0:T(8,128)S(1)}, u32[]{:S(2)}, u32[]{:S(2)}) %collective-permute-start.10) | collective-permute-done | bytes 4128 | tf_op jit(solution)/shard_map/ppermute | solution.py:14
  29.3 0.8 %shard_map.80 = bf16[1,1,256,256]{3,2,1,0:T(8,128)(2,1)} custom-call(f32[1,1,256,256]{3,2,1,0:T(8,128)S(1)} %get-tuple-element.14.raw, f32[8,128]{1,0:T(8,128)S(1)} %add.11.norm, f32[8,128]{1,0:T(8,128)S(1)} %collective-permute-done.10.other), custom_call_target="tpu_custom_call" | custom-call | tf_op jit(solution)/shard_map/pallas_call | solution.py:190
  (7 shorter events, 0.0 us)
Async XLA Ops:
  0.6 12.2 %copy-start.4 = (s32[1,4]{1,0:T(1,128)S(1)}, s32[1,4]{1,0:T(1,128)}, u32[]{:S(2)}) copy-start(s32[1,4]{1,0:T(1,128)} %live.1) | copy-start | bytes 52
  0.6 12.2 %copy-start.3 = (s32[4]{0:T(128)S(1)}, s32[4]{0:T(128)}, u32[]{:S(2)}) copy-start(s32[4]{0:T(128)} %cols.1) | copy-start | bytes 52
  0.7 8.8 %collective-permute-start = (bf16[1,1,256,256]{3,2,1,0:T(8,128)(2,1)}, bf16[1,1,256,256]{3,2,1,0:T(8,128)(2,1)S(1)}, u32[]{:S(2)}, u32[]{:S(2)}) collective-permute-start(bf16[1,1,256,256]{3,2,1,0:T(8,128)(2,1)} %mine.3), channel_id=1, source_target_pairs={{1,0},{4,1},{9,2},{15,3},{2,4},{6,5},{11,6},{13,7},{0,8},{5,9},{8,... | collective-permute-start | bytes 393224 | tf_op jit(solution)/shard_map/ppermute | solution.py:14
  4.7 6.6 %collective-permute-start.2 = (bf16[1,1,256,256]{3,2,1,0:T(8,128)(2,1)}, bf16[1,1,256,256]{3,2,1,0:T(8,128)(2,1)S(1)}, u32[]{:S(2)}, u32[]{:S(2)}) collective-permute-start(bf16[1,1,256,256]{3,2,1,0:T(8,128)(2,1)} %refs_0_.3), channel_id=1, source_target_pairs={{0,3},{1,2},{2,1},{3,0},{4,7},{5,6},{6,5},{7,4},{8,11},{9,10},{10,... | collective-permute-start | bytes 393224 | tf_op jit(solution)/shard_map/ppermute | solution.py:14
  6.9 7.8 %collective-permute-start.6 = (bf16[1,1,256,256]{3,2,1,0:T(8,128)(2,1)}, bf16[1,1,256,256]{3,2,1,0:T(8,128)(2,1)S(1)}, u32[]{:S(2)}, u32[]{:S(2)}) collective-permute-start(bf16[1,1,256,256]{3,2,1,0:T(8,128)(2,1)} %mine.3), channel_id=1, source_target_pairs={{3,0},{5,1},{8,2},{14,3},{0,4},{7,5},{10,6},{12,7},{2,8},{4,9},{9,... | collective-permute-start | bytes 393224 | tf_op jit(solution)/shard_map/ppermute | solution.py:14
  6.9 7.8 %collective-permute-start.5 = (bf16[1,1,256,256]{3,2,1,0:T(8,128)(2,1)}, bf16[1,1,256,256]{3,2,1,0:T(8,128)(2,1)S(1)}, u32[]{:S(2)}, u32[]{:S(2)}) collective-permute-start(bf16[1,1,256,256]{3,2,1,0:T(8,128)(2,1)} %mine.3), channel_id=1, source_target_pairs={{2,0},{6,1},{10,2},{13,3},{1,4},{4,5},{8,6},{15,7},{3,8},{7,9},{11... | collective-permute-start | bytes 393224 | tf_op jit(solution)/shard_map/ppermute | solution.py:14
  8.7 6.0 %collective-permute-start.4 = (bf16[1,1,256,256]{3,2,1,0:T(8,128)(2,1)}, bf16[1,1,256,256]{3,2,1,0:T(8,128)(2,1)S(1)}, u32[]{:S(2)}, u32[]{:S(2)}) collective-permute-start(bf16[1,1,256,256]{3,2,1,0:T(8,128)(2,1)} %mine.3), channel_id=1, source_target_pairs={{7,1},{11,2},{12,3},{3,4},{9,6},{14,7},{1,8},{6,9},{13,11},{2,12},... | collective-permute-start | bytes 393224 | tf_op jit(solution)/shard_map/ppermute | solution.py:14
  11.3 3.5 %collective-permute-start.3 = (bf16[1,1,256,256]{3,2,1,0:T(8,128)(2,1)S(1)}, bf16[1,1,256,256]{3,2,1,0:T(8,128)(2,1)S(1)}, u32[]{:S(2)}, u32[]{:S(2)}) collective-permute-start(bf16[1,1,256,256]{3,2,1,0:T(8,128)(2,1)S(1)} %collective-permute-done.2.refs_3_), channel_id=1, source_target_pairs={{0,1},{1,0},{2,3},{3,2},{4,5},{5,4},{6,7},{7,6},{8,9},{9,8},{10,11... | collective-permute-start | bytes 393224 | tf_op jit(solution)/shard_map/ppermute | solution.py:14
  12.1 2.7 %collective-permute-start.1 = (bf16[1,1,256,256]{3,2,1,0:T(8,128)(2,1)}, bf16[1,1,256,256]{3,2,1,0:T(8,128)(2,1)S(1)}, u32[]{:S(2)}, u32[]{:S(2)}) collective-permute-start(bf16[1,1,256,256]{3,2,1,0:T(8,128)(2,1)} %refs_0_.3), channel_id=1, source_target_pairs={{0,1},{1,0},{2,3},{3,2},{4,5},{5,4},{6,7},{7,6},{8,9},{9,8},{10,11... | collective-permute-start | bytes 393224 | tf_op jit(solution)/shard_map/ppermute | solution.py:14
  12.8 1.0 %copy-start.2 = (bf16[1,4,256,256]{3,2,1,0:T(8,128)(2,1)S(1)}, bf16[1,4,256,256]{3,2,1,0:T(8,128)(2,1)}, u32[]{:S(2)}) copy-start(bf16[1,4,256,256]{3,2,1,0:T(8,128)(2,1)} %two_site.1) | copy-start | bytes 1572868
  13.9 0.9 %copy-start = (bf16[1,1,256,256]{3,2,1,0:T(8,128)(2,1)S(1)}, bf16[1,1,256,256]{3,2,1,0:T(8,128)(2,1)}, u32[]{:S(2)}) copy-start(bf16[1,1,256,256]{3,2,1,0:T(8,128)(2,1)} %mine.3) | copy-start | bytes 393220
  13.9 1.0 %copy-start.1 = (bf16[1,1,256,256]{3,2,1,0:T(8,128)(2,1)S(1)}, bf16[1,1,256,256]{3,2,1,0:T(8,128)(2,1)}, u32[]{:S(2)}) copy-start(bf16[1,1,256,256]{3,2,1,0:T(8,128)(2,1)} %refs_0_.3) | copy-start | bytes 393220
  15.6 5.1 %collective-permute-start.7 = (f32[8,128]{1,0:T(8,128)S(1)}, f32[8,128]{1,0:T(8,128)S(1)}, u32[]{:S(2)}, u32[]{:S(2)}) collective-permute-start(f32[8,128]{1,0:T(8,128)S(1)} %get-tuple-element.15), channel_id=1, source_target_pairs={{0,3},{1,2},{2,1},{3,0},{4,7},{5,6},{6,5},{7,4},{8,11},{9,10},{10,... | collective-permute-start | bytes 12296 | tf_op jit(solution)/shard_map/ppermute | solution.py:14
  20.8 4.3 %collective-permute-start.8 = (f32[8,128]{1,0:T(8,128)S(1)}, f32[8,128]{1,0:T(8,128)S(1)}, u32[]{:S(2)}, u32[]{:S(2)}) collective-permute-start(f32[8,128]{1,0:T(8,128)S(1)} %add.9), channel_id=1, source_target_pairs={{0,9},{1,8},{2,11},{3,10},{4,13},{5,12},{6,15},{7,14},{8,1},{9,0},... | collective-permute-start | bytes 12296 | tf_op jit(solution)/shard_map/ppermute | solution.py:14
  25.1 1.2 %collective-permute-start.9 = (f32[8,128]{1,0:T(8,128)S(1)}, f32[8,128]{1,0:T(8,128)S(1)}, u32[]{:S(2)}, u32[]{:S(2)}) collective-permute-start(f32[8,128]{1,0:T(8,128)S(1)} %add.10), channel_id=1, source_target_pairs={{0,1},{1,0},{2,3},{3,2},{4,5},{5,4},{6,7},{7,6},{8,9},{9,8},{10,11... | collective-permute-start | bytes 12296 | tf_op jit(solution)/shard_map/ppermute | solution.py:14
  26.3 3.0 %collective-permute-start.10 = (f32[8,128]{1,0:T(8,128)S(1)}, f32[8,128]{1,0:T(8,128)S(1)}, u32[]{:S(2)}, u32[]{:S(2)}) collective-permute-start(f32[8,128]{1,0:T(8,128)S(1)} %add.11.norm), channel_id=1, source_target_pairs={{0,5},{1,4},{2,7},{3,6},{4,1},{5,0},{6,3},{7,2},{8,13},{9,12},{10,... | collective-permute-start | bytes 12296 | tf_op jit(solution)/shard_map/ppermute | solution.py:14

commit v8 on v7

--- a/solution.py
+++ b/solution.py
@@ -87,7 +87,9 @@
 
     sums = []
     for o in range(own):
-        total = sum(dot(left[0, 0], products[o * terms + (term ^ m)]) for m, left in enumerate(lefts))
+        wide = jnp.concatenate([left[0, 0] for left in lefts], axis=1)
+        tall = jnp.concatenate([products[o * terms + (term ^ m)] for m in range(terms)], axis=0)
+        total = dot(wide, tall)
         sums.append(jnp.where(keep[o] != 0.0, total, 0.0))
     return sums
 

time: 30.3 us -> 30.3 us (level)
  no operation moved by 1% of the time
where the time goes in v8:
time: 30.3 us; the launch traced here: 30.1 us
  starting transfers between devices  17.8 us (59%)
  waiting for transfers between devices  6.2 us (20%)
  Pallas kernels  3.63 us (12%)
  between operations  1.41 us (5%)
  local copies, waits for them, and re-layouts  1.08 us (4%)
    ppermute x11, starting transfers between devices, move(): lax.ppermute(value, AXES, [(a * terms + b, c * terms + d) for (a, b), (c,...  17.8 us
    ppermute x11, waiting for transfers between devices, move(): lax.ppermute(value, AXES, [(a * terms + b, c * terms + d) for (a, b), (c,...  6.2 us
    pallas_call x2, Pallas kernels, apply_call(): pl.pallas_call(functools.partial(kernel, blocks, terms, own), out_shape=o...  1.94 us
    unnamed x10, local copies, waits for them, and re-layouts  1.08 us
    pallas_call x1, Pallas kernels, local(): pl.pallas_call(functools.partial(start_kernel, own), out_shape=(jax.Shape...  0.86 us
    pallas_call x1, Pallas kernels, local(): pl.pallas_call(functools.partial(scale_kernel, float(blocks * n_cols * wi...  0.83 us
  transfers between devices with their start and end apart: 11, of which 5 were waited for; matrix products, arithmetic and copies ran while one was open for 0% of the time, Pallas kernels for 7%

profile of v8, /device:TPU:0, one launch (start us, length us, event | category | flops | bytes accessed | tf_op | source)
XLA Modules:
  0.0 30.1 jit_solution(6245725650114026786)
XLA Ops:
  0.7 4.1 %collective-permute-start = (bf16[1,1,256,256]{3,2,1,0:T(8,128)(2,1)}, bf16[1,1,256,256]{3,2,1,0:T(8,128)(2,1)S(1)}, u32[]{:S(2)}, u32[]{:S(2)}) collective-permute-start(bf16[1,1,256,256]{3,2,1,0:T(8,128)(2,1)} %mine.3), channel_id=1, source_target_pairs={{1,0},{4,1},{9,2},{15,3},{2,4},{6,5},{11,6},{13,7},{0,8},{5,9},{8,... | collective-permute-start | bytes 393224 | tf_op jit(solution)/shard_map/ppermute | solution.py:14
  4.7 2.2 %collective-permute-start.2 = (bf16[1,1,256,256]{3,2,1,0:T(8,128)(2,1)}, bf16[1,1,256,256]{3,2,1,0:T(8,128)(2,1)S(1)}, u32[]{:S(2)}, u32[]{:S(2)}) collective-permute-start(bf16[1,1,256,256]{3,2,1,0:T(8,128)(2,1)} %refs_0_.3), channel_id=1, source_target_pairs={{0,3},{1,2},{2,1},{3,0},{4,7},{5,6},{6,5},{7,4},{8,11},{9,10},{10,... | collective-permute-start | bytes 393224 | tf_op jit(solution)/shard_map/ppermute | solution.py:14
  6.9 0.0 collective-permute-start.6
  6.9 1.8 %collective-permute-start.5 = (bf16[1,1,256,256]{3,2,1,0:T(8,128)(2,1)}, bf16[1,1,256,256]{3,2,1,0:T(8,128)(2,1)S(1)}, u32[]{:S(2)}, u32[]{:S(2)}) collective-permute-start(bf16[1,1,256,256]{3,2,1,0:T(8,128)(2,1)} %mine.3), channel_id=1, source_target_pairs={{2,0},{6,1},{10,2},{13,3},{1,4},{4,5},{8,6},{15,7},{3,8},{7,9},{11... | collective-permute-start | bytes 393224 | tf_op jit(solution)/shard_map/ppermute | solution.py:14
  8.7 0.7 %collective-permute-start.4 = (bf16[1,1,256,256]{3,2,1,0:T(8,128)(2,1)}, bf16[1,1,256,256]{3,2,1,0:T(8,128)(2,1)S(1)}, u32[]{:S(2)}, u32[]{:S(2)}) collective-permute-start(bf16[1,1,256,256]{3,2,1,0:T(8,128)(2,1)} %mine.3), channel_id=1, source_target_pairs={{7,1},{11,2},{12,3},{3,4},{9,6},{14,7},{1,8},{6,9},{13,11},{2,12},... | collective-permute-start | bytes 393224 | tf_op jit(solution)/shard_map/ppermute | solution.py:14
  9.4 0.0 collective-permute-done.refs_7_
  9.4 1.9 %collective-permute-done.2.refs_3_ = bf16[1,1,256,256]{3,2,1,0:T(8,128)(2,1)S(1)} collective-permute-done((bf16[1,1,256,256]{3,2,1,0:T(8,128)(2,1)}, bf16[1,1,256,256]{3,2,1,0:T(8,128)(2,1)S(1)}, u32[]{:S(2)}, u32[]{:S(2)}) %collective-permute-start.2) | collective-permute-done | bytes 131104 | tf_op jit(solution)/shard_map/ppermute | solution.py:14
  11.3 0.8 %collective-permute-start.3 = (bf16[1,1,256,256]{3,2,1,0:T(8,128)(2,1)S(1)}, bf16[1,1,256,256]{3,2,1,0:T(8,128)(2,1)S(1)}, u32[]{:S(2)}, u32[]{:S(2)}) collective-permute-start(bf16[1,1,256,256]{3,2,1,0:T(8,128)(2,1)S(1)} %collective-permute-done.2.refs_3_), channel_id=1, source_target_pairs={{0,1},{1,0},{2,3},{3,2},{4,5},{5,4},{6,7},{7,6},{8,9},{9,8},{10,11... | collective-permute-start | bytes 393224 | tf_op jit(solution)/shard_map/ppermute | solution.py:14
  12.1 0.1 collective-permute-start.1
  12.8 0.0 copy-done.4
  12.8 0.0 copy-done.3
  12.8 0.0 copy-start.2
  12.8 1.0 %copy-done.2 = bf16[1,4,256,256]{3,2,1,0:T(8,128)(2,1)S(1)} copy-done((bf16[1,4,256,256]{3,2,1,0:T(8,128)(2,1)S(1)}, bf16[1,4,256,256]{3,2,1,0:T(8,128)(2,1)}, u32[]{:S(2)}) %copy-start.2) | copy-done | bytes 524312
  13.9 0.9 %shard_map.77 = (bf16[1,256,256]{2,1,0:T(8,128)(2,1)S(1)}, f32[1,256,256]{2,1,0:T(8,128)S(1)}) custom-call(bf16[1,4,256,256]{3,2,1,0:T(8,128)(2,1)S(1)} %copy-done.2, s32[1]{0:T(128)S(6)} %copy.8.rows, s32[4]{0:T(128)S(1)} %copy-done.3, s32[1,4]{1,0:T(1,128)S(1)} %copy-done.4), custom_call_target="tpu_custom_call" | custom-call | bytes 524288 | tf_op jit(solution)/shard_map/pallas_call | solution.py:142
  14.7 0.0 collective-permute-done.6.refs_6_
  14.8 0.0 collective-permute-done.5.refs_5_
  14.8 0.0 collective-permute-done.4.refs_4_
  14.8 0.0 collective-permute-done.3.refs_2_
  14.8 0.0 collective-permute-done.1.refs_1_
  14.8 0.0 copy-done
  14.8 0.0 copy-done.1
  14.8 0.8 %shard_map.78 = (bf16[1,256,256]{2,1,0:T(8,128)(2,1)S(1)}, f32[8,128]{1,0:T(8,128)S(1)}) custom-call(bf16[1,256,256]{2,1,0:T(8,128)(2,1)S(1)} %get-tuple-element.9.start, f32[1,256,256]{2,1,0:T(8,128)S(1)} %get-tuple-element.10.keep, bf16[1,1,256,256]{3,2,1,0:T(8,128)(2,1)S(1)} %copy-done, bf16[1,1,256,256]{3,2,1,0:T(8,128)(2,1)S(1)} %copy-done.1, ...), custom_call_target="tpu_custom_call" | custom-call | flops 268435456 | bytes 524288 | tf_op jit(solution)/shard_map/pallas_call | solution.py:162
  15.6 3.8 %collective-permute-start.7 = (f32[8,128]{1,0:T(8,128)S(1)}, f32[8,128]{1,0:T(8,128)S(1)}, u32[]{:S(2)}, u32[]{:S(2)}) collective-permute-start(f32[8,128]{1,0:T(8,128)S(1)} %get-tuple-element.15), channel_id=1, source_target_pairs={{0,3},{1,2},{2,1},{3,0},{4,7},{5,6},{6,5},{7,4},{8,11},{9,10},{10,... | collective-permute-start | bytes 12296 | tf_op jit(solution)/shard_map/ppermute | solution.py:14
  19.4 1.3 %collective-permute-done.7 = f32[8,128]{1,0:T(8,128)S(1)} collective-permute-done((f32[8,128]{1,0:T(8,128)S(1)}, f32[8,128]{1,0:T(8,128)S(1)}, u32[]{:S(2)}, u32[]{:S(2)}) %collective-permute-start.7) | collective-permute-done | bytes 4128 | tf_op jit(solution)/shard_map/ppermute | solution.py:14
  20.8 3.0 %collective-permute-start.8 = (f32[8,128]{1,0:T(8,128)S(1)}, f32[8,128]{1,0:T(8,128)S(1)}, u32[]{:S(2)}, u32[]{:S(2)}) collective-permute-start(f32[8,128]{1,0:T(8,128)S(1)} %add.9), channel_id=1, source_target_pairs={{0,9},{1,8},{2,11},{3,10},{4,13},{5,12},{6,15},{7,14},{8,1},{9,0},... | collective-permute-start | bytes 12296 | tf_op jit(solution)/shard_map/ppermute | solution.py:14
  23.8 1.3 %collective-permute-done.8 = f32[8,128]{1,0:T(8,128)S(1)} collective-permute-done((f32[8,128]{1,0:T(8,128)S(1)}, f32[8,128]{1,0:T(8,128)S(1)}, u32[]{:S(2)}, u32[]{:S(2)}) %collective-permute-start.8) | collective-permute-done | bytes 4128 | tf_op jit(solution)/shard_map/ppermute | solution.py:14
  25.1 0.3 %collective-permute-start.9 = (f32[8,128]{1,0:T(8,128)S(1)}, f32[8,128]{1,0:T(8,128)S(1)}, u32[]{:S(2)}, u32[]{:S(2)}) collective-permute-start(f32[8,128]{1,0:T(8,128)S(1)} %add.10), channel_id=1, source_target_pairs={{0,1},{1,0},{2,3},{3,2},{4,5},{5,4},{6,7},{7,6},{8,9},{9,8},{10,11... | collective-permute-start | bytes 12296 | tf_op jit(solution)/shard_map/ppermute | solution.py:14
  25.5 0.8 %collective-permute-done.9 = f32[8,128]{1,0:T(8,128)S(1)} collective-permute-done((f32[8,128]{1,0:T(8,128)S(1)}, f32[8,128]{1,0:T(8,128)S(1)}, u32[]{:S(2)}, u32[]{:S(2)}) %collective-permute-start.9) | collective-permute-done | bytes 4128 | tf_op jit(solution)/shard_map/ppermute | solution.py:14
  26.3 1.1 %collective-permute-start.10 = (f32[8,128]{1,0:T(8,128)S(1)}, f32[8,128]{1,0:T(8,128)S(1)}, u32[]{:S(2)}, u32[]{:S(2)}) collective-permute-start(f32[8,128]{1,0:T(8,128)S(1)} %add.11.norm), channel_id=1, source_target_pairs={{0,5},{1,4},{2,7},{3,6},{4,1},{5,0},{6,3},{7,2},{8,13},{9,12},{10,... | collective-permute-start | bytes 12296 | tf_op jit(solution)/shard_map/ppermute | solution.py:14
  27.3 1.2 %shard_map.79 = (bf16[1,1,256,256]{3,2,1,0:T(8,128)(2,1)}, f32[1,1,256,256]{3,2,1,0:T(8,128)S(1)}) custom-call(bf16[1,256,256]{2,1,0:T(8,128)(2,1)S(1)} %get-tuple-element.12.image, f32[1,256,256]{2,1,0:T(8,128)S(1)} %get-tuple-element.10.keep, bf16[1,1,256,256]{3,2,1,0:T(8,128)(2,1)S(1)} %copy-done, bf16[1,1,256,256]{3,2,1,0:T(8,128)(2,1)S(1)} %copy-done.1, ...), custom_call_target="tpu_custom_call" | custom-call | flops 268435456 | bytes 524288 | tf_op jit(solution)/shard_map/pallas_call | solution.py:162
  28.5 0.8 %collective-permute-done.10.other = f32[8,128]{1,0:T(8,128)S(1)} collective-permute-done((f32[8,128]{1,0:T(8,128)S(1)}, f32[8,128]{1,0:T(8,128)S(1)}, u32[]{:S(2)}, u32[]{:S(2)}) %collective-permute-start.10) | collective-permute-done | bytes 4128 | tf_op jit(solution)/shard_map/ppermute | solution.py:14
  29.3 0.8 %shard_map.80 = bf16[1,1,256,256]{3,2,1,0:T(8,128)(2,1)} custom-call(f32[1,1,256,256]{3,2,1,0:T(8,128)S(1)} %get-tuple-element.14.raw, f32[8,128]{1,0:T(8,128)S(1)} %add.11.norm, f32[8,128]{1,0:T(8,128)S(1)} %collective-permute-done.10.other), custom_call_target="tpu_custom_call" | custom-call | tf_op jit(solution)/shard_map/pallas_call | solution.py:192
  (7 shorter events, 0.0 us)
Async XLA Ops:
  0.6 12.2 %copy-start.4 = (s32[1,4]{1,0:T(1,128)S(1)}, s32[1,4]{1,0:T(1,128)}, u32[]{:S(2)}) copy-start(s32[1,4]{1,0:T(1,128)} %live.1) | copy-start | bytes 52
  0.6 12.2 %copy-start.3 = (s32[4]{0:T(128)S(1)}, s32[4]{0:T(128)}, u32[]{:S(2)}) copy-start(s32[4]{0:T(128)} %cols.1) | copy-start | bytes 52
  0.7 8.8 %collective-permute-start = (bf16[1,1,256,256]{3,2,1,0:T(8,128)(2,1)}, bf16[1,1,256,256]{3,2,1,0:T(8,128)(2,1)S(1)}, u32[]{:S(2)}, u32[]{:S(2)}) collective-permute-start(bf16[1,1,256,256]{3,2,1,0:T(8,128)(2,1)} %mine.3), channel_id=1, source_target_pairs={{1,0},{4,1},{9,2},{15,3},{2,4},{6,5},{11,6},{13,7},{0,8},{5,9},{8,... | collective-permute-start | bytes 393224 | tf_op jit(solution)/shard_map/ppermute | solution.py:14
  4.7 6.6 %collective-permute-start.2 = (bf16[1,1,256,256]{3,2,1,0:T(8,128)(2,1)}, bf16[1,1,256,256]{3,2,1,0:T(8,128)(2,1)S(1)}, u32[]{:S(2)}, u32[]{:S(2)}) collective-permute-start(bf16[1,1,256,256]{3,2,1,0:T(8,128)(2,1)} %refs_0_.3), channel_id=1, source_target_pairs={{0,3},{1,2},{2,1},{3,0},{4,7},{5,6},{6,5},{7,4},{8,11},{9,10},{10,... | collective-permute-start | bytes 393224 | tf_op jit(solution)/shard_map/ppermute | solution.py:14
  6.9 7.8 %collective-permute-start.6 = (bf16[1,1,256,256]{3,2,1,0:T(8,128)(2,1)}, bf16[1,1,256,256]{3,2,1,0:T(8,128)(2,1)S(1)}, u32[]{:S(2)}, u32[]{:S(2)}) collective-permute-start(bf16[1,1,256,256]{3,2,1,0:T(8,128)(2,1)} %mine.3), channel_id=1, source_target_pairs={{3,0},{5,1},{8,2},{14,3},{0,4},{7,5},{10,6},{12,7},{2,8},{4,9},{9,... | collective-permute-start | bytes 393224 | tf_op jit(solution)/shard_map/ppermute | solution.py:14
  6.9 7.8 %collective-permute-start.5 = (bf16[1,1,256,256]{3,2,1,0:T(8,128)(2,1)}, bf16[1,1,256,256]{3,2,1,0:T(8,128)(2,1)S(1)}, u32[]{:S(2)}, u32[]{:S(2)}) collective-permute-start(bf16[1,1,256,256]{3,2,1,0:T(8,128)(2,1)} %mine.3), channel_id=1, source_target_pairs={{2,0},{6,1},{10,2},{13,3},{1,4},{4,5},{8,6},{15,7},{3,8},{7,9},{11... | collective-permute-start | bytes 393224 | tf_op jit(solution)/shard_map/ppermute | solution.py:14
  8.7 6.0 %collective-permute-start.4 = (bf16[1,1,256,256]{3,2,1,0:T(8,128)(2,1)}, bf16[1,1,256,256]{3,2,1,0:T(8,128)(2,1)S(1)}, u32[]{:S(2)}, u32[]{:S(2)}) collective-permute-start(bf16[1,1,256,256]{3,2,1,0:T(8,128)(2,1)} %mine.3), channel_id=1, source_target_pairs={{7,1},{11,2},{12,3},{3,4},{9,6},{14,7},{1,8},{6,9},{13,11},{2,12},... | collective-permute-start | bytes 393224 | tf_op jit(solution)/shard_map/ppermute | solution.py:14
  11.3 3.5 %collective-permute-start.3 = (bf16[1,1,256,256]{3,2,1,0:T(8,128)(2,1)S(1)}, bf16[1,1,256,256]{3,2,1,0:T(8,128)(2,1)S(1)}, u32[]{:S(2)}, u32[]{:S(2)}) collective-permute-start(bf16[1,1,256,256]{3,2,1,0:T(8,128)(2,1)S(1)} %collective-permute-done.2.refs_3_), channel_id=1, source_target_pairs={{0,1},{1,0},{2,3},{3,2},{4,5},{5,4},{6,7},{7,6},{8,9},{9,8},{10,11... | collective-permute-start | bytes 393224 | tf_op jit(solution)/shard_map/ppermute | solution.py:14
  12.1 2.7 %collective-permute-start.1 = (bf16[1,1,256,256]{3,2,1,0:T(8,128)(2,1)}, bf16[1,1,256,256]{3,2,1,0:T(8,128)(2,1)S(1)}, u32[]{:S(2)}, u32[]{:S(2)}) collective-permute-start(bf16[1,1,256,256]{3,2,1,0:T(8,128)(2,1)} %refs_0_.3), channel_id=1, source_target_pairs={{0,1},{1,0},{2,3},{3,2},{4,5},{5,4},{6,7},{7,6},{8,9},{9,8},{10,11... | collective-permute-start | bytes 393224 | tf_op jit(solution)/shard_map/ppermute | solution.py:14
  12.8 1.0 %copy-start.2 = (bf16[1,4,256,256]{3,2,1,0:T(8,128)(2,1)S(1)}, bf16[1,4,256,256]{3,2,1,0:T(8,128)(2,1)}, u32[]{:S(2)}) copy-start(bf16[1,4,256,256]{3,2,1,0:T(8,128)(2,1)} %two_site.1) | copy-start | bytes 1572868
  13.9 0.9 %copy-start = (bf16[1,1,256,256]{3,2,1,0:T(8,128)(2,1)S(1)}, bf16[1,1,256,256]{3,2,1,0:T(8,128)(2,1)}, u32[]{:S(2)}) copy-start(bf16[1,1,256,256]{3,2,1,0:T(8,128)(2,1)} %mine.3) | copy-start | bytes 393220
  13.9 1.0 %copy-start.1 = (bf16[1,1,256,256]{3,2,1,0:T(8,128)(2,1)S(1)}, bf16[1,1,256,256]{3,2,1,0:T(8,128)(2,1)}, u32[]{:S(2)}) copy-start(bf16[1,1,256,256]{3,2,1,0:T(8,128)(2,1)} %refs_0_.3) | copy-start | bytes 393220
  15.6 5.1 %collective-permute-start.7 = (f32[8,128]{1,0:T(8,128)S(1)}, f32[8,128]{1,0:T(8,128)S(1)}, u32[]{:S(2)}, u32[]{:S(2)}) collective-permute-start(f32[8,128]{1,0:T(8,128)S(1)} %get-tuple-element.15), channel_id=1, source_target_pairs={{0,3},{1,2},{2,1},{3,0},{4,7},{5,6},{6,5},{7,4},{8,11},{9,10},{10,... | collective-permute-start | bytes 12296 | tf_op jit(solution)/shard_map/ppermute | solution.py:14
  20.8 4.3 %collective-permute-start.8 = (f32[8,128]{1,0:T(8,128)S(1)}, f32[8,128]{1,0:T(8,128)S(1)}, u32[]{:S(2)}, u32[]{:S(2)}) collective-permute-start(f32[8,128]{1,0:T(8,128)S(1)} %add.9), channel_id=1, source_target_pairs={{0,9},{1,8},{2,11},{3,10},{4,13},{5,12},{6,15},{7,14},{8,1},{9,0},... | collective-permute-start | bytes 12296 | tf_op jit(solution)/shard_map/ppermute | solution.py:14
  25.1 1.2 %collective-permute-start.9 = (f32[8,128]{1,0:T(8,128)S(1)}, f32[8,128]{1,0:T(8,128)S(1)}, u32[]{:S(2)}, u32[]{:S(2)}) collective-permute-start(f32[8,128]{1,0:T(8,128)S(1)} %add.10), channel_id=1, source_target_pairs={{0,1},{1,0},{2,3},{3,2},{4,5},{5,4},{6,7},{7,6},{8,9},{9,8},{10,11... | collective-permute-start | bytes 12296 | tf_op jit(solution)/shard_map/ppermute | solution.py:14
  26.3 3.0 %collective-permute-start.10 = (f32[8,128]{1,0:T(8,128)S(1)}, f32[8,128]{1,0:T(8,128)S(1)}, u32[]{:S(2)}, u32[]{:S(2)}) collective-permute-start(f32[8,128]{1,0:T(8,128)S(1)} %add.11.norm), channel_id=1, source_target_pairs={{0,5},{1,4},{2,7},{3,6},{4,1},{5,0},{6,3},{7,2},{8,13},{9,12},{10,... | collective-permute-start | bytes 12296 | tf_op jit(solution)/shard_map/ppermute | solution.py:14
